TPU v7x, 32 devices: a whole 2x2x4 slice. The times are simulated.
32 devices in a mesh: dp: 4 (over y, core), tensor: 8 (over z, x).
Axes of the slice: x: 2, y: 2, z: 4, core: 2. Of those that a mesh axis runs over, the one named last changes fastest.
Arguments:
- tokens: bfloat16 [2048, 2048], P(('dp', 'tensor')), may hold values from -6 to 6
- norm_gain: bfloat16 [2048], replicated, may hold values from 0.25 to 1.75
- query_weight: bfloat16 [2048, 2048], P('dp'), may hold values from -0.125 to 0.125
- keyval_weight: bfloat16 [2, 2048, 512], P(None, 'dp'), may hold values from -0.125 to 0.125
- query_gain: float32 [64], replicated, may hold values from 0.5 to 2
- key_gain: float32 [64], replicated, may hold values from 0.5 to 2
- output_weight: bfloat16 [2048, 2048], P(None, 'dp'), may hold values from -0.75 to 0.75
- keyval_cache: bfloat16 [32, 2048, 128], P(('dp', 'tensor')), may hold values from -96 to 96
- cached_lengths: int32 [4], P('dp'), may hold values from 1 to 2048, as said below
- sink_count: int32 [4], P('dp'), may hold values from 1 to 32
- window: int32 [4], P('dp'), may hold values from 512 to 4096, as said below
Outputs:
- attended: bfloat16 [2048, 2048], P(('dp', 'tensor'))
- fresh_keyvals: bfloat16 [32, 512, 128], P(('dp', 'tensor'))
Inputs may be any that keep to these rules, and one draw needn't show every extreme that they name: `cached_lengths`: some request has exactly 2048 cached tokens. Some request has a window of exactly 4096.
All inputs are finite; a program needn't handle non-finite values.
Results may differ from a plain program's by a relative error of at most 0.014.
The roundings to bfloat16 on the way count: a program that leaves them out, or rounds other values in their place, can miss the bound.
Values may be sent and summed in bfloat16 or wider, within the bound.
No kernel may reach another device: no remote copies, remote signals or barrier semaphores. Data moves between devices by JAX's collectives and lax.ppermute only.
A program may use at most 64 MiB of HBM per device.

v0:
```python
import jax
import jax.numpy as jnp
from jax import lax
from jax.sharding import PartitionSpec as P

epsilon = 1e-05
theta_base = 1000000.0
key_block = 1024
query_block = 512


def from_partner(block, axis, apart):
    count = lax.axis_size(axis)
    route = []
    for low in range(count):
        high = low | 1 << apart
        if high != low and high < count:
            route += [(low, high), (high, low)]
    return lax.ppermute(block, axis, route)


def rms_scale(values, weights):
    mean_square = jnp.mean(values * values, axis=-1, keepdims=True)
    return values * lax.rsqrt(mean_square + epsilon) * weights


def rotate(values, positions):
    half_dim = values.shape[-1] // 2
    inverse_freq = theta_base ** (-2.0 * jnp.arange(half_dim, dtype=jnp.float32) / values.shape[-1])
    angles = positions.astype(jnp.float32)[:, None] * inverse_freq[None, :]
    cosine = jnp.cos(angles)
    sine_part = jnp.sin(angles)
    first_half = values[..., :half_dim]
    second_half = values[..., half_dim:]
    return jnp.concatenate(
        [
            first_half * cosine - second_half * sine_part,
            second_half * cosine + first_half * sine_part,
        ],
        axis=-1,
    )


def ordered_pair(mine, partner, upper_side, axis_index):
    return jnp.where(
        upper_side,
        jnp.concatenate([partner, mine], axis=axis_index),
        jnp.concatenate([mine, partner], axis=axis_index),
    )


def body(
    tokens,
    norm_gain,
    query_weight,
    keyval_weight,
    query_gain,
    key_gain,
    output_weight,
    keyval_cache,
    cached_lengths,
    sink_count,
    window,
):
    tensor_rank = lax.axis_index("tensor")
    head_dim = query_gain.shape[0]
    kv_heads = keyval_weight.shape[2] // head_dim
    group_bits = kv_heads.bit_length() - 1
    member = tensor_rank % kv_heads
    request_slot = tensor_rank // kv_heads
    length = cached_lengths[request_slot]
    sink_total = sink_count[request_slot]
    window_len = window[request_slot]
    block_cols = query_weight.shape[1] // kv_heads
    head_count = block_cols // head_dim
    new_rows = tokens.shape[0] * kv_heads

    def bit_set(bit_index):
        return tensor_rank // 2**bit_index % 2 == 1

    normed = rms_scale(tokens.astype(jnp.float32), norm_gain.astype(jnp.float32)).astype(
        jnp.bfloat16
    )
    gathered = normed
    for bit_index in range(group_bits):
        partner = from_partner(gathered, "tensor", bit_index)
        gathered = ordered_pair(gathered, partner, bit_set(bit_index), 0)
    query_local = lax.dynamic_slice_in_dim(query_weight, member * block_cols, block_cols, 1)
    keyval_local = lax.dynamic_slice_in_dim(keyval_weight, member * head_dim, head_dim, 2)
    combined = jnp.concatenate([query_local, keyval_local[0], keyval_local[1]], axis=1)
    projected = jnp.dot(
        gathered,
        lax.all_gather(combined, "dp", axis=0, tiled=True),
        preferred_element_type=jnp.float32,
    )
    query_raw = projected[:, :block_cols].reshape(new_rows, head_count, head_dim).transpose(1, 0, 2)
    key_raw = projected[:, block_cols : block_cols + head_dim]
    value_new = projected[:, block_cols + head_dim :].astype(jnp.bfloat16)
    positions = length + jnp.arange(new_rows, dtype=jnp.int32)
    queries = rotate(rms_scale(query_raw, query_gain), positions).astype(jnp.bfloat16)
    key_new = rotate(rms_scale(key_raw, key_gain), positions).astype(jnp.bfloat16)
    fresh = jnp.concatenate([key_new, value_new], axis=1)[None]
    cache_rows = keyval_cache[0]
    cache_slots = cache_rows.shape[0]
    all_keys = jnp.concatenate([cache_rows[:, :head_dim], key_new], axis=0)
    all_values = jnp.concatenate([cache_rows[:, head_dim:], value_new], axis=0)
    slot_pos = jnp.arange(cache_slots, dtype=jnp.int32)
    key_pos = jnp.concatenate([slot_pos, positions])
    key_live = jnp.concatenate([slot_pos < length, jnp.ones((new_rows,), jnp.bool_)])
    total_keys = all_keys.shape[0]
    bounds = [
        (block_low, min(block_low + key_block, total_keys))
        for block_low in range(0, total_keys, key_block)
    ]
    scale = head_dim ** (-0.5)
    flat_rows = head_count * new_rows
    flat_pos = jnp.tile(positions, head_count).reshape(flat_rows // query_block, query_block)

    def allowed_in(query_pos, block_low, block_high):
        block_pos = key_pos[block_low:block_high][None, :]
        block_live = key_live[block_low:block_high][None, :]
        return (
            block_live
            & (block_pos <= query_pos[:, None])
            & ((block_pos < sink_total) | (query_pos[:, None] - block_pos < window_len))
        )

    def attend(operands):
        block_queries, query_pos = operands
        masked_blocks = []
        for block_low, block_high in bounds:
            allowed = allowed_in(query_pos, block_low, block_high)

            def score_block(unused, block_low=block_low, block_high=block_high, allowed=allowed):
                scores = (
                    jnp.einsum(
                        "qd,kd->qk",
                        block_queries,
                        all_keys[block_low:block_high],
                        preferred_element_type=jnp.float32,
                    )
                    * scale
                )
                return jnp.where(allowed, scores, -jnp.inf)

            masked = score_block(0)
            masked_blocks.append((allowed, masked))
        row_max = jnp.full((query_block,), -jnp.inf, jnp.float32)
        for allowed, masked in masked_blocks:
            row_max = jnp.maximum(row_max, jnp.max(masked, axis=1))
        running = jnp.zeros((query_block,), jnp.float32)
        accum = jnp.zeros((query_block, head_dim), jnp.float32)
        for (block_low, block_high), (allowed, masked) in zip(bounds, masked_blocks):

            def add_block(
                carried, block_low=block_low, block_high=block_high, allowed=allowed, masked=masked
            ):
                weights = jnp.where(allowed, jnp.exp(masked - row_max[:, None]), 0.0)
                return (
                    carried[0] + jnp.sum(weights, axis=1),
                    carried[1]
                    + jnp.dot(
                        weights.astype(jnp.bfloat16),
                        all_values[block_low:block_high],
                        preferred_element_type=jnp.float32,
                    ),
                )

            running, accum = add_block((running, accum))
        return (accum / running[:, None]).astype(jnp.bfloat16)

    outputs = lax.map(attend, (queries, flat_pos))
    head_out = (
        outputs.reshape(head_count, new_rows, head_dim)
        .transpose(1, 0, 2)
        .reshape(new_rows, block_cols)
    )
    out_rows = lax.dynamic_slice_in_dim(output_weight, member * block_cols, block_cols, 0)
    current = jnp.dot(
        head_out,
        lax.all_gather(out_rows, "dp", axis=1, tiled=True),
        preferred_element_type=jnp.float32,
    )
    for bit_index in reversed(range(group_bits)):
        half = current.shape[0] // 2
        upper_side = bit_set(bit_index)
        keep = jnp.where(upper_side, current[half:], current[:half])
        send = jnp.where(upper_side, current[:half], current[half:])
        current = keep + from_partner(send.astype(jnp.bfloat16), "tensor", bit_index).astype(
            send.dtype
        )
    attended = current.astype(jnp.bfloat16)
    return (attended, fresh)


def solution(mesh):
    in_specs = (
        P(("dp", "tensor"), None),
        P(),
        P("dp", None),
        P(None, "dp", None),
        P(),
        P(),
        P(None, "dp"),
        P(("dp", "tensor"), None, None),
        P("dp"),
        P("dp"),
        P("dp"),
    )
    out_specs = (P(("dp", "tensor"), None), P(("dp", "tensor"), None, None))
    return jax.shard_map(body, mesh=mesh, in_specs=in_specs, out_specs=out_specs, check_vma=False)
```

profile of v0, /device:TPU:0, one launch (start us, length us, event | category | flops | bytes accessed | tf_op | source)
XLA Modules:
  0.0 243.5 jit_solution(955688088426862728)
XLA Ops:
  11.2 3.0 %collective-permute-start = (bf16[64,2048]{1,0:T(8,128)(2,1)S(1)}, bf16[64,2048]{1,0:T(8,128)(2,1)}, u32[]{:S(2)}, u32[]{:S(2)}) collective-permute-start(bf16[64,2048]{1,0:T(8,128)(2,1)S(1)} %fusion.66), channel_id=1, source_target_pairs={{0,1},{1,0},{2,3},{3,2},{4,5},{5,4},{6,7},{7,6},{8,9},{9,8},{10,11... | collective-permute-start | bytes 786440 | tf_op jit(solution)/shard_map/ppermute | solution.py:19
  14.2 6.4 %collective-permute-done = bf16[64,2048]{1,0:T(8,128)(2,1)} collective-permute-done((bf16[64,2048]{1,0:T(8,128)(2,1)S(1)}, bf16[64,2048]{1,0:T(8,128)(2,1)}, u32[]{:S(2)}, u32[]{:S(2)}) %collective-permute-start) | collective-permute-done | bytes 262176 | tf_op jit(solution)/shard_map/ppermute | solution.py:19
  23.7 11.4 %collective-permute-done.1 = bf16[128,2048]{1,0:T(8,128)(2,1)} collective-permute-done((bf16[128,2048]{1,0:T(8,128)(2,1)S(1)}, bf16[128,2048]{1,0:T(8,128)(2,1)}, u32[]{:S(2)}, u32[]{:S(2)}) %collective-permute-start.1) | collective-permute-done | bytes 524320 | tf_op jit(solution)/shard_map/ppermute | solution.py:19
  35.1 2.5 %maximum_select_fusion.2 = bf16[256,2048]{1,0:T(8,128)(2,1)} fusion(bf16[128,2048]{1,0:T(8,128)(2,1)S(1)} %maximum_select_fusion.3, bf16[128,2048]{1,0:T(8,128)(2,1)} %collective-permute-done.1, pred[]{:T(512)S(6)} %eq.21), kind=kLoop, calls=%fused_computation.76 | loop fusion | flops 4718592 | bytes 2097153 | tf_op jit(solution)/shard_map/jit(_where)/select_n | solution.py:45
  37.6 2.5 %collective-permute-start.2 = (bf16[256,2048]{1,0:T(8,128)(2,1)}, bf16[256,2048]{1,0:T(8,128)(2,1)}, u32[]{:S(2)}, u32[]{:S(2)}) collective-permute-start(bf16[256,2048]{1,0:T(8,128)(2,1)} %maximum_select_fusion.2), channel_id=1, source_target_pairs={{0,4},{4,0},{1,5},{5,1},{2,6},{6,2},{3,7},{7,3},{8,12},{12,8},{9,1... | collective-permute-start | bytes 3145736 | tf_op jit(solution)/shard_map/ppermute | solution.py:19
  43.8 40.9 %collective-permute-done.2 = bf16[256,2048]{1,0:T(8,128)(2,1)} collective-permute-done((bf16[256,2048]{1,0:T(8,128)(2,1)}, bf16[256,2048]{1,0:T(8,128)(2,1)}, u32[]{:S(2)}, u32[]{:S(2)}) %collective-permute-start.2) | collective-permute-done | bytes 1048608 | tf_op jit(solution)/shard_map/ppermute | solution.py:19
  84.7 3.7 %fusion.55 = f32[512,384]{0,1:T(8,128)S(1)} fusion(bf16[2048,384]{1,0:T(8,128)(2,1)} %all-gather.3.cloned.1.call-done, bf16[256,2048]{1,0:T(8,128)(2,1)} %maximum_select_fusion.2, bf16[256,2048]{1,0:T(8,128)(2,1)} %collective-permute-done.2, pred[]{:T(512)S(6)} %eq.22), kind=kOutput, calls=%fused_computation.67 | convolution fusion | flops 814743552 | bytes 4456449 | tf_op jit(solution)/shard_map/dot_general | solution.py:91
  96.1 67.7 %while.12 = (s32[]{:T(128)}, bf16[4,512,64]{1,2,0:T(8,128)(2,1)}, pred[2048]{0:T(1024)(128)(4,1)S(1)}, s32[2048]{0:T(1024)S(1)}, s32[4,512]{1,0:T(4,128)S(1)}, /...) while((s32[]{:T(128)}, bf16[4,512,64]{1,2,0:T(8,128)(2,1)}, ...), condition=%wide.region_10.11_spmd.clone.clone, body=%wide.region_3.10_spmd.clone.clone.sunk | while | flops 374475264 | bytes 21765392 | solution.py:172
  97.2 2.5 %fusion.108 = (f32[512]{0:T(512)S(1)}, f32[512]{0:T(512)S(1)}, f32[512,1024]{1,0:T(8,128)S(1)}) fusion(s32[]{:T(128)} %get-tuple-element.355, pred[1024]{0:T(1024)(128)(4,1)S(1)} %get-tuple-element.309, s32[512]{0:T(512)S(1)} %bitcast.60, s32[1024]{0:T(1024)S(1)} %get-tuple-element.310, pred[1024]{0:T(1024)(128)(4,1)S(1)} %get-tuple-element.311, ...), kind=kOutput, calls=%fused_computation.12.clone.1 | convolution fusion | flops 76545024 | bytes 4605960 | tf_op jit(solution)/shard_map/while/body/eval_jaxpr/qd,kd->qk/dot_general | solution.py:136
  102.9 3.2 %fusion.111 = (f32[512]{0:T(512)S(1)}, f32[512]{0:T(512)S(1)}) fusion(f32[512,1024]{1,0:T(8,128)S(1)} %get-tuple-element.317, f32[512]{0:T(512)S(1)} %maximum_maximum_fusion.2, s32[]{:T(128)} %get-tuple-element.355, pred[1024]{0:T(1024)(128)(4,1)S(1)} %get-tuple-element.309, s32[512]{0:T(512)S(1)} %bitcast.62, s32[1024]{0:T(1024)S(1)} %get-tuple-element.310, ...), kind=kLoop, calls=%fused_computation.17.clone.1 | loop fusion | flops 11533312 | bytes 4214788 | tf_op jit(solution)/shard_map/while/body/eval_jaxpr/reduce_sum | solution.py:160
  107.3 1.9 fusion.109
  109.2 1.9 convolution_add_fusion.3
  111.1 1.9 fusion.112
  114.1 2.5 %fusion.108 = (f32[512]{0:T(512)S(1)}, f32[512]{0:T(512)S(1)}, f32[512,1024]{1,0:T(8,128)S(1)}) fusion(s32[]{:T(128)} %get-tuple-element.355, pred[1024]{0:T(1024)(128)(4,1)S(1)} %get-tuple-element.309, s32[512]{0:T(512)S(1)} %bitcast.60, s32[1024]{0:T(1024)S(1)} %get-tuple-element.310, pred[1024]{0:T(1024)(128)(4,1)S(1)} %get-tuple-element.311, ...), kind=kOutput, calls=%fused_computation.12.clone.1 | convolution fusion | flops 76545024 | bytes 4605960 | tf_op jit(solution)/shard_map/while/body/eval_jaxpr/qd,kd->qk/dot_general | solution.py:136
  119.8 3.2 %fusion.111 = (f32[512]{0:T(512)S(1)}, f32[512]{0:T(512)S(1)}) fusion(f32[512,1024]{1,0:T(8,128)S(1)} %get-tuple-element.317, f32[512]{0:T(512)S(1)} %maximum_maximum_fusion.2, s32[]{:T(128)} %get-tuple-element.355, pred[1024]{0:T(1024)(128)(4,1)S(1)} %get-tuple-element.309, s32[512]{0:T(512)S(1)} %bitcast.62, s32[1024]{0:T(1024)S(1)} %get-tuple-element.310, ...), kind=kLoop, calls=%fused_computation.17.clone.1 | loop fusion | flops 11533312 | bytes 4214788 | tf_op jit(solution)/shard_map/while/body/eval_jaxpr/reduce_sum | solution.py:160
  124.2 1.9 fusion.109
  126.1 1.9 convolution_add_fusion.3
  128.0 1.9 fusion.112
  131.1 2.5 %fusion.108 = (f32[512]{0:T(512)S(1)}, f32[512]{0:T(512)S(1)}, f32[512,1024]{1,0:T(8,128)S(1)}) fusion(s32[]{:T(128)} %get-tuple-element.355, pred[1024]{0:T(1024)(128)(4,1)S(1)} %get-tuple-element.309, s32[512]{0:T(512)S(1)} %bitcast.60, s32[1024]{0:T(1024)S(1)} %get-tuple-element.310, pred[1024]{0:T(1024)(128)(4,1)S(1)} %get-tuple-element.311, ...), kind=kOutput, calls=%fused_computation.12.clone.1 | convolution fusion | flops 76545024 | bytes 4605960 | tf_op jit(solution)/shard_map/while/body/eval_jaxpr/qd,kd->qk/dot_general | solution.py:136
  136.8 3.2 %fusion.111 = (f32[512]{0:T(512)S(1)}, f32[512]{0:T(512)S(1)}) fusion(f32[512,1024]{1,0:T(8,128)S(1)} %get-tuple-element.317, f32[512]{0:T(512)S(1)} %maximum_maximum_fusion.2, s32[]{:T(128)} %get-tuple-element.355, pred[1024]{0:T(1024)(128)(4,1)S(1)} %get-tuple-element.309, s32[512]{0:T(512)S(1)} %bitcast.62, s32[1024]{0:T(1024)S(1)} %get-tuple-element.310, ...), kind=kLoop, calls=%fused_computation.17.clone.1 | loop fusion | flops 11533312 | bytes 4214788 | tf_op jit(solution)/shard_map/while/body/eval_jaxpr/reduce_sum | solution.py:160
  141.2 1.9 fusion.109
  143.0 1.9 convolution_add_fusion.3
  145.0 1.9 fusion.112
  148.0 2.5 %fusion.108 = (f32[512]{0:T(512)S(1)}, f32[512]{0:T(512)S(1)}, f32[512,1024]{1,0:T(8,128)S(1)}) fusion(s32[]{:T(128)} %get-tuple-element.355, pred[1024]{0:T(1024)(128)(4,1)S(1)} %get-tuple-element.309, s32[512]{0:T(512)S(1)} %bitcast.60, s32[1024]{0:T(1024)S(1)} %get-tuple-element.310, pred[1024]{0:T(1024)(128)(4,1)S(1)} %get-tuple-element.311, ...), kind=kOutput, calls=%fused_computation.12.clone.1 | convolution fusion | flops 76545024 | bytes 4605960 | tf_op jit(solution)/shard_map/while/body/eval_jaxpr/qd,kd->qk/dot_general | solution.py:136
  153.7 3.2 %fusion.111 = (f32[512]{0:T(512)S(1)}, f32[512]{0:T(512)S(1)}) fusion(f32[512,1024]{1,0:T(8,128)S(1)} %get-tuple-element.317, f32[512]{0:T(512)S(1)} %maximum_maximum_fusion.2, s32[]{:T(128)} %get-tuple-element.355, pred[1024]{0:T(1024)(128)(4,1)S(1)} %get-tuple-element.309, s32[512]{0:T(512)S(1)} %bitcast.62, s32[1024]{0:T(1024)S(1)} %get-tuple-element.310, ...), kind=kLoop, calls=%fused_computation.17.clone.1 | loop fusion | flops 11533312 | bytes 4214788 | tf_op jit(solution)/shard_map/while/body/eval_jaxpr/reduce_sum | solution.py:160
  158.1 1.9 fusion.109
  160.0 1.9 convolution_add_fusion.3
  161.9 1.9 fusion.112
  163.8 2.0 fusion.73
  166.1 47.7 %collective-permute-done.3 = bf16[256,2048]{1,0:T(8,128)(2,1)S(1)} collective-permute-done((bf16[256,2048]{1,0:T(8,128)(2,1)S(1)}, bf16[256,2048]{1,0:T(8,128)(2,1)S(1)}, u32[]{:S(2)}, u32[]{:S(2)}) %collective-permute-start.3) | collective-permute-done | bytes 1048608 | tf_op jit(solution)/shard_map/ppermute | solution.py:19
  214.6 12.7 %collective-permute-done.4 = bf16[128,2048]{1,0:T(8,128)(2,1)S(1)} collective-permute-done((bf16[128,2048]{1,0:T(8,128)(2,1)S(1)}, bf16[128,2048]{1,0:T(8,128)(2,1)S(1)}, u32[]{:S(2)}, u32[]{:S(2)}) %collective-permute-start.4) | collective-permute-done | bytes 524320 | tf_op jit(solution)/shard_map/ppermute | solution.py:19
  229.2 5.7 %collective-permute-done.5 = bf16[64,2048]{1,0:T(8,128)(2,1)} collective-permute-done((bf16[64,2048]{1,0:T(8,128)(2,1)}, bf16[64,2048]{1,0:T(8,128)(2,1)}, u32[]{:S(2)}, u32[]{:S(2)}) %collective-permute-start.5) | collective-permute-done | bytes 262176 | tf_op jit(solution)/shard_map/ppermute | solution.py:19
  (129 shorter events, 43.7 us)
Async XLA Ops:
  7.2 1.6 copy-start
  7.2 3.7 %copy-start.8 = (bf16[2048]{0:T(1024)(128)(2,1)S(1)}, bf16[2048]{0:T(1024)(128)(2,1)}, u32[]{:S(2)}) copy-start(bf16[2048]{0:T(1024)(128)(2,1)} %param.14) | copy-start | bytes 12292
  7.2 3.7 %copy-start.4 = (bf16[64,2048]{1,0:T(8,128)(2,1)S(1)}, bf16[64,2048]{1,0:T(8,128)(2,1)}, u32[]{:S(2)}) copy-start(bf16[64,2048]{1,0:T(8,128)(2,1)} %param.13) | copy-start | bytes 786436
  7.2 77.5 %all-gather.3.cloned.1.call-start = ((), (), s32[]{:S(2)}) async-start(), calls=%async_computation | async-start | bytes 1966080 | tf_op jit(solution)/shard_map/all_gather | solution.py:93
  10.8 153.0 %all-gather.5.cloned.1.call-start = ((), (), s32[]{:S(2)}) async-start(), calls=%async_computation.1 | async-start | bytes 1310720 | tf_op jit(solution)/shard_map/all_gather | solution.py:181
  11.2 31.4 %copy-start.2 = (bf16[1,2048,128]{2,1,0:T(8,128)(2,1)S(1)}, bf16[1,2048,128]{2,1,0:T(8,128)(2,1)}, u32[]{:S(2)}) copy-start(bf16[1,2048,128]{2,1,0:T(8,128)(2,1)} %param.20) | copy-start | bytes 1572868
  11.2 9.4 %collective-permute-start = (bf16[64,2048]{1,0:T(8,128)(2,1)S(1)}, bf16[64,2048]{1,0:T(8,128)(2,1)}, u32[]{:S(2)}, u32[]{:S(2)}) collective-permute-start(bf16[64,2048]{1,0:T(8,128)(2,1)S(1)} %fusion.66), channel_id=1, source_target_pairs={{0,1},{1,0},{2,3},{3,2},{4,5},{5,4},{6,7},{7,6},{8,9},{9,8},{10,11... | collective-permute-start | bytes 786440 | tf_op jit(solution)/shard_map/ppermute | solution.py:19
  21.9 13.2 %collective-permute-start.1 = (bf16[128,2048]{1,0:T(8,128)(2,1)S(1)}, bf16[128,2048]{1,0:T(8,128)(2,1)}, u32[]{:S(2)}, u32[]{:S(2)}) collective-permute-start(bf16[128,2048]{1,0:T(8,128)(2,1)S(1)} %maximum_select_fusion.3), channel_id=1, source_target_pairs={{0,2},{2,0},{1,3},{3,1},{4,6},{6,4},{5,7},{7,5},{8,10},{10,8},{9,1... | collective-permute-start | bytes 1572872 | tf_op jit(solution)/shard_map/ppermute | solution.py:19
  37.6 47.1 %collective-permute-start.2 = (bf16[256,2048]{1,0:T(8,128)(2,1)}, bf16[256,2048]{1,0:T(8,128)(2,1)}, u32[]{:S(2)}, u32[]{:S(2)}) collective-permute-start(bf16[256,2048]{1,0:T(8,128)(2,1)} %maximum_select_fusion.2), channel_id=1, source_target_pairs={{0,4},{4,0},{1,5},{5,1},{2,6},{6,2},{3,7},{7,3},{8,12},{12,8},{9,1... | collective-permute-start | bytes 3145736 | tf_op jit(solution)/shard_map/ppermute | solution.py:19
  43.8 45.5 %copy-start.9 = (f32[64]{0:T(128)S(1)}, f32[64]{0:T(128)}, u32[]{:S(2)}) copy-start(f32[64]{0:T(128)} %param.18) | copy-start | bytes 772
  94.0 1.0 copy-start.3
  95.0 1.0 copy-start.1
  97.2 4.5 %copy-start.6 = (bf16[512,64]{1,0:T(8,128)(2,1)S(1)}, bf16[512,64]{1,0:T(8,128)(2,1)}, u32[]{:S(2)}) copy-start(bf16[512,64]{1,0:T(8,128)(2,1)} %get-tuple-element.358) | copy-start | bytes 196612 | tf_op jit(solution)/shard_map/while
  102.9 4.4 %copy-start.5 = (bf16[2048,64]{1,0:T(8,128)(2,1)S(1)}, bf16[2048,64]{1,0:T(8,128)(2,1)}, u32[]{:S(2)}) copy-start(bf16[2048,64]{1,0:T(8,128)(2,1)} %get-tuple-element.359) | copy-start | bytes 786436 | tf_op jit(solution)/shard_map/while
  109.2 1.9 copy-start.7
  114.1 4.5 %copy-start.6 = (bf16[512,64]{1,0:T(8,128)(2,1)S(1)}, bf16[512,64]{1,0:T(8,128)(2,1)}, u32[]{:S(2)}) copy-start(bf16[512,64]{1,0:T(8,128)(2,1)} %get-tuple-element.358) | copy-start | bytes 196612 | tf_op jit(solution)/shard_map/while
  119.8 4.4 %copy-start.5 = (bf16[2048,64]{1,0:T(8,128)(2,1)S(1)}, bf16[2048,64]{1,0:T(8,128)(2,1)}, u32[]{:S(2)}) copy-start(bf16[2048,64]{1,0:T(8,128)(2,1)} %get-tuple-element.359) | copy-start | bytes 786436 | tf_op jit(solution)/shard_map/while
  126.1 1.9 copy-start.7
  131.1 4.5 %copy-start.6 = (bf16[512,64]{1,0:T(8,128)(2,1)S(1)}, bf16[512,64]{1,0:T(8,128)(2,1)}, u32[]{:S(2)}) copy-start(bf16[512,64]{1,0:T(8,128)(2,1)} %get-tuple-element.358) | copy-start | bytes 196612 | tf_op jit(solution)/shard_map/while
  136.7 4.4 %copy-start.5 = (bf16[2048,64]{1,0:T(8,128)(2,1)S(1)}, bf16[2048,64]{1,0:T(8,128)(2,1)}, u32[]{:S(2)}) copy-start(bf16[2048,64]{1,0:T(8,128)(2,1)} %get-tuple-element.359) | copy-start | bytes 786436 | tf_op jit(solution)/shard_map/while
  143.0 1.9 copy-start.7
  148.0 4.5 %copy-start.6 = (bf16[512,64]{1,0:T(8,128)(2,1)S(1)}, bf16[512,64]{1,0:T(8,128)(2,1)}, u32[]{:S(2)}) copy-start(bf16[512,64]{1,0:T(8,128)(2,1)} %get-tuple-element.358) | copy-start | bytes 196612 | tf_op jit(solution)/shard_map/while
  153.7 4.4 %copy-start.5 = (bf16[2048,64]{1,0:T(8,128)(2,1)S(1)}, bf16[2048,64]{1,0:T(8,128)(2,1)}, u32[]{:S(2)}) copy-start(bf16[2048,64]{1,0:T(8,128)(2,1)} %get-tuple-element.359) | copy-start | bytes 786436 | tf_op jit(solution)/shard_map/while
  160.0 1.9 copy-start.7
  166.0 47.8 %collective-permute-start.3 = (bf16[256,2048]{1,0:T(8,128)(2,1)S(1)}, bf16[256,2048]{1,0:T(8,128)(2,1)S(1)}, u32[]{:S(2)}, u32[]{:S(2)}) collective-permute-start(bf16[256,2048]{1,0:T(8,128)(2,1)S(1)} %select_convert_fusion), channel_id=1, source_target_pairs={{0,4},{4,0},{1,5},{5,1},{2,6},{6,2},{3,7},{7,3},{8,12},{12,8},{9,1... | collective-permute-start | bytes 3145736 | tf_op jit(solution)/shard_map/ppermute | solution.py:19
  214.6 12.7 %collective-permute-start.4 = (bf16[128,2048]{1,0:T(8,128)(2,1)S(1)}, bf16[128,2048]{1,0:T(8,128)(2,1)S(1)}, u32[]{:S(2)}, u32[]{:S(2)}) collective-permute-start(bf16[128,2048]{1,0:T(8,128)(2,1)S(1)} %select_convert_fusion.1), channel_id=1, source_target_pairs={{0,2},{2,0},{1,3},{3,1},{4,6},{6,4},{5,7},{7,5},{8,10},{10,8},{9,1... | collective-permute-start | bytes 1572872 | tf_op jit(solution)/shard_map/ppermute | solution.py:19
  228.2 6.7 %collective-permute-start.5 = (bf16[64,2048]{1,0:T(8,128)(2,1)}, bf16[64,2048]{1,0:T(8,128)(2,1)}, u32[]{:S(2)}, u32[]{:S(2)}) collective-permute-start(bf16[64,2048]{1,0:T(8,128)(2,1)} %select_convert_fusion.2), channel_id=1, source_target_pairs={{0,1},{1,0},{2,3},{3,2},{4,5},{5,4},{6,7},{7,6},{8,9},{9,8},{10,11... | collective-permute-start | bytes 786440 | tf_op jit(solution)/shard_map/ppermute | solution.py:19
Sparse Core Ops, SparseCore 0:
  10.9 22.3 all-gather.2
  42.0 15.9 all-gather.4
where the time goes:
time: 244 us; the launch traced here: 243 us
  waiting for transfers between devices  125 us (51%)
  matrix products  44.9 us (18%)
  other arithmetic  39.1 us (16%)
  between operations  15 us (6%)
  local copies, waits for them, and re-layouts  11.4 us (5%)
  starting transfers between devices  7.8 us (3%)
    ppermute x6, waiting for transfers between devices, from_partner(): return lax.ppermute(block, axis, route)  125 us
    dot_general x12, matrix products, add_block(): jnp.dot(weights.astype(jnp.bfloat16), all_values[block_low:block_high], p...  22.7 us
    reduce_sum x8, other arithmetic, add_block(): jnp.sum(weights, axis=1)  17.5 us
    dot_general x12, matrix products, score_block(): jnp.einsum('qd,kd->qk', block_queries, all_keys[block_low:block_high], pr...  16.5 us
    lt x8, other arithmetic, allowed_in(): block_pos < sink_total  7.82 us
    ppermute x6, starting transfers between devices, from_partner(): return lax.ppermute(block, axis, route)  7.72 us
  transfers between devices with their start and end apart: 8, of which 6 were waited for; matrix products, arithmetic and copies ran while one was open for 35% of the time, Pallas kernels for 0%

commit v1 on v0

v1 whole, which is shorter than its diff:
```python
import functools

import jax
import jax.numpy as jnp
from jax import lax
from jax.experimental import pallas as pl
from jax.experimental.pallas import tpu as pltpu
from jax.sharding import PartitionSpec as P

epsilon = 1e-05
theta_base = 1000000.0
masked_score = -1e30
vmem_bytes = 48 * 1024 * 1024


def rope_tables(positions, head_dim):
    half_dim = head_dim // 2
    inverse_freq = theta_base ** (-2.0 * jnp.arange(half_dim, dtype=jnp.float32) / head_dim)
    angles = positions.astype(jnp.float32)[:, None] * inverse_freq[None, :]
    cosine = jnp.cos(angles)
    sine = jnp.sin(angles)
    return (
        jnp.concatenate([cosine] * 4, axis=1),
        jnp.concatenate([-sine, sine] * 2, axis=1),
    )


def lanes_of(value):
    return lax.broadcasted_iota(jnp.int32, value.shape, value.ndim - 1)


def norm_rope_pair(pair, gain, cosine, sine, head_dim):
    lane = lanes_of(pair)
    low = lane < head_dim
    squared = pair * pair
    low_sum = jnp.sum(jnp.where(low, squared, 0.0), axis=1, keepdims=True)
    high_sum = jnp.sum(jnp.where(low, 0.0, squared), axis=1, keepdims=True)
    inverse = jnp.where(
        low,
        lax.rsqrt(low_sum / head_dim + epsilon),
        lax.rsqrt(high_sum / head_dim + epsilon),
    )
    normed = pair * inverse * gain
    half_dim = head_dim // 2
    swapped = jnp.where(
        lane % head_dim < half_dim,
        pltpu.roll(normed, 2 * head_dim - half_dim, 1),
        pltpu.roll(normed, half_dim, 1),
    )
    return normed * cosine + swapped * sine


def table_entry(table, index):
    found = jnp.int32(table[0])
    for place in range(1, len(table)):
        found = jnp.where(index == place, jnp.int32(table[place]), found)
    return found


def stage_kernel(plan, final, length_ref, window_ref, *refs):
    old, offsets, parts = plan["old"], plan["offsets"], plan["parts"]
    pieces, head_dim, ring = plan["pieces"], plan["head_dim"], plan["ring"]
    new = sum(parts_of_block for parts_of_block in parts)
    refs = list(refs)

    def take(count):
        taken = refs[:count]
        del refs[:count]
        return taken

    tokens = take(new)
    norm_gain, query_gain, key_gain, cosine_ref, sine_ref, keys_ref, values_ref, reach_ref = take(8)
    weights = take(pieces)
    if old:
        queries_in, keyval_in, stats_in = take(3)
    if final:
        heads_out, fresh_out = take(2)
    else:
        queries_out, keyval_out, stats_out = take(3)
    normed_ref, projected_ref = take(2)
    if final:
        queries_out, keyval_out, stats_out = take(3)
    new_keys_ref, new_values_ref = take(2)

    fresh_blocks = len(parts)
    blocks = old + fresh_blocks
    members = len(ring)
    rows = normed_ref.shape[0] // fresh_blocks
    lanes = 2 * head_dim
    query_cols = projected_ref.shape[1] - lanes
    pairs = query_cols // lanes
    count = 2 * pairs * rows
    length = length_ref[0]
    window_len = window_ref[0]
    rank = lax.axis_index("tensor")
    own = lax.axis_index("dp")
    if length_ref.shape[0] > 1:
        length = length_ref[rank // members]
        window_len = window_ref[rank // members]
    place = table_entry([ring.index(one) for one in range(members)], rank % members)
    ids = [table_entry(ring, (place + offset + members) % members) for offset in offsets]

    gain = norm_gain[...].astype(jnp.float32)
    start = 0
    for part in tokens:
        values = part[...].astype(jnp.float32)
        mean_square = jnp.mean(values * values, axis=1, keepdims=True)
        normed_ref[pl.ds(start, part.shape[0]), :] = (
            values * lax.rsqrt(mean_square + epsilon) * gain
        ).astype(jnp.bfloat16)
        start += part.shape[0]
    depth = weights[0].shape[0]
    total = None
    for piece in range(pieces):
        from_column = pl.multiple_of((own ^ piece) * depth, depth)
        term = jnp.dot(
            normed_ref[:, pl.ds(from_column, depth)],
            weights[piece][...],
            preferred_element_type=jnp.float32,
        )
        total = term if total is None else total + term
    projected_ref[...] = total
    scale = head_dim ** (-0.5)

    if old:
        queries_out[pl.ds(0, old * count), :] = queries_in[...]
        keyval_out[pl.ds(0, old * rows), :] = keyval_in[...]
    query_gains = jnp.concatenate([query_gain[...]] * 2, axis=1)
    key_gains = jnp.concatenate([key_gain[...]] * 2, axis=1)
    for block in range(fresh_blocks):
        from_row = pl.multiple_of(ids[old + block] * rows, rows)
        cosine = cosine_ref[pl.ds(from_row, rows), :]
        sine = sine_ref[pl.ds(from_row, rows), :]
        here = pl.ds(block * rows, rows)
        for pair in range(pairs):
            roped = norm_rope_pair(
                projected_ref[here, pl.ds(pair * lanes, lanes)],
                query_gains,
                cosine,
                sine,
                head_dim,
            )
            scaled = roped.astype(jnp.bfloat16).astype(jnp.float32) * scale
            low = lanes_of(scaled) < head_dim
            to_row = (old + block) * count + 2 * pair * rows
            queries_out[pl.ds(to_row, rows), :] = jnp.where(low, scaled, 0.0).astype(jnp.bfloat16)
            queries_out[pl.ds(to_row + rows, rows), :] = jnp.where(low, 0.0, scaled).astype(
                jnp.bfloat16
            )
        last = projected_ref[here, pl.ds(query_cols, lanes)]
        roped = norm_rope_pair(last, key_gains, cosine, sine, head_dim)
        keyval_out[pl.ds((old + block) * rows, rows), :] = jnp.where(
            lanes_of(last) < head_dim, roped, last
        ).astype(jnp.bfloat16)

    keyval = keyval_out[...].astype(jnp.float32)
    low = lanes_of(keyval) < head_dim
    new_keys_ref[...] = jnp.where(low, keyval, pltpu.roll(keyval, head_dim, 1)).astype(jnp.bfloat16)
    new_values_ref[...] = jnp.where(low, 1.0, keyval).astype(jnp.bfloat16)

    token = lax.broadcasted_iota(jnp.int32, (1, blocks * rows), 1)
    key_token = token % rows + ids[0] * rows
    for block in range(1, blocks):
        key_token = jnp.where(token // rows == block, token % rows + ids[block] * rows, key_token)
    row_token = lax.broadcasted_iota(jnp.int32, (count, 1), 0) % rows

    def first_token(block, low_block, high_block):
        found = ids[low_block]
        for other in range(low_block + 1, high_block):
            found = jnp.where(block == other, ids[other], found)
        return found * rows

    def attend_new(block, unused):
        span = pl.ds(pl.multiple_of(block * count, count), count)
        queries = queries_out[span, :]
        at = first_token(block, old, blocks) + row_token
        scores = jnp.dot(queries, keys_ref[...], preferred_element_type=jnp.float32)
        masked = jnp.where(reach_ref[...] > length + at - window_len, scores, masked_score)
        near_scores = lax.dot_general(
            queries,
            new_keys_ref[...],
            (((1,), (1,)), ((), ())),
            preferred_element_type=jnp.float32,
        )
        near_masked = jnp.where(key_token <= at, near_scores, masked_score)
        row_max = jnp.maximum(
            jnp.max(masked, axis=1, keepdims=True),
            jnp.max(near_masked, axis=1, keepdims=True),
        )
        unnormed = jnp.exp(masked - row_max).astype(jnp.bfloat16)
        near_unnormed = jnp.exp(near_masked - row_max).astype(jnp.bfloat16)
        sums = jnp.dot(
            unnormed, values_ref[...], preferred_element_type=jnp.float32
        ) + jnp.dot(near_unnormed, new_values_ref[...], preferred_element_type=jnp.float32)
        stats_out[span, :] = jnp.where(lanes_of(sums) == 0, row_max, sums)
        return unused

    lax.fori_loop(old, blocks, attend_new, 0)

    def attend_old(block, unused):
        span = pl.ds(pl.multiple_of(block * count, count), count)
        at = first_token(block, 0, old) + row_token
        near_scores = lax.dot_general(
            queries_in[span, :],
            new_keys_ref[pl.ds(old * rows, fresh_blocks * rows), :],
            (((1,), (1,)), ((), ())),
            preferred_element_type=jnp.float32,
        )
        near_masked = jnp.where(key_token[:, old * rows :] <= at, near_scores, masked_score)
        before = stats_in[span, :]
        old_max = before[:, 0:1]
        before = jnp.where(lanes_of(before) == 0, before[:, 1:2], before)
        row_max = jnp.maximum(jnp.max(near_masked, axis=1, keepdims=True), old_max)
        unnormed = jnp.exp(near_masked - row_max).astype(jnp.bfloat16)
        sums = before * jnp.exp(old_max - row_max) + jnp.dot(
            unnormed,
            new_values_ref[pl.ds(old * rows, fresh_blocks * rows), :],
            preferred_element_type=jnp.float32,
        )
        stats_out[span, :] = jnp.where(lanes_of(sums) == 0, row_max, sums)
        return unused

    if old:
        lax.fori_loop(0, old, attend_old, 0)

    if final:
        for block in range(blocks):
            target = pl.ds(pl.multiple_of(ids[block] * rows, rows), rows)
            fresh_out[target, :] = keyval_out[pl.ds(block * rows, rows), :]
            for pair in range(pairs):
                joined = []
                for head in range(2):
                    from_row = block * count + (2 * pair + head) * rows
                    sums = stats_out[pl.ds(from_row, rows), :]
                    joined.append(sums / sums[:, 1:2])
                heads_out[target, pl.ds(pair * lanes, lanes)] = jnp.where(
                    lanes_of(joined[1]) < head_dim,
                    pltpu.roll(joined[0], head_dim, 1),
                    joined[1],
                ).astype(jnp.bfloat16)


def output_kernel(piece_count, heads_ref, *refs):
    weights = refs[:piece_count]
    attended, total = refs[piece_count:]
    step = pl.program_id(0)

    @pl.when(step == 0)
    def _():
        total[...] = jnp.zeros_like(total)

    for piece in range(piece_count):
        total[piece] += jnp.dot(
            heads_ref[0], weights[piece][...], preferred_element_type=jnp.float32
        )

    @pl.when(step == pl.num_programs(0) - 1)
    def _():
        width = weights[0].shape[1]
        for piece in range(piece_count):
            start = pl.multiple_of((lax.axis_index("dp") ^ piece) * width, width)
            attended[:, pl.ds(start, width)] = total[piece].astype(attended.dtype)


def whole_vmem():
    return pl.BlockSpec(memory_space=pltpu.VMEM)


def in_smem():
    return pl.BlockSpec(memory_space=pltpu.SMEM)


def run_stage(plan, final, lengths, windows, tokens, shared, weights, state):
    rows = plan["rows"]
    head_dim = plan["head_dim"]
    old, fresh_blocks = plan["old"], len(plan["parts"])
    blocks = old + fresh_blocks
    lanes = 2 * head_dim
    width = weights[0].shape[1]
    query_cols = width - lanes
    count = rows * query_cols // head_dim
    features = tokens[0].shape[1]
    slots = shared[-1].shape[1]
    state_shapes = [
        ((blocks * count, lanes), jnp.bfloat16),
        ((blocks * rows, lanes), jnp.bfloat16),
        ((blocks * count, lanes), jnp.float32),
    ]
    scratch = [
        pltpu.VMEM((fresh_blocks * rows, features), jnp.bfloat16),
        pltpu.VMEM((fresh_blocks * rows, width), jnp.float32),
    ]
    if final:
        out_shape = (
            jax.ShapeDtypeStruct((blocks * rows, query_cols), jnp.bfloat16),
            jax.ShapeDtypeStruct((blocks * rows, lanes), jnp.bfloat16),
        )
        scratch += [pltpu.VMEM(*one) for one in state_shapes]
    else:
        out_shape = tuple(jax.ShapeDtypeStruct(*one) for one in state_shapes)
    scratch += [pltpu.VMEM((blocks * rows, lanes), jnp.bfloat16)] * 2
    operands = [*tokens, *shared, *weights, *state]
    return pl.pallas_call(
        functools.partial(stage_kernel, plan, final),
        out_shape=out_shape,
        in_specs=[in_smem()] * 2 + [whole_vmem()] * len(operands),
        out_specs=(whole_vmem(),) * len(out_shape),
        scratch_shapes=scratch,
        compiler_params=pltpu.CompilerParams(vmem_limit_bytes=vmem_bytes),
        cost_estimate=pl.CostEstimate(
            flops=2 * fresh_blocks * rows * features * width
            + 16 * fresh_blocks * count * slots * lanes,
            bytes_accessed=4 * 1024 * 1024,
            transcendentals=fresh_blocks * count * slots,
        ),
    )(lengths, windows, *operands)


def body(
    tokens,
    norm_gain,
    query_weight,
    keyval_weight,
    query_gain,
    key_gain,
    output_weight,
    keyval_cache,
    cached_lengths,
    sink_count,
    window,
):
    tensor_rank = lax.axis_index("tensor")
    tensor_size = lax.axis_size("tensor")
    dp_size = lax.axis_size("dp")
    head_dim = query_gain.shape[0]
    kv_heads = keyval_weight.shape[2] // head_dim
    member = tensor_rank % kv_heads
    request_slot = tensor_rank // kv_heads
    length = cached_lengths[request_slot]
    sink_total = sink_count[request_slot]
    block_cols = query_weight.shape[1] // kv_heads
    rows = tokens.shape[0]
    new_rows = rows * kv_heads

    if tensor_size == kv_heads == 8:
        ring = [0, 2, 4, 6, 7, 5, 3, 1]
    else:
        ring = list(range(kv_heads))
    def ring_route(step):
        route = []
        for group in range(0, tensor_size, kv_heads):
            for place in range(kv_heads):
                route.append(
                    (group + ring[place], group + ring[(place + step) % kv_heads])
                )
        return route

    def forward(block):
        return lax.ppermute(block, "tensor", ring_route(1))

    def backward(block):
        return lax.ppermute(block, "tensor", ring_route(-1))

    def from_dp(block, apart):
        return lax.ppermute(block, "dp", [(one, one ^ apart) for one in range(dp_size)])

    query_local = lax.dynamic_slice_in_dim(query_weight, member * block_cols, block_cols, 1)
    keyval_local = lax.dynamic_slice_in_dim(keyval_weight, member * head_dim, head_dim, 2)
    combined = jnp.concatenate([query_local, keyval_local[0], keyval_local[1]], axis=1)
    far = dp_size // 2
    pieces = {0: combined}
    apart = far
    while apart >= 1:
        for known in list(pieces):
            pieces[known ^ apart] = from_dp(pieces[known], apart)
        apart //= 2
    weights = [pieces[k] for k in range(dp_size)]

    positions = length + jnp.arange(new_rows, dtype=jnp.int32)
    cosine, sine = rope_tables(positions, head_dim)
    cache_rows = keyval_cache[0]
    slots = cache_rows.shape[0]
    key_columns = cache_rows[:, :head_dim].T
    keys = jnp.concatenate([key_columns, key_columns], axis=0)
    values = jnp.concatenate(
        [jnp.ones((slots, head_dim), jnp.bfloat16), cache_rows[:, head_dim:]], axis=1
    )
    slot = jnp.arange(slots, dtype=jnp.int32)
    far_away = jnp.int32(1 << 29)
    reach = jnp.where(slot < length, jnp.where(slot < sink_total, far_away, slot), -far_away)
    shared = (
        norm_gain[None],
        query_gain[None],
        key_gain[None],
        cosine,
        sine,
        keys,
        values,
        reach[None],
    )

    def after(value, *others):
        return lax.optimization_barrier((value, *others))[0]

    ahead, behind = tokens, tokens
    arrived, arrived_offsets = [tokens], [0]
    offsets = []
    state = ()
    steps = (kv_heads - 1) // 2
    for step in range(1, steps + 2):
        final = step > steps
        if final:
            half = rows // 2
            arrived = [forward(ahead[:half]), backward(behind[half:])]
            arrived_offsets = [step]
            parts = (2,)
        else:
            ahead, behind = forward(ahead), backward(behind)
            arrived += [ahead, behind]
            arrived_offsets += [-step, step]
            parts = (1,) * len(arrived)
        if step == 1:
            far_out = from_dp(after(output_weight, pieces[far], ahead, behind), far)
        offsets += arrived_offsets
        plan = {
            "old": len(offsets) - len(parts),
            "offsets": tuple(offsets),
            "parts": parts,
            "pieces": dp_size,
            "head_dim": head_dim,
            "ring": tuple(ring),
            "rows": rows,
        }
        state = run_stage(
            plan, final, cached_lengths, window, arrived, shared, weights, state
        )
        if step == steps:
            out_pieces = {0: output_weight, far: after(far_out, *state)}
        arrived, arrived_offsets = [], []
    head_out, fresh = state
    apart = far // 2
    while apart >= 1:
        for known in list(out_pieces):
            out_pieces[known ^ apart] = from_dp(out_pieces[known], apart)
        apart //= 2
    out_weights = [out_pieces[k] for k in range(dp_size)]

    groups = [
        list(range(group, group + kv_heads)) for group in range(0, tensor_size, kv_heads)
    ]
    parts = lax.all_to_all(
        head_out.reshape(kv_heads, rows, block_cols),
        "tensor",
        0,
        0,
        axis_index_groups=groups,
    )
    width = output_weight.shape[1]
    attended = pl.pallas_call(
        functools.partial(output_kernel, dp_size),
        grid=(kv_heads,),
        out_shape=jax.ShapeDtypeStruct((rows, width * dp_size), jnp.bfloat16),
        in_specs=[
            pl.BlockSpec((1, rows, block_cols), lambda step: (step, 0, 0)),
        ]
        + [pl.BlockSpec((block_cols, width), lambda step: (step, 0))] * dp_size,
        out_specs=pl.BlockSpec((rows, width * dp_size), lambda step: (0, 0)),
        scratch_shapes=[pltpu.VMEM((dp_size, rows, width), jnp.float32)],
        compiler_params=pltpu.CompilerParams(vmem_limit_bytes=vmem_bytes),
    )(parts, *out_weights)
    return (attended, fresh[None])


def solution(mesh):
    in_specs = (
        P(("dp", "tensor"), None),
        P(),
        P("dp", None),
        P(None, "dp", None),
        P(),
        P(),
        P(None, "dp"),
        P(("dp", "tensor"), None, None),
        P("dp"),
        P("dp"),
        P("dp"),
    )
    out_specs = (P(("dp", "tensor"), None), P(("dp", "tensor"), None, None))
    return jax.shard_map(body, mesh=mesh, in_specs=in_specs, out_specs=out_specs, check_vma=False)
```

time: 244 us -> 102 us (0.42)
  waiting for transfers between devices: 125 us -> 23.1 us
  matrix products: 44.9 us -> 0 us
  Pallas kernels: 0 us -> 36.9 us
  other arithmetic: 39.1 us -> 2.69 us
  blocking collectives: 0 us -> 13.1 us
  between operations: 15 us -> 2.79 us
  starting transfers between devices: 7.8 us -> 13.1 us
    ppermute x6 -> x14, waiting for transfers between devices: 125 us -> 23.1 us  [the longest x4 11.6 us: forward(): return lax.ppermute(block, 'tensor', ring_route(1))]
    dot_general x26 -> x0, matrix products: 44.9 us -> none  [the longest x12 22.7 us: add_block(): jnp.dot(weights.astype(jnp.bfloat16), all_values[block_low:block_high], p...]
    pallas_call x0 -> x5, Pallas kernels: none -> 36.9 us  [the longest x4 30.4 us: run_stage(): pl.pallas_call(functools.partial(stage_kernel, plan, final), out_shape=ou...]
    reduce_sum x11 -> x0, other arithmetic: 18 us -> none  [the longest x8 17.5 us: add_block(): jnp.sum(weights, axis=1)]
    all_to_all x0 -> x1, blocking collectives: none -> 13.1 us  [body(): lax.all_to_all(head_out.reshape(kv_heads, rows, block_cols), 'tensor', 0,...]
    lt x9 -> x0, other arithmetic: 7.83 us -> none  [the longest x8 7.82 us: allowed_in(): block_pos < sink_total]
    ppermute x6 -> x14, starting transfers between devices: 7.72 us -> 13.1 us  [the longest x4 6.26 us: forward(): return lax.ppermute(block, 'tensor', ring_route(1))]
    select_n x2 -> x1, other arithmetic: 3.76 us -> 0.02 us  [body(): jnp.where(slot < length, jnp.where(slot < sink_total, far_away, slot), -f...]
  transfers between devices with their start and end apart: 8 -> 14, of which waited for: 6 -> 6; matrix products, arithmetic and copies ran while one was open for 35% -> 6% of each run, Pallas kernels for 0% -> 30%
where the time goes in v1:
time: 102 us; the launch traced here: 101 us
  Pallas kernels  36.9 us (36%)
  waiting for transfers between devices  23.1 us (23%)
  starting transfers between devices  13.1 us (13%)
  blocking collectives  13.1 us (13%)
  local copies, waits for them, and re-layouts  9.71 us (10%)
  between operations  2.79 us (3%)
  other arithmetic  2.69 us (3%)
    pallas_call x4, Pallas kernels, run_stage(): pl.pallas_call(functools.partial(stage_kernel, plan, final), out_shape=ou...  30.4 us
    all_to_all x1, blocking collectives, body(): lax.all_to_all(head_out.reshape(kv_heads, rows, block_cols), 'tensor', 0,...  13.1 us
    ppermute x4, waiting for transfers between devices, forward(): return lax.ppermute(block, 'tensor', ring_route(1))  11.6 us
    ppermute x6, waiting for transfers between devices, from_dp(): lax.ppermute(block, 'dp', [(one, one ^ apart) for one in range(dp_size)])  8.76 us
    pallas_call x1, Pallas kernels, body(): pl.pallas_call(functools.partial(output_kernel, dp_size), grid=(kv_heads,...  6.53 us
    ppermute x4, starting transfers between devices, forward(): return lax.ppermute(block, 'tensor', ring_route(1))  6.26 us
    unnamed x18, local copies, waits for them, and re-layouts  5 us
    ppermute x6, starting transfers between devices, from_dp(): lax.ppermute(block, 'dp', [(one, one ^ apart) for one in range(dp_size)])  4.69 us
  transfers between devices with their start and end apart: 14, of which 6 were waited for; matrix products, arithmetic and copies ran while one was open for 6% of the time, Pallas kernels for 30%

profile of v1, /device:TPU:0, one launch (start us, length us, event | category | flops | bytes accessed | tf_op | source)
XLA Modules:
  0.0 101.4 jit_solution(11649284162929779532)
XLA Ops:
  0.7 1.6 %copy-done = bf16[512,2048]{1,0:T(8,128)(2,1)S(1)} copy-done((bf16[512,2048]{1,0:T(8,128)(2,1)S(1)}, bf16[512,2048]{1,0:T(8,128)(2,1)}, u32[]{:S(2)}) %copy-start) | copy-done | bytes 2097176
  2.3 1.1 %dynamic-slice_bitcast_fusion.1 = (bf16[512,64]{1,0:T(8,128)(2,1)S(1)}, bf16[512,64]{1,0:T(8,128)(2,1)S(1)}) fusion(bf16[2,512,512]{2,1,0:T(8,128)(2,1)} %param.14, s32[]{:T(128)S(6)} %select_n.43, s32[]{:T(128)S(6)} %add.30), kind=kLoop, calls=%fused_computation.8 | loop fusion | bytes 262152 | tf_op jit(solution)/shard_map/squeeze | solution.py:369
  3.5 3.0 %collective-permute-start.9 = (bf16[512,384]{1,0:T(8,128)(2,1)S(1)}, bf16[512,384]{1,0:T(8,128)(2,1)}, u32[]{:S(2)}, u32[]{:S(2)}) collective-permute-start(bf16[512,384]{1,0:T(8,128)(2,1)S(1)} %pad_maximum_fusion.1.refs_11_.refs_10_), channel_id=1, source_target_pairs={{0,16},{8,24},{16,0},{24,8},{1,17},{9,25},{17,1},{25,9},{2,18},{10... | collective-permute-start | bytes 1179656 | tf_op jit(solution)/shard_map/ppermute | solution.py:365
  6.5 1.6 %collective-permute-start = (bf16[64,2048]{1,0:T(8,128)(2,1)}, bf16[64,2048]{1,0:T(8,128)(2,1)}, u32[]{:S(2)}, u32[]{:S(2)}) collective-permute-start(bf16[64,2048]{1,0:T(8,128)(2,1)} %refs_0_.2), channel_id=1, source_target_pairs={{0,2},{2,4},{4,6},{6,7},{7,5},{5,3},{3,1},{1,0},{8,10},{10,12},{12... | collective-permute-start | bytes 786440 | tf_op jit(solution)/shard_map/ppermute | solution.py:359
  8.1 0.5 collective-permute-start.4
  9.2 5.4 %collective-permute-done.refs_1_ = bf16[64,2048]{1,0:T(8,128)(2,1)} collective-permute-done((bf16[64,2048]{1,0:T(8,128)(2,1)}, bf16[64,2048]{1,0:T(8,128)(2,1)}, u32[]{:S(2)}, u32[]{:S(2)}) %collective-permute-start) | collective-permute-done | bytes 262176 | tf_op jit(solution)/shard_map/ppermute | solution.py:359
  14.6 1.3 %collective-permute-done.4.refs_2_ = bf16[64,2048]{1,0:T(8,128)(2,1)} collective-permute-done((bf16[64,2048]{1,0:T(8,128)(2,1)}, bf16[64,2048]{1,0:T(8,128)(2,1)}, u32[]{:S(2)}, u32[]{:S(2)}) %collective-permute-start.4) | collective-permute-done | bytes 262176 | tf_op jit(solution)/shard_map/ppermute | solution.py:362
  15.9 1.6 %collective-permute-start.12 = (bf16[2048,512]{1,0:T(8,128)(2,1)}, bf16[2048,512]{1,0:T(8,128)(2,1)}, u32[]{:S(2)}, u32[]{:S(2)}) collective-permute-start(bf16[2048,512]{1,0:T(8,128)(2,1)} %refs_0_.3), channel_id=1, source_target_pairs={{0,16},{8,24},{16,0},{24,8},{1,17},{9,25},{17,1},{25,9},{2,18},{10... | collective-permute-start | bytes 6291464 | tf_op jit(solution)/shard_map/ppermute | solution.py:365
  17.5 1.0 fusion
  18.5 1.0 %fusion.1 = (bf16[2048,64]{1,0:T(8,128)(2,1)}, bf16[64,2048]{0,1:T(8,128)(2,1)S(1)}) fusion(bf16[2048,128]{1,0:T(8,128)(2,1)S(1)} %bitcast.25), kind=kLoop, calls=%fused_computation.15 | loop fusion | bytes 1048576 | tf_op jit(solution)/shard_map/slice | solution.py:386
  19.6 1.1 %pad_maximum_fusion = bf16[128,2048]{0,1:T(8,128)(2,1)} fusion(bf16[64,2048]{0,1:T(8,128)(2,1)S(1)} %get-tuple-element.31), kind=kLoop, calls=%fused_computation.1 | loop fusion | flops 1048576 | bytes 786432 | tf_op jit(solution)/shard_map/concatenate | solution.py:384
  20.6 1.6 %collective-permute-start.1 = (bf16[64,2048]{1,0:T(8,128)(2,1)}, bf16[64,2048]{1,0:T(8,128)(2,1)}, u32[]{:S(2)}, u32[]{:S(2)}) collective-permute-start(bf16[64,2048]{1,0:T(8,128)(2,1)} %collective-permute-done.refs_1_), channel_id=1, source_target_pairs={{0,2},{2,4},{4,6},{6,7},{7,5},{5,3},{3,1},{1,0},{8,10},{10,12},{12... | collective-permute-start | bytes 786440 | tf_op jit(solution)/shard_map/ppermute | solution.py:359
  22.7 0.5 pad_maximum_fusion.2
  24.5 1.2 %copy.21.refs_8_.refs_7_ = bf16[128,2048]{1,0:T(8,128)(2,1)S(1)} copy(bf16[128,2048]{0,1:T(8,128)(2,1)} %pad_maximum_fusion) | data formatting | bytes 1048576 | tf_op jit(solution)/shard_map/concatenate | solution.py:384
  25.7 1.3 %concatenate.18.refs_9_.refs_8_ = bf16[2048,128]{1,0:T(8,128)(2,1)S(1)} pad(bf16[2048,64]{1,0:T(8,128)(2,1)} %get-tuple-element.30, bf16[]{:T(256)} %constant.20.clone.1), padding=0_0x64_0 | pad | bytes 786434 | tf_op jit(solution)/shard_map/concatenate | solution.py:385
  27.1 2.6 %collective-permute-done.1.refs_0_ = bf16[64,2048]{1,0:T(8,128)(2,1)} collective-permute-done((bf16[64,2048]{1,0:T(8,128)(2,1)}, bf16[64,2048]{1,0:T(8,128)(2,1)}, u32[]{:S(2)}, u32[]{:S(2)}) %collective-permute-start.1) | collective-permute-done | bytes 262176 | tf_op jit(solution)/shard_map/ppermute | solution.py:359
  29.7 1.6 %collective-permute-start.2 = (bf16[64,2048]{1,0:T(8,128)(2,1)}, bf16[64,2048]{1,0:T(8,128)(2,1)S(1)}, u32[]{:S(2)}, u32[]{:S(2)}) collective-permute-start(bf16[64,2048]{1,0:T(8,128)(2,1)} %collective-permute-done.1.refs_0_), channel_id=1, source_target_pairs={{0,2},{2,4},{4,6},{6,7},{7,5},{5,3},{3,1},{1,0},{8,10},{10,12},{12... | collective-permute-start | bytes 786440 | tf_op jit(solution)/shard_map/ppermute | solution.py:359
  31.3 0.5 collective-permute-start.6
  31.7 0.9 copy-done.5
  32.7 6.1 %shard_map.122 = (bf16[768,128]{1,0:T(8,128)(2,1)S(1)}, bf16[192,128]{1,0:T(8,128)(2,1)S(1)}, f32[768,128]{1,0:T(8,128)S(1)}) custom-call(s32[1]{0:T(128)} %copy.22.length_ref, s32[1]{0:T(128)S(6)} %copy.24.window_ref, bf16[64,2048]{1,0:T(8,128)(2,1)S(1)} %copy-done.5, bf16[64,2048]{1,0:T(8,128)(2,1)} %collective-permute-done.refs_1_, ...), custom_call_target="tpu_custom_call" | custom-call | flops 3523215360 | bytes 4194304 | tf_op jit(solution)/shard_map/pallas_call | solution.py:303
  38.8 6.6 %shard_map.123 = (bf16[1280,128]{1,0:T(8,128)(2,1)S(1)}, bf16[320,128]{1,0:T(8,128)(2,1)S(1)}, f32[1280,128]{1,0:T(8,128)S(1)}) custom-call(s32[1]{0:T(128)} %copy.22.length_ref, s32[1]{0:T(128)S(6)} %copy.24.window_ref, bf16[64,2048]{1,0:T(8,128)(2,1)} %collective-permute-done.1.refs_0_, bf16[64,2048]{1,0:T(8,128)(2,1)} %collective-permute-done.5.refs_1_, ...), custom_call_target="tpu_custom_call" | custom-call | flops 2348810240 | bytes 4194304 | tf_op jit(solution)/shard_map/pallas_call | solution.py:303
  45.4 8.7 %shard_map.124 = (bf16[1792,128]{1,0:T(8,128)(2,1)S(1)}, bf16[448,128]{1,0:T(8,128)(2,1)S(1)}, f32[1792,128]{1,0:T(8,128)}) custom-call(s32[1]{0:T(128)} %copy.22.length_ref, s32[1]{0:T(128)S(6)} %copy.24.window_ref, bf16[64,2048]{1,0:T(8,128)(2,1)S(1)} %collective-permute-done.2.refs_0_, bf16[64,2048]{1,0:T(8,128)(2,1)S(1)} %collective-permute-done.6.refs_1_, ...), custom_call_target="tpu_custom_call" | custom-call | flops 2348810240 | bytes 4194304 | tf_op jit(solution)/shard_map/pallas_call | solution.py:303
  54.1 8.7 %collective-permute-done.12.refs_2_ = bf16[2048,512]{1,0:T(8,128)(2,1)} collective-permute-done((bf16[2048,512]{1,0:T(8,128)(2,1)}, bf16[2048,512]{1,0:T(8,128)(2,1)}, u32[]{:S(2)}, u32[]{:S(2)}) %collective-permute-start.12) | collective-permute-done | bytes 2097184 | tf_op jit(solution)/shard_map/ppermute | solution.py:365
  62.9 1.5 %collective-permute-start.3 = (bf16[32,2048]{1,0:T(8,128)(2,1)S(1)}, bf16[32,2048]{1,0:T(8,128)(2,1)S(1)}, u32[]{:S(2)}, u32[]{:S(2)}) collective-permute-start(bf16[32,2048]{1,0:T(8,128)(2,1)S(1)} %slice.24), channel_id=1, source_target_pairs={{0,2},{2,4},{4,6},{6,7},{7,5},{5,3},{3,1},{1,0},{8,10},{10,12},{12... | collective-permute-start | bytes 393224 | tf_op jit(solution)/shard_map/ppermute | solution.py:359
  64.5 0.8 collective-permute-start.7
  65.2 3.6 %collective-permute-done.3.refs_0_ = bf16[32,2048]{1,0:T(8,128)(2,1)S(1)} collective-permute-done((bf16[32,2048]{1,0:T(8,128)(2,1)S(1)}, bf16[32,2048]{1,0:T(8,128)(2,1)S(1)}, u32[]{:S(2)}, u32[]{:S(2)}) %collective-permute-start.3) | collective-permute-done | bytes 131104 | tf_op jit(solution)/shard_map/ppermute | solution.py:359
  68.9 1.5 %collective-permute-done.7.refs_1_ = bf16[32,2048]{1,0:T(8,128)(2,1)S(1)} collective-permute-done((bf16[32,2048]{1,0:T(8,128)(2,1)S(1)}, bf16[32,2048]{1,0:T(8,128)(2,1)S(1)}, u32[]{:S(2)}, u32[]{:S(2)}) %collective-permute-start.7) | collective-permute-done | bytes 131104 | tf_op jit(solution)/shard_map/ppermute | solution.py:362
  70.3 1.2 %copy-done.2 = f32[1792,128]{1,0:T(8,128)S(1)} copy-done((f32[1792,128]{1,0:T(8,128)S(1)}, f32[1792,128]{1,0:T(8,128)}, u32[]{:S(2)}) %copy-start.2) | copy-done | bytes 917528
  71.5 9.0 %shard_map.125 = (bf16[512,256]{1,0:T(8,128)(2,1)S(1)}, bf16[512,128]{1,0:T(8,128)(2,1)}) custom-call(s32[1]{0:T(128)} %copy.22.length_ref, s32[1]{0:T(128)S(6)} %copy.24.window_ref, bf16[32,2048]{1,0:T(8,128)(2,1)S(1)} %collective-permute-done.3.refs_0_, bf16[32,2048]{1,0:T(8,128)(2,1)S(1)} %collective-permute-done.7.refs_1_, ...), custom_call_target="tpu_custom_call" | custom-call | flops 1174405120 | bytes 4194304 | tf_op jit(solution)/shard_map/pallas_call | solution.py:303
  80.5 13.1 %all_to_all.5.heads_ref = bf16[8,64,256]{2,1,0:T(8,128)(2,1)S(1)} all-to-all(bf16[8,64,256]{2,1,0:T(8,128)(2,1)S(1)} %bitcast.16), channel_id=1, replica_groups={{0,1,2,3,4,5,6,7},{8,9,10,11,12,13,14,15},{16,17,18,19,20,21,22,23},{24..., dimensions={0} | all-to-all | bytes 524288 | tf_op jit(solution)/shard_map/all_to_all | solution.py:451
  93.6 1.3 %copy-done.6 = bf16[2048,512]{1,0:T(8,128)(2,1)} copy-done((bf16[2048,512]{1,0:T(8,128)(2,1)}, bf16[2048,512]{1,0:T(8,128)(2,1)S(1)}, u32[]{:S(2)}) %copy-start.6) | copy-done | bytes 2097176
  94.9 6.5 %shard_map.126 = bf16[64,2048]{1,0:T(8,128)(2,1)} custom-call(bf16[8,64,256]{2,1,0:T(8,128)(2,1)S(1)} %all_to_all.5.heads_ref, bf16[2048,512]{1,0:T(8,128)(2,1)S(1)} %copy-done.1, bf16[2048,512]{1,0:T(8,128)(2,1)S(1)} %collective-permute-done.11.refs_1_, bf16[2048,512]{1,0:T(8,128)(2,1)} %collective-permute-done.12.refs_2_, bf16[2048,512]{1,0:T(8,128)(2,1)} %copy-done.6), custom_call_target="tpu_custom_call" | custom-call | tf_op jit(solution)/shard_map/pallas_call | solution.py:459
  (35 shorter events, 0.8 us)
Async XLA Ops:
  0.6 1.6 %copy-start = (bf16[512,2048]{1,0:T(8,128)(2,1)S(1)}, bf16[512,2048]{1,0:T(8,128)(2,1)}, u32[]{:S(2)}) copy-start(bf16[512,2048]{1,0:T(8,128)(2,1)} %param.13) | copy-start | bytes 6291460
  0.6 17.9 %copy-start.7 = (bf16[1,2048,128]{2,1,0:T(8,128)(2,1)S(1)}, bf16[1,2048,128]{2,1,0:T(8,128)(2,1)}, u32[]{:S(2)}) copy-start(bf16[1,2048,128]{2,1,0:T(8,128)(2,1)} %param.18) | copy-start | bytes 1572868
  3.5 12.4 %collective-permute-start.9 = (bf16[512,384]{1,0:T(8,128)(2,1)S(1)}, bf16[512,384]{1,0:T(8,128)(2,1)}, u32[]{:S(2)}, u32[]{:S(2)}) collective-permute-start(bf16[512,384]{1,0:T(8,128)(2,1)S(1)} %pad_maximum_fusion.1.refs_11_.refs_10_), channel_id=1, source_target_pairs={{0,16},{8,24},{16,0},{24,8},{1,17},{9,25},{17,1},{25,9},{2,18},{10... | collective-permute-start | bytes 1179656 | tf_op jit(solution)/shard_map/ppermute | solution.py:365
  6.5 8.1 %collective-permute-start = (bf16[64,2048]{1,0:T(8,128)(2,1)}, bf16[64,2048]{1,0:T(8,128)(2,1)}, u32[]{:S(2)}, u32[]{:S(2)}) collective-permute-start(bf16[64,2048]{1,0:T(8,128)(2,1)} %refs_0_.2), channel_id=1, source_target_pairs={{0,2},{2,4},{4,6},{6,7},{7,5},{5,3},{3,1},{1,0},{8,10},{10,12},{12... | collective-permute-start | bytes 786440 | tf_op jit(solution)/shard_map/ppermute | solution.py:359
  8.1 7.8 %collective-permute-start.4 = (bf16[64,2048]{1,0:T(8,128)(2,1)}, bf16[64,2048]{1,0:T(8,128)(2,1)}, u32[]{:S(2)}, u32[]{:S(2)}) collective-permute-start(bf16[64,2048]{1,0:T(8,128)(2,1)} %refs_0_.2), channel_id=1, source_target_pairs={{0,1},{2,0},{4,2},{6,4},{7,6},{5,7},{3,5},{1,3},{8,9},{10,8},{12,1... | collective-permute-start | bytes 786440 | tf_op jit(solution)/shard_map/ppermute | solution.py:362
  8.6 18.5 %collective-permute-start.8 = (bf16[512,384]{1,0:T(8,128)(2,1)S(1)}, bf16[512,384]{1,0:T(8,128)(2,1)}, u32[]{:S(2)}, u32[]{:S(2)}) collective-permute-start(bf16[512,384]{1,0:T(8,128)(2,1)S(1)} %pad_maximum_fusion.1.refs_11_.refs_10_), channel_id=1, source_target_pairs={{0,8},{8,0},{16,24},{24,16},{1,9},{9,1},{17,25},{25,17},{2,10},{10... | collective-permute-start | bytes 1179656 | tf_op jit(solution)/shard_map/ppermute | solution.py:365
  15.9 47.0 %collective-permute-start.12 = (bf16[2048,512]{1,0:T(8,128)(2,1)}, bf16[2048,512]{1,0:T(8,128)(2,1)}, u32[]{:S(2)}, u32[]{:S(2)}) collective-permute-start(bf16[2048,512]{1,0:T(8,128)(2,1)} %refs_0_.3), channel_id=1, source_target_pairs={{0,16},{8,24},{16,0},{24,8},{1,17},{9,25},{17,1},{25,9},{2,18},{10... | collective-permute-start | bytes 6291464 | tf_op jit(solution)/shard_map/ppermute | solution.py:365
  18.5 5.9 %copy-start.8 = (bf16[2048]{0:T(1024)(128)(2,1)S(1)}, bf16[2048]{0:T(1024)(128)(2,1)}, u32[]{:S(2)}) copy-start(bf16[2048]{0:T(1024)(128)(2,1)} %param.12) | copy-start | bytes 12292
  19.6 12.2 %collective-permute-start.10 = (bf16[512,384]{1,0:T(8,128)(2,1)}, bf16[512,384]{1,0:T(8,128)(2,1)}, u32[]{:S(2)}, u32[]{:S(2)}) collective-permute-start(bf16[512,384]{1,0:T(8,128)(2,1)} %collective-permute-done.9.refs_13_.refs_12_), channel_id=1, source_target_pairs={{0,8},{8,0},{16,24},{24,16},{1,9},{9,1},{17,25},{25,17},{2,10},{10... | collective-permute-start | bytes 1179656 | tf_op jit(solution)/shard_map/ppermute | solution.py:365
  19.6 12.2 %copy-start.3 = (f32[64]{0:T(128)S(1)}, f32[64]{0:T(128)}, u32[]{:S(2)}) copy-start(f32[64]{0:T(128)} %param.15) | copy-start | bytes 772
  19.6 12.2 %copy-start.4 = (f32[64]{0:T(128)S(1)}, f32[64]{0:T(128)}, u32[]{:S(2)}) copy-start(f32[64]{0:T(128)} %param.16) | copy-start | bytes 772
  20.6 9.0 %collective-permute-start.1 = (bf16[64,2048]{1,0:T(8,128)(2,1)}, bf16[64,2048]{1,0:T(8,128)(2,1)}, u32[]{:S(2)}, u32[]{:S(2)}) collective-permute-start(bf16[64,2048]{1,0:T(8,128)(2,1)} %collective-permute-done.refs_1_), channel_id=1, source_target_pairs={{0,2},{2,4},{4,6},{6,7},{7,5},{5,3},{3,1},{1,0},{8,10},{10,12},{12... | collective-permute-start | bytes 786440 | tf_op jit(solution)/shard_map/ppermute | solution.py:359
  22.2 9.0 %collective-permute-start.5 = (bf16[64,2048]{1,0:T(8,128)(2,1)}, bf16[64,2048]{1,0:T(8,128)(2,1)}, u32[]{:S(2)}, u32[]{:S(2)}) collective-permute-start(bf16[64,2048]{1,0:T(8,128)(2,1)} %collective-permute-done.4.refs_2_), channel_id=1, source_target_pairs={{0,1},{2,0},{4,2},{6,4},{7,6},{5,7},{3,5},{1,3},{8,9},{10,8},{12,1... | collective-permute-start | bytes 786440 | tf_op jit(solution)/shard_map/ppermute | solution.py:362
  27.0 66.5 %collective-permute-start.11 = (bf16[2048,512]{1,0:T(8,128)(2,1)}, bf16[2048,512]{1,0:T(8,128)(2,1)S(1)}, u32[]{:S(2)}, u32[]{:S(2)}) collective-permute-start(bf16[2048,512]{1,0:T(8,128)(2,1)} %refs_0_.3), channel_id=1, source_target_pairs={{0,8},{8,0},{16,24},{24,16},{1,9},{9,1},{17,25},{25,17},{2,10},{10... | collective-permute-start | bytes 6291464 | tf_op jit(solution)/shard_map/ppermute | solution.py:365
  29.7 15.7 %collective-permute-start.2 = (bf16[64,2048]{1,0:T(8,128)(2,1)}, bf16[64,2048]{1,0:T(8,128)(2,1)S(1)}, u32[]{:S(2)}, u32[]{:S(2)}) collective-permute-start(bf16[64,2048]{1,0:T(8,128)(2,1)} %collective-permute-done.1.refs_0_), channel_id=1, source_target_pairs={{0,2},{2,4},{4,6},{6,7},{7,5},{5,3},{3,1},{1,0},{8,10},{10,12},{12... | collective-permute-start | bytes 786440 | tf_op jit(solution)/shard_map/ppermute | solution.py:359
  31.3 14.1 %collective-permute-start.6 = (bf16[64,2048]{1,0:T(8,128)(2,1)}, bf16[64,2048]{1,0:T(8,128)(2,1)S(1)}, u32[]{:S(2)}, u32[]{:S(2)}) collective-permute-start(bf16[64,2048]{1,0:T(8,128)(2,1)} %collective-permute-done.5.refs_1_), channel_id=1, source_target_pairs={{0,1},{2,0},{4,2},{6,4},{7,6},{5,7},{3,5},{1,3},{8,9},{10,8},{12,1... | collective-permute-start | bytes 786440 | tf_op jit(solution)/shard_map/ppermute | solution.py:362
  31.7 1.0 copy-start.5
  62.9 30.7 %collective-permute-start.13 = (bf16[2048,512]{1,0:T(8,128)(2,1)}, bf16[2048,512]{1,0:T(8,128)(2,1)S(1)}, u32[]{:S(2)}, u32[]{:S(2)}) collective-permute-start(bf16[2048,512]{1,0:T(8,128)(2,1)} %collective-permute-done.12.refs_2_), channel_id=1, source_target_pairs={{0,8},{8,0},{16,24},{24,16},{1,9},{9,1},{17,25},{25,17},{2,10},{10... | collective-permute-start | bytes 6291464 | tf_op jit(solution)/shard_map/ppermute | solution.py:365
  62.9 6.0 %collective-permute-start.3 = (bf16[32,2048]{1,0:T(8,128)(2,1)S(1)}, bf16[32,2048]{1,0:T(8,128)(2,1)S(1)}, u32[]{:S(2)}, u32[]{:S(2)}) collective-permute-start(bf16[32,2048]{1,0:T(8,128)(2,1)S(1)} %slice.24), channel_id=1, source_target_pairs={{0,2},{2,4},{4,6},{6,7},{7,5},{5,3},{3,1},{1,0},{8,10},{10,12},{12... | collective-permute-start | bytes 393224 | tf_op jit(solution)/shard_map/ppermute | solution.py:359
  64.4 30.4 %copy-start.1 = (bf16[2048,512]{1,0:T(8,128)(2,1)S(1)}, bf16[2048,512]{1,0:T(8,128)(2,1)}, u32[]{:S(2)}) copy-start(bf16[2048,512]{1,0:T(8,128)(2,1)} %refs_0_.3) | copy-start | bytes 6291460
  64.5 5.9 %collective-permute-start.7 = (bf16[32,2048]{1,0:T(8,128)(2,1)S(1)}, bf16[32,2048]{1,0:T(8,128)(2,1)S(1)}, u32[]{:S(2)}, u32[]{:S(2)}) collective-permute-start(bf16[32,2048]{1,0:T(8,128)(2,1)S(1)} %slice.25), channel_id=1, source_target_pairs={{0,1},{2,0},{4,2},{6,4},{7,6},{5,7},{3,5},{1,3},{8,9},{10,8},{12,1... | collective-permute-start | bytes 393224 | tf_op jit(solution)/shard_map/ppermute | solution.py:362
  70.3 1.2 %copy-start.2 = (f32[1792,128]{1,0:T(8,128)S(1)}, f32[1792,128]{1,0:T(8,128)}, u32[]{:S(2)}) copy-start(f32[1792,128]{1,0:T(8,128)} %get-tuple-element.23.refs_16_) | copy-start | bytes 2752516
  93.6 1.3 %copy-start.6 = (bf16[2048,512]{1,0:T(8,128)(2,1)}, bf16[2048,512]{1,0:T(8,128)(2,1)S(1)}, u32[]{:S(2)}) copy-start(bf16[2048,512]{1,0:T(8,128)(2,1)S(1)} %collective-permute-done.13.refs_3_) | copy-start | bytes 6291460

commit v2 on v1

v2 whole, which is shorter than its diff:
```python
import functools

import jax
import jax.numpy as jnp
from jax import lax
from jax.experimental import pallas as pl
from jax.experimental.pallas import tpu as pltpu
from jax.sharding import PartitionSpec as P

epsilon = 1e-05
theta_base = 1000000.0
masked_score = -1e30
vmem_bytes = 48 * 1024 * 1024


def lanes_of(value):
    return lax.broadcasted_iota(jnp.int32, value.shape, value.ndim - 1)


def norm_rope(head, gain, cosine, sine):
    mean_square = jnp.mean(head * head, axis=0, keepdims=True)
    normed = head * lax.rsqrt(mean_square + epsilon) * gain
    half_dim = head.shape[0] // 2
    first, second = normed[:half_dim], normed[half_dim:]
    return jnp.concatenate(
        [first * cosine - second * sine, second * cosine + first * sine], axis=0
    )


def table_entry(table, index):
    found = jnp.int32(table[0])
    for place in range(1, len(table)):
        found = jnp.where(index == place, jnp.int32(table[place]), found)
    return found


def stage_kernel(plan, final, length_ref, window_ref, sink_ref, *refs):
    old, offsets, parts = plan["old"], plan["offsets"], plan["parts"]
    pieces, head_dim, ring = plan["pieces"], plan["head_dim"], plan["ring"]
    members = len(ring)
    refs = list(refs)

    def take(count):
        taken = refs[:count]
        del refs[:count]
        return taken

    tokens = take(sum(parts))
    norm_gain, query_gain, key_gain, freq_ref, cache_ref, values_ref = take(6)
    weights = take(pieces)
    if old:
        queries_in, keyval_in, stats_in = take(3)
    if final:
        heads_out = take(members // 2)
        fresh_out = take(1)[0]
    else:
        queries_out, keyval_out, stats_out = take(3)
    normed_ref, projected_ref = take(2)
    if final:
        queries_out, keyval_out, stats_out, joined_ref = take(4)

    fresh_blocks = len(parts)
    blocks = old + fresh_blocks
    rows = normed_ref.shape[0] // fresh_blocks
    lanes = 2 * head_dim
    query_cols = projected_ref.shape[1] - lanes
    heads = query_cols // head_dim
    count = heads * rows
    rank = lax.axis_index("tensor")
    own = lax.axis_index("dp")
    slot = rank // members if length_ref.shape[0] > 1 else 0
    length = length_ref[slot]
    window_len = window_ref[slot]
    sink_total = sink_ref[slot]
    place = table_entry([ring.index(one) for one in range(members)], rank % members)
    ids = [table_entry(ring, (place + offset + members) % members) for offset in offsets]

    gain = norm_gain[...].astype(jnp.float32)
    start = 0
    for part in tokens:
        values = part[...].astype(jnp.float32)
        mean_square = jnp.mean(values * values, axis=1, keepdims=True)
        normed_ref[pl.ds(start, part.shape[0]), :] = (
            values * lax.rsqrt(mean_square + epsilon) * gain
        ).astype(jnp.bfloat16)
        start += part.shape[0]
    depth = weights[0].shape[0]
    total = None
    for piece in range(pieces):
        from_column = pl.multiple_of((own ^ piece) * depth, depth)
        term = jnp.dot(
            normed_ref[:, pl.ds(from_column, depth)],
            weights[piece][...],
            preferred_element_type=jnp.float32,
        )
        total = term if total is None else total + term
    projected_ref[...] = total
    scale = head_dim ** (-0.5)

    if old:
        queries_out[:, pl.ds(0, old * count)] = queries_in[...]
        keyval_out[pl.ds(0, old * rows), :] = keyval_in[...]
    padding = jnp.zeros((head_dim, count), jnp.bfloat16)
    for block in range(fresh_blocks):
        position = length + ids[old + block] * rows + lax.broadcasted_iota(jnp.int32, (1, rows), 1)
        angles = position.astype(jnp.float32) * freq_ref[...]
        cosine, sine = jnp.cos(angles), jnp.sin(angles)
        here = pl.ds(block * rows, rows)
        turned = projected_ref[here, :].T
        roped = [
            norm_rope(
                turned[head * head_dim : (head + 1) * head_dim],
                query_gain[...] if head < heads else key_gain[...],
                cosine,
                sine,
            )
            for head in range(heads + 1)
        ]
        queries = jnp.concatenate(roped[:heads], axis=1).astype(jnp.bfloat16)
        queries = (queries.astype(jnp.float32) * scale).astype(jnp.bfloat16)
        queries_out[:, pl.ds((old + block) * count, count)] = jnp.concatenate(
            [queries, padding], axis=0
        )
        keys = jnp.concatenate([roped[heads], roped[heads]], axis=0).T
        last = projected_ref[here, pl.ds(query_cols, lanes)]
        keyval_out[pl.ds((old + block) * rows, rows), :] = jnp.where(
            lanes_of(last) < head_dim, keys, last
        ).astype(jnp.bfloat16)

    turned = keyval_out[...].astype(jnp.float32).T
    new_values = jnp.where(
        lax.broadcasted_iota(jnp.int32, turned.shape, 0) < head_dim, 1.0, turned
    ).astype(jnp.bfloat16)

    def token_rows(low_block, high_block):
        step = lax.broadcasted_iota(jnp.int32, (rows, 1), 0)
        return jnp.concatenate(
            [step + ids[block] * rows for block in range(low_block, high_block)], axis=0
        )

    lane_token = lax.broadcasted_iota(jnp.int32, (1, count), 1) % rows

    def pack(row_max, sums):
        return jnp.concatenate(
            [
                jnp.broadcast_to(row_max, (8, row_max.shape[1])),
                sums[:8],
                sums[head_dim:],
            ],
            axis=0,
        )

    cache_slots = cache_ref.shape[0]
    key_token = token_rows(0, blocks)

    def attend_new(block, unused):
        span = pl.ds(pl.multiple_of(block * count, count), count)
        queries = queries_out[:, span]
        first = ids[old]
        for other in range(old + 1, blocks):
            first = jnp.where(block == other, ids[other], first)
        at = first * rows + lane_token
        scores = jnp.dot(cache_ref[...], queries, preferred_element_type=jnp.float32)
        cached = lax.broadcasted_iota(jnp.int32, (cache_slots, 1), 0)
        far_away = jnp.int32(1 << 29)
        reach = jnp.where(
            cached < length, jnp.where(cached < sink_total, far_away, cached), -far_away
        )
        masked = jnp.where(reach > length - window_len + at, scores, masked_score)
        near_scores = jnp.dot(keyval_out[...], queries, preferred_element_type=jnp.float32)
        near_masked = jnp.where(key_token <= at, near_scores, masked_score)
        row_max = jnp.maximum(
            jnp.max(masked, axis=0, keepdims=True),
            jnp.max(near_masked, axis=0, keepdims=True),
        )
        unnormed = jnp.exp(masked - row_max).astype(jnp.bfloat16)
        near_unnormed = jnp.exp(near_masked - row_max).astype(jnp.bfloat16)
        sums = jnp.dot(
            values_ref[...], unnormed, preferred_element_type=jnp.float32
        ) + jnp.dot(new_values, near_unnormed, preferred_element_type=jnp.float32)
        stats_out[:, span] = pack(row_max, sums)
        return unused

    lax.fori_loop(old, blocks, attend_new, 0)

    if old:
        span = pl.ds(0, old * count)
        at = jnp.concatenate([lane_token + ids[block] * rows for block in range(old)], axis=1)
        near_scores = jnp.dot(
            keyval_out[pl.ds(old * rows, fresh_blocks * rows), :],
            queries_in[...],
            preferred_element_type=jnp.float32,
        )
        near_masked = jnp.where(token_rows(old, blocks) <= at, near_scores, masked_score)
        old_max = stats_in[0:1, :]
        row_max = jnp.maximum(jnp.max(near_masked, axis=0, keepdims=True), old_max)
        unnormed = jnp.exp(near_masked - row_max).astype(jnp.bfloat16)
        sums = jnp.dot(
            new_values[:, old * rows :], unnormed, preferred_element_type=jnp.float32
        )
        before = stats_in[...] * jnp.exp(old_max - row_max)
        stats_out[:, span] = pack(row_max, sums) + jnp.where(
            lax.broadcasted_iota(jnp.int32, before.shape, 0) < 8, 0.0, before
        )

    if final:
        for block in range(blocks):
            target = pl.ds(pl.multiple_of(ids[block] * rows, rows), rows)
            fresh_out[target, :] = keyval_out[pl.ds(block * rows, rows), :]
            sums = stats_out[:, pl.ds(block * count, count)]
            result = sums[16:] / sums[8:9]
            pair = (ids[block] // 2) ^ (rank % members // 2)
            to_row = pl.multiple_of((pair * 2 + ids[block] % 2) * rows, rows)
            joined_ref[pl.ds(to_row, rows), :] = jnp.concatenate(
                [result[:, head * rows : (head + 1) * rows] for head in range(heads)], axis=0
            ).T.astype(jnp.bfloat16)
        for pair in range(members // 2):
            heads_out[pair][...] = joined_ref[pl.ds(pair * 2 * rows, 2 * rows), :]


def output_kernel(members, pieces, *refs):
    parts = refs[: members // 2]
    weights = refs[members // 2 : members // 2 + pieces]
    kept_ref, sent_ref, total_ref = refs[members // 2 + pieces :]
    rows, depth = kept_ref.shape[0], parts[0].shape[1]
    width = weights[0].shape[1]
    member = lax.axis_index("tensor") % members
    own = lax.axis_index("dp")
    for piece in range(pieces):
        total = None
        for pair in range(members // 2):
            from_row = pl.multiple_of(((member // 2) ^ pair) * depth, depth)
            term = jnp.dot(
                parts[pair][...],
                weights[piece][pl.ds(from_row, depth), :],
                preferred_element_type=jnp.float32,
            )
            total = term if total is None else total + term
        total_ref[...] = total
        columns = pl.ds(pl.multiple_of((own ^ piece) * width, width), width)
        mine = pl.multiple_of(member % 2 * rows, rows)
        kept_ref[:, columns] = total_ref[pl.ds(mine, rows), :]
        sent_ref[:, columns] = total_ref[pl.ds(rows - mine, rows), :].astype(sent_ref.dtype)


def whole_vmem():
    return pl.BlockSpec(memory_space=pltpu.VMEM)


def in_smem():
    return pl.BlockSpec(memory_space=pltpu.SMEM)


def run_stage(plan, final, limits, tokens, shared, weights, state):
    rows = plan["rows"]
    head_dim = plan["head_dim"]
    old, fresh_blocks = plan["old"], len(plan["parts"])
    blocks = old + fresh_blocks
    lanes = 2 * head_dim
    width = weights[0].shape[1]
    query_cols = width - lanes
    count = rows * query_cols // head_dim
    features = tokens[0].shape[1]
    slots = shared[-1].shape[1]
    state_shapes = [
        ((lanes, blocks * count), jnp.bfloat16),
        ((blocks * rows, lanes), jnp.bfloat16),
        ((head_dim + 16, blocks * count), jnp.float32),
    ]
    scratch = [
        pltpu.VMEM((fresh_blocks * rows, features), jnp.bfloat16),
        pltpu.VMEM((fresh_blocks * rows, width), jnp.float32),
    ]
    if final:
        out_shape = (
            *[jax.ShapeDtypeStruct((2 * rows, query_cols), jnp.bfloat16)] * (blocks // 2),
            jax.ShapeDtypeStruct((blocks * rows, lanes), jnp.bfloat16),
        )
        scratch += [pltpu.VMEM(*one) for one in state_shapes]
        scratch += [pltpu.VMEM((blocks * rows, query_cols), jnp.bfloat16)]
    else:
        out_shape = tuple(jax.ShapeDtypeStruct(*one) for one in state_shapes)
    operands = [*tokens, *shared, *weights, *state]
    return pl.pallas_call(
        functools.partial(stage_kernel, plan, final),
        out_shape=out_shape,
        in_specs=[in_smem()] * len(limits) + [whole_vmem()] * len(operands),
        out_specs=(whole_vmem(),) * len(out_shape),
        scratch_shapes=scratch,
        compiler_params=pltpu.CompilerParams(vmem_limit_bytes=vmem_bytes),
        cost_estimate=pl.CostEstimate(
            flops=2 * fresh_blocks * rows * features * width
            + 16 * fresh_blocks * count * slots * lanes,
            bytes_accessed=4 * 1024 * 1024,
            transcendentals=fresh_blocks * count * slots,
        ),
    )(*limits, *operands)


def body(
    tokens,
    norm_gain,
    query_weight,
    keyval_weight,
    query_gain,
    key_gain,
    output_weight,
    keyval_cache,
    cached_lengths,
    sink_count,
    window,
):
    tensor_rank = lax.axis_index("tensor")
    tensor_size = lax.axis_size("tensor")
    dp_size = lax.axis_size("dp")
    head_dim = query_gain.shape[0]
    kv_heads = keyval_weight.shape[2] // head_dim
    member = tensor_rank % kv_heads
    block_cols = query_weight.shape[1] // kv_heads
    rows = tokens.shape[0]

    if tensor_size == kv_heads == 8:
        ring = [0, 2, 4, 6, 7, 5, 3, 1]
    else:
        ring = list(range(kv_heads))
    def ring_route(step):
        route = []
        for group in range(0, tensor_size, kv_heads):
            for place in range(kv_heads):
                route.append(
                    (group + ring[place], group + ring[(place + step) % kv_heads])
                )
        return route

    def forward(block):
        return lax.ppermute(block, "tensor", ring_route(1))

    def backward(block):
        return lax.ppermute(block, "tensor", ring_route(-1))

    def from_dp(block, apart):
        return lax.ppermute(block, "dp", [(one, one ^ apart) for one in range(dp_size)])

    query_local = lax.dynamic_slice_in_dim(query_weight, member * block_cols, block_cols, 1)
    keyval_local = lax.dynamic_slice_in_dim(keyval_weight, member * head_dim, head_dim, 2)
    combined = jnp.concatenate([query_local, keyval_local[0], keyval_local[1]], axis=1)
    far = dp_size // 2
    pieces = {0: combined}
    apart = far
    while apart >= 1:
        for known in list(pieces):
            pieces[known ^ apart] = from_dp(pieces[known], apart)
        apart //= 2
    weights = [pieces[k] for k in range(dp_size)]

    half_dim = head_dim // 2
    inverse_freq = theta_base ** (-2.0 * jnp.arange(half_dim, dtype=jnp.float32) / head_dim)
    cache_rows = keyval_cache[0]
    turned = cache_rows.T
    values = jnp.where(
        lax.broadcasted_iota(jnp.int32, turned.shape, 0) < head_dim,
        jnp.ones((), jnp.bfloat16),
        turned,
    )
    shared = (
        norm_gain[None],
        query_gain[:, None],
        key_gain[:, None],
        inverse_freq[:, None],
        cache_rows,
        values,
    )
    limits = (cached_lengths, window, sink_count)

    def after(value, *others):
        return lax.optimization_barrier((value, *others))[0]

    out_local = output_weight.reshape(kv_heads // 2, 2, block_cols, -1)
    out_local = lax.dynamic_index_in_dim(out_local, member % 2, 1, keepdims=False)
    out_local = out_local.reshape(kv_heads // 2 * block_cols, -1)

    ahead, behind = tokens, tokens
    offsets = []
    state, before = (), ()
    steps = (kv_heads - 1) // 2
    for step in range(1, steps + 2):
        final = step > steps
        if before:
            ahead, behind = after(ahead, *before), after(behind, *before)
        before = state
        ahead = forward(ahead)
        if final:
            arrived, arrived_offsets = [ahead], [-step]
        else:
            behind = backward(behind)
            arrived, arrived_offsets = [ahead, behind], [-step, step]
        if step == 1:
            arrived, arrived_offsets = [tokens] + arrived, [0] + arrived_offsets
            far_out = from_dp(after(out_local, pieces[far], ahead, behind), far)
        offsets += arrived_offsets
        plan = {
            "old": len(offsets) - len(arrived),
            "offsets": tuple(offsets),
            "parts": (1,) * len(arrived),
            "pieces": dp_size,
            "head_dim": head_dim,
            "ring": tuple(ring),
            "rows": rows,
        }
        state = run_stage(plan, final, limits, arrived, shared, weights, state)
        if step == 1:
            out_pieces = {0: after(out_local, *state)}
    *head_out, fresh = state
    apart = far
    while apart >= 1:
        for known in list(out_pieces):
            if known == 0 and apart == far:
                out_pieces[far] = after(far_out, *head_out)
            else:
                out_pieces[known ^ apart] = from_dp(out_pieces[known], apart)
        apart //= 2
    out_weights = [out_pieces[k] for k in range(dp_size)]

    def from_member(block, apart):
        route = [(one, one ^ apart) for one in range(tensor_size)]
        return lax.ppermute(block, "tensor", route)

    parts = [head_out[0]] + [
        from_member(head_out[pair], 2 * pair) for pair in range(1, kv_heads // 2)
    ]
    width = output_weight.shape[1]
    kept, sent = pl.pallas_call(
        functools.partial(output_kernel, kv_heads, dp_size),
        out_shape=(
            jax.ShapeDtypeStruct((rows, width * dp_size), jnp.float32),
            jax.ShapeDtypeStruct((rows, width * dp_size), jnp.bfloat16),
        ),
        in_specs=[whole_vmem()] * (len(parts) + dp_size),
        out_specs=(whole_vmem(),) * 2,
        scratch_shapes=[pltpu.VMEM((2 * rows, width), jnp.float32)],
        compiler_params=pltpu.CompilerParams(vmem_limit_bytes=vmem_bytes),
    )(*parts, *out_weights)
    attended = (kept + from_member(sent, 1).astype(jnp.float32)).astype(jnp.bfloat16)
    return (attended, fresh[None])


def solution(mesh):
    in_specs = (
        P(("dp", "tensor"), None),
        P(),
        P("dp", None),
        P(None, "dp", None),
        P(),
        P(),
        P(None, "dp"),
        P(("dp", "tensor"), None, None),
        P("dp"),
        P("dp"),
        P("dp"),
    )
    out_specs = (P(("dp", "tensor"), None), P(("dp", "tensor"), None, None))
    return jax.shard_map(body, mesh=mesh, in_specs=in_specs, out_specs=out_specs, check_vma=False)
```

time: 102 us -> 69.5 us (0.68)
  Pallas kernels: 36.9 us -> 21.7 us
  blocking collectives: 13.1 us -> 0 us
  starting transfers between devices: 13.1 us -> 18.5 us
  waiting for transfers between devices: 23.1 us -> 18.6 us
  local copies, waits for them, and re-layouts: 9.71 us -> 5.44 us
    all_to_all x1 -> x0, blocking collectives: 13.1 us -> none  [body(): lax.all_to_all(head_out.reshape(kv_heads, rows, block_cols), 'tensor', 0,...]
    ppermute x0 -> x4, waiting for transfers between devices: none -> 11.4 us  [from_member(): return lax.ppermute(block, 'tensor', route)]
    ppermute x4, waiting for transfers between devices: 11.6 us -> 1.01 us  [forward(): return lax.ppermute(block, 'tensor', ring_route(1))]
    pallas_call x4, Pallas kernels: 30.4 us -> 21 us  [run_stage(): pl.pallas_call(functools.partial(stage_kernel, plan, final), out_shape=ou...]
    pallas_call x1, Pallas kernels: 6.53 us -> 0.76 us  [body(): pl.pallas_call(functools.partial(output_kernel, kv_heads, dp_size), out_s...]
    ppermute x0 -> x4, starting transfers between devices: none -> 5.5 us  [from_member(): return lax.ppermute(block, 'tensor', route)]
    unnamed x18 -> x15, local copies, waits for them, and re-layouts: 5 us -> 1.06 us
    ppermute x4 -> x3, waiting for transfers between devices: 2.76 us -> 0.01 us  [backward(): return lax.ppermute(block, 'tensor', ring_route(-1))]
  transfers between devices with their start and end apart: 14 -> 17, of which waited for: 6 -> 6; matrix products, arithmetic and copies ran while one was open for 6% -> 6% of each run, Pallas kernels for 30% -> 30%
where the time goes in v2:
time: 69.5 us; the launch traced here: 69.2 us
  Pallas kernels  21.7 us (31%)
  waiting for transfers between devices  18.6 us (27%)
  starting transfers between devices  18.5 us (27%)
  local copies, waits for them, and re-layouts  5.44 us (8%)
  between operations  2.8 us (4%)
  other arithmetic  2.05 us (3%)
    pallas_call x4, Pallas kernels, run_stage(): pl.pallas_call(functools.partial(stage_kernel, plan, final), out_shape=ou...  21 us
    ppermute x4, waiting for transfers between devices, from_member(): return lax.ppermute(block, 'tensor', route)  11.4 us
    ppermute x4, starting transfers between devices, forward(): return lax.ppermute(block, 'tensor', ring_route(1))  6.36 us
    ppermute x6, waiting for transfers between devices, from_dp(): lax.ppermute(block, 'dp', [(one, one ^ apart) for one in range(dp_size)])  6.17 us
    ppermute x4, starting transfers between devices, from_member(): return lax.ppermute(block, 'tensor', route)  5.5 us
    ppermute x6, starting transfers between devices, from_dp(): lax.ppermute(block, 'dp', [(one, one ^ apart) for one in range(dp_size)])  5.34 us
  transfers between devices with their start and end apart: 17, of which 6 were waited for; matrix products, arithmetic and copies ran while one was open for 6% of the time, Pallas kernels for 30%

profile of v2, /device:TPU:0, one launch (start us, length us, event | category | flops | bytes accessed | tf_op | source)
XLA Modules:
  0.0 69.2 jit_solution(2342260726929442345)
XLA Ops:
  0.7 1.1 %constant_dynamic-slice_fusion.1 = bf16[512,256]{1,0:T(8,128)(2,1)S(1)} fusion(bf16[512,2048]{1,0:T(8,128)(2,1)} %param.13, s32[]{:T(128)S(6)} %select_n.30), kind=kLoop, calls=%fused_computation.8 | loop fusion | bytes 524292 | tf_op jit(solution)/shard_map/dynamic_slice | solution.py:344
  1.8 1.1 %dynamic-slice_bitcast_fusion.1 = (bf16[512,64]{1,0:T(8,128)(2,1)S(1)}, bf16[512,64]{1,0:T(8,128)(2,1)S(1)}) fusion(bf16[2,512,512]{2,1,0:T(8,128)(2,1)} %param.14, s32[]{:T(128)S(6)} %select_n.31, s32[]{:T(128)S(6)} %add.26), kind=kLoop, calls=%fused_computation.5 | loop fusion | bytes 262152 | tf_op jit(solution)/shard_map/squeeze | solution.py:346
  3.1 3.0 %collective-permute-start.4 = (bf16[512,384]{1,0:T(8,128)(2,1)S(1)}, bf16[512,384]{1,0:T(8,128)(2,1)}, u32[]{:S(2)}, u32[]{:S(2)}) collective-permute-start(bf16[512,384]{1,0:T(8,128)(2,1)S(1)} %pad_maximum_fusion.refs_9_.refs_8_.refs_7_), channel_id=1, source_target_pairs={{0,16},{8,24},{16,0},{24,8},{1,17},{9,25},{17,1},{25,9},{2,18},{10... | collective-permute-start | bytes 1179656 | tf_op jit(solution)/shard_map/ppermute | solution.py:342
  6.1 1.6 %collective-permute-start = (bf16[64,2048]{1,0:T(8,128)(2,1)}, bf16[64,2048]{1,0:T(8,128)(2,1)}, u32[]{:S(2)}, u32[]{:S(2)}) collective-permute-start(bf16[64,2048]{1,0:T(8,128)(2,1)} %refs_0_.1), channel_id=1, source_target_pairs={{0,2},{2,4},{4,6},{6,7},{7,5},{5,3},{3,1},{1,0},{8,10},{10,12},{12... | collective-permute-start | bytes 786440 | tf_op jit(solution)/shard_map/ppermute | solution.py:336
  7.7 0.4 collective-permute-start.2
  8.1 1.0 %copy.13 = bf16[1,2048,128]{1,2,0:T(8,128)(2,1)} copy(bf16[1,2048,128]{2,1,0:T(8,128)(2,1)S(1)} %copy-done.1) | data formatting | bytes 1048576 | tf_op args[7]
  9.2 6.2 %collective-permute-done.4.refs_11_.refs_10_.refs_9_ = bf16[512,384]{1,0:T(8,128)(2,1)} collective-permute-done((bf16[512,384]{1,0:T(8,128)(2,1)S(1)}, bf16[512,384]{1,0:T(8,128)(2,1)}, u32[]{:S(2)}, u32[]{:S(2)}) %collective-permute-start.4) | collective-permute-done | bytes 393248 | tf_op jit(solution)/shard_map/ppermute | solution.py:342
  15.3 1.2 %fusion.refs_8_.refs_7_.refs_6_ = bf16[128,2048]{1,0:T(8,128)(2,1)S(1)} fusion(bf16[1,2048,128]{1,2,0:T(8,128)(2,1)} %copy.13, pred[128]{0:T(512)(128)(4,1)S(1)} %iota_compare_fusion), kind=kLoop, calls=%fused_computation.1 | loop fusion | flops 262144 | bytes 1048704 | tf_op jit(solution)/shard_map/jit(_where)/select_n | solution.py:360
  18.5 0.7 %copy.14.refs_4_.refs_3_.refs_2_ = f32[64,1]{1,0:T(8,128)} copy(f32[64,1]{0,1:T(1,128)S(1)} %bitcast.26) | data formatting | bytes 512 | tf_op jit(solution)/shard_map/broadcast_in_dim | solution.py:367
  19.2 1.4 %copy.15.refs_5_.refs_4_.refs_3_ = f32[64,1]{1,0:T(8,128)} copy(f32[64,1]{0,1:T(1,128)} %bitcast.27) | data formatting | bytes 512 | tf_op jit(solution)/shard_map/broadcast_in_dim | solution.py:368
  20.7 1.8 %collective-permute-start.14 = (bf16[1024,512]{1,0:T(8,128)(2,1)S(1)}, bf16[1024,512]{1,0:T(8,128)(2,1)S(1)}, u32[]{:S(2)}, u32[]{:S(2)}) collective-permute-start(bf16[1024,512]{1,0:T(8,128)(2,1)S(1)} %bitcast.19), channel_id=1, source_target_pairs={{0,16},{8,24},{16,0},{24,8},{1,17},{9,25},{17,1},{25,9},{2,18},{10... | collective-permute-start | bytes 3145736 | tf_op jit(solution)/shard_map/ppermute | solution.py:342
  22.5 1.6 %collective-permute-start.1 = (bf16[64,2048]{1,0:T(8,128)(2,1)}, bf16[64,2048]{1,0:T(8,128)(2,1)S(1)}, u32[]{:S(2)}, u32[]{:S(2)}) collective-permute-start(bf16[64,2048]{1,0:T(8,128)(2,1)} %collective-permute-done.refs_1_), channel_id=1, source_target_pairs={{0,2},{2,4},{4,6},{6,7},{7,5},{5,3},{3,1},{1,0},{8,10},{10,12},{12... | collective-permute-start | bytes 786440 | tf_op jit(solution)/shard_map/ppermute | solution.py:336
  24.1 0.4 collective-permute-start.7
  24.6 6.1 %shard_map.122 = (bf16[128,768]{1,0:T(8,128)(2,1)S(1)}, bf16[192,128]{1,0:T(8,128)(2,1)S(1)}, f32[80,768]{1,0:T(8,128)S(1)}) custom-call(s32[1]{0:T(128)S(6)} %copy.29.length_ref, s32[1]{0:T(128)S(6)} %copy.31.window_ref, s32[1]{0:T(128)S(6)} %copy.30.sink_ref, bf16[64,2048]{1,0:T(8,128)(2,1)S(1)} %copy-done.4, ...), custom_call_target="tpu_custom_call" | custom-call | flops 3523215360 | bytes 4194304 | tf_op jit(solution)/shard_map/pallas_call | solution.py:284
  30.7 0.5 collective-permute-done.1.refs_0_
  31.2 1.6 %collective-permute-start.6 = (bf16[64,2048]{1,0:T(8,128)(2,1)S(1)}, bf16[64,2048]{1,0:T(8,128)(2,1)S(1)}, u32[]{:S(2)}, u32[]{:S(2)}) collective-permute-start(bf16[64,2048]{1,0:T(8,128)(2,1)S(1)} %collective-permute-done.1.refs_0_), channel_id=1, source_target_pairs={{0,2},{2,4},{4,6},{6,7},{7,5},{5,3},{3,1},{1,0},{8,10},{10,12},{12... | collective-permute-start | bytes 786440 | tf_op jit(solution)/shard_map/ppermute | solution.py:336
  32.8 0.5 collective-permute-start.9
  33.2 5.1 %shard_map.123 = (bf16[128,1280]{1,0:T(8,128)(2,1)S(1)}, bf16[320,128]{1,0:T(8,128)(2,1)S(1)}, f32[80,1280]{1,0:T(8,128)S(1)}) custom-call(s32[1]{0:T(128)S(6)} %copy.29.length_ref, s32[1]{0:T(128)S(6)} %copy.31.window_ref, s32[1]{0:T(128)S(6)} %copy.30.sink_ref, bf16[64,2048]{1,0:T(8,128)(2,1)S(1)} %collective-permute-done.1.refs_0_, ...), custom_call_target="tpu_custom_call" | custom-call | flops 2348810240 | bytes 4194304 | tf_op jit(solution)/shard_map/pallas_call | solution.py:284
  38.3 0.5 collective-permute-done.6.refs_0_
  38.8 1.6 %collective-permute-start.8 = (bf16[64,2048]{1,0:T(8,128)(2,1)S(1)}, bf16[64,2048]{1,0:T(8,128)(2,1)S(1)}, u32[]{:S(2)}, u32[]{:S(2)}) collective-permute-start(bf16[64,2048]{1,0:T(8,128)(2,1)S(1)} %collective-permute-done.6.refs_0_), channel_id=1, source_target_pairs={{0,2},{2,4},{4,6},{6,7},{7,5},{5,3},{3,1},{1,0},{8,10},{10,12},{12... | collective-permute-start | bytes 786440 | tf_op jit(solution)/shard_map/ppermute | solution.py:336
  40.4 5.2 %shard_map.124 = (bf16[128,1792]{1,0:T(8,128)(2,1)S(1)}, bf16[448,128]{1,0:T(8,128)(2,1)S(1)}, f32[80,1792]{1,0:T(8,128)S(1)}) custom-call(s32[1]{0:T(128)S(6)} %copy.29.length_ref, s32[1]{0:T(128)S(6)} %copy.31.window_ref, s32[1]{0:T(128)S(6)} %copy.30.sink_ref, bf16[64,2048]{1,0:T(8,128)(2,1)S(1)} %collective-permute-done.6.refs_0_, ...), custom_call_target="tpu_custom_call" | custom-call | flops 2348810240 | bytes 4194304 | tf_op jit(solution)/shard_map/pallas_call | solution.py:284
  45.6 4.6 %shard_map.125 = (bf16[128,256]{1,0:T(8,128)(2,1)S(1)}, bf16[128,256]{1,0:T(8,128)(2,1)S(1)}, bf16[128,256]{1,0:T(8,128)(2,1)S(1)}, bf16[128,256]{1,0:T(8,128)(2,1)S(1)}, bf16[512,128]{1,0:T(8,128)(2,1)}) custom-call(s32[1]{0:T(128)S(6)} %copy.29.length_ref, s32[1]{0:T(128)S(6)} %copy.31.window_ref, s32[1]{0:T(128)S(6)} %copy.30.sink_ref, ...), custom_call_target="tpu_custom_call" | custom-call | flops 1174405120 | bytes 4194304 | tf_op jit(solution)/shard_map/pallas_call | solution.py:284
  50.2 0.5 collective-permute-start.15
  50.7 1.6 %collective-permute-start.10 = (bf16[128,256]{1,0:T(8,128)(2,1)S(1)}, bf16[128,256]{1,0:T(8,128)(2,1)S(1)}, u32[]{:S(2)}, u32[]{:S(2)}) collective-permute-start(bf16[128,256]{1,0:T(8,128)(2,1)S(1)} %get-tuple-element.37), channel_id=1, source_target_pairs={{0,2},{1,3},{2,0},{3,1},{4,6},{5,7},{6,4},{7,5},{8,10},{9,11},{10,... | collective-permute-start | bytes 196616 | tf_op jit(solution)/shard_map/ppermute | solution.py:426
  52.3 2.5 %collective-permute-start.11 = (bf16[128,256]{1,0:T(8,128)(2,1)S(1)}, bf16[128,256]{1,0:T(8,128)(2,1)S(1)}, u32[]{:S(2)}, u32[]{:S(2)}) collective-permute-start(bf16[128,256]{1,0:T(8,128)(2,1)S(1)} %get-tuple-element.38), channel_id=1, source_target_pairs={{0,4},{1,5},{2,6},{3,7},{4,0},{5,1},{6,2},{7,3},{8,12},{9,13},{10,... | collective-permute-start | bytes 196616 | tf_op jit(solution)/shard_map/ppermute | solution.py:426
  54.8 0.3 collective-permute-start.12
  55.1 4.7 %collective-permute-done.11.refs_2_ = bf16[128,256]{1,0:T(8,128)(2,1)S(1)} collective-permute-done((bf16[128,256]{1,0:T(8,128)(2,1)S(1)}, bf16[128,256]{1,0:T(8,128)(2,1)S(1)}, u32[]{:S(2)}, u32[]{:S(2)}) %collective-permute-start.11) | collective-permute-done | bytes 65568 | tf_op jit(solution)/shard_map/ppermute | solution.py:426
  59.8 1.2 %collective-permute-done.12.refs_3_ = bf16[128,256]{1,0:T(8,128)(2,1)S(1)} collective-permute-done((bf16[128,256]{1,0:T(8,128)(2,1)S(1)}, bf16[128,256]{1,0:T(8,128)(2,1)S(1)}, u32[]{:S(2)}, u32[]{:S(2)}) %collective-permute-start.12) | collective-permute-done | bytes 65568 | tf_op jit(solution)/shard_map/ppermute | solution.py:426
  61.0 0.8 %shard_map.126 = (f32[64,2048]{1,0:T(8,128)S(1)}, bf16[64,2048]{1,0:T(8,128)(2,1)S(1)}) custom-call(bf16[128,256]{1,0:T(8,128)(2,1)S(1)} %get-tuple-element.36.refs_0_, bf16[128,256]{1,0:T(8,128)(2,1)S(1)} %collective-permute-done.10.refs_1_, bf16[128,256]{1,0:T(8,128)(2,1)S(1)} %collective-permute-done.11.refs_2_, ...), custom_call_target="tpu_custom_call" | custom-call | tf_op jit(solution)/shard_map/pallas_call | solution.py:432
  61.7 1.1 %collective-permute-start.16 = (bf16[64,2048]{1,0:T(8,128)(2,1)S(1)}, bf16[64,2048]{1,0:T(8,128)(2,1)S(1)}, u32[]{:S(2)}, u32[]{:S(2)}) collective-permute-start(bf16[64,2048]{1,0:T(8,128)(2,1)S(1)} %get-tuple-element.44), channel_id=1, source_target_pairs={{0,1},{1,0},{2,3},{3,2},{4,5},{5,4},{6,7},{7,6},{8,9},{9,8},{10,11... | collective-permute-start | bytes 786440 | tf_op jit(solution)/shard_map/ppermute | solution.py:426
  62.8 5.6 %collective-permute-done.16 = bf16[64,2048]{1,0:T(8,128)(2,1)S(1)} collective-permute-done((bf16[64,2048]{1,0:T(8,128)(2,1)S(1)}, bf16[64,2048]{1,0:T(8,128)(2,1)S(1)}, u32[]{:S(2)}, u32[]{:S(2)}) %collective-permute-start.16) | collective-permute-done | bytes 262176 | tf_op jit(solution)/shard_map/ppermute | solution.py:426
  68.4 0.8 %add_convert_fusion = bf16[64,2048]{1,0:T(8,128)(2,1)} fusion(f32[64,2048]{1,0:T(8,128)S(1)} %get-tuple-element.43, bf16[64,2048]{1,0:T(8,128)(2,1)S(1)} %collective-permute-done.16), kind=kLoop, calls=%fused_computation.2 | loop fusion | flops 393216 | bytes 1048576 | tf_op jit(solution)/shard_map/convert_element_type | solution.py:443
  (33 shorter events, 0.3 us)
Async XLA Ops:
  0.6 19.9 %copy-start = (bf16[2048,512]{1,0:T(8,128)(2,1)S(1)}, bf16[2048,512]{1,0:T(8,128)(2,1)}, u32[]{:S(2)}) copy-start(bf16[2048,512]{1,0:T(8,128)(2,1)} %param.17) | copy-start | bytes 6291460
  0.6 7.5 %copy-start.1 = (bf16[1,2048,128]{2,1,0:T(8,128)(2,1)S(1)}, bf16[1,2048,128]{2,1,0:T(8,128)(2,1)}, u32[]{:S(2)}) copy-start(bf16[1,2048,128]{2,1,0:T(8,128)(2,1)} %param.18) | copy-start | bytes 1572868
  0.7 17.8 %copy-start.5 = (bf16[2048]{0:T(1024)(128)(2,1)S(1)}, bf16[2048]{0:T(1024)(128)(2,1)}, u32[]{:S(2)}) copy-start(bf16[2048]{0:T(1024)(128)(2,1)} %param.12) | copy-start | bytes 12292
  0.7 17.8 %copy-start.6 = (f32[64]{0:T(128)S(1)}, f32[64]{0:T(128)}, u32[]{:S(2)}) copy-start(f32[64]{0:T(128)} %param.15) | copy-start | bytes 772
  3.1 12.3 %collective-permute-start.4 = (bf16[512,384]{1,0:T(8,128)(2,1)S(1)}, bf16[512,384]{1,0:T(8,128)(2,1)}, u32[]{:S(2)}, u32[]{:S(2)}) collective-permute-start(bf16[512,384]{1,0:T(8,128)(2,1)S(1)} %pad_maximum_fusion.refs_9_.refs_8_.refs_7_), channel_id=1, source_target_pairs={{0,16},{8,24},{16,0},{24,8},{1,17},{9,25},{17,1},{25,9},{2,18},{10... | collective-permute-start | bytes 1179656 | tf_op jit(solution)/shard_map/ppermute | solution.py:342
  6.1 14.6 %collective-permute-start = (bf16[64,2048]{1,0:T(8,128)(2,1)}, bf16[64,2048]{1,0:T(8,128)(2,1)}, u32[]{:S(2)}, u32[]{:S(2)}) collective-permute-start(bf16[64,2048]{1,0:T(8,128)(2,1)} %refs_0_.1), channel_id=1, source_target_pairs={{0,2},{2,4},{4,6},{6,7},{7,5},{5,3},{3,1},{1,0},{8,10},{10,12},{12... | collective-permute-start | bytes 786440 | tf_op jit(solution)/shard_map/ppermute | solution.py:336
  7.7 13.0 %collective-permute-start.2 = (bf16[64,2048]{1,0:T(8,128)(2,1)}, bf16[64,2048]{1,0:T(8,128)(2,1)}, u32[]{:S(2)}, u32[]{:S(2)}) collective-permute-start(bf16[64,2048]{1,0:T(8,128)(2,1)} %refs_0_.1), channel_id=1, source_target_pairs={{0,1},{2,0},{4,2},{6,4},{7,6},{5,7},{3,5},{1,3},{8,9},{10,8},{12,1... | collective-permute-start | bytes 786440 | tf_op jit(solution)/shard_map/ppermute | solution.py:339
  8.1 16.4 %collective-permute-start.3 = (bf16[512,384]{1,0:T(8,128)(2,1)S(1)}, bf16[512,384]{1,0:T(8,128)(2,1)}, u32[]{:S(2)}, u32[]{:S(2)}) collective-permute-start(bf16[512,384]{1,0:T(8,128)(2,1)S(1)} %pad_maximum_fusion.refs_9_.refs_8_.refs_7_), channel_id=1, source_target_pairs={{0,8},{8,0},{16,24},{24,16},{1,9},{9,1},{17,25},{25,17},{2,10},{10... | collective-permute-start | bytes 1179656 | tf_op jit(solution)/shard_map/ppermute | solution.py:342
  15.3 9.3 %collective-permute-start.5 = (bf16[512,384]{1,0:T(8,128)(2,1)}, bf16[512,384]{1,0:T(8,128)(2,1)}, u32[]{:S(2)}, u32[]{:S(2)}) collective-permute-start(bf16[512,384]{1,0:T(8,128)(2,1)} %collective-permute-done.4.refs_11_.refs_10_.refs_9_), channel_id=1, source_target_pairs={{0,8},{8,0},{16,24},{24,16},{1,9},{9,1},{17,25},{25,17},{2,10},{10... | collective-permute-start | bytes 1179656 | tf_op jit(solution)/shard_map/ppermute | solution.py:342
  20.5 4.0 %copy-start.2 = (f32[64,1]{1,0:T(8,128)S(1)}, f32[64,1]{1,0:T(8,128)}, u32[]{:S(2)}) copy-start(f32[64,1]{1,0:T(8,128)} %copy.14.refs_4_.refs_3_.refs_2_) | copy-start | bytes 772
  20.6 4.0 %copy-start.3 = (f32[64,1]{1,0:T(8,128)S(1)}, f32[64,1]{1,0:T(8,128)}, u32[]{:S(2)}) copy-start(f32[64,1]{1,0:T(8,128)} %copy.15.refs_5_.refs_4_.refs_3_) | copy-start | bytes 772
  20.6 4.0 %copy-start.4 = (bf16[64,2048]{1,0:T(8,128)(2,1)S(1)}, bf16[64,2048]{1,0:T(8,128)(2,1)}, u32[]{:S(2)}) copy-start(bf16[64,2048]{1,0:T(8,128)(2,1)} %refs_0_.1) | copy-start | bytes 786436
  20.7 29.6 %collective-permute-start.14 = (bf16[1024,512]{1,0:T(8,128)(2,1)S(1)}, bf16[1024,512]{1,0:T(8,128)(2,1)S(1)}, u32[]{:S(2)}, u32[]{:S(2)}) collective-permute-start(bf16[1024,512]{1,0:T(8,128)(2,1)S(1)} %bitcast.19), channel_id=1, source_target_pairs={{0,16},{8,24},{16,0},{24,8},{1,17},{9,25},{17,1},{25,9},{2,18},{10... | collective-permute-start | bytes 3145736 | tf_op jit(solution)/shard_map/ppermute | solution.py:342
  22.5 8.7 %collective-permute-start.1 = (bf16[64,2048]{1,0:T(8,128)(2,1)}, bf16[64,2048]{1,0:T(8,128)(2,1)S(1)}, u32[]{:S(2)}, u32[]{:S(2)}) collective-permute-start(bf16[64,2048]{1,0:T(8,128)(2,1)} %collective-permute-done.refs_1_), channel_id=1, source_target_pairs={{0,2},{2,4},{4,6},{6,7},{7,5},{5,3},{3,1},{1,0},{8,10},{10,12},{12... | collective-permute-start | bytes 786440 | tf_op jit(solution)/shard_map/ppermute | solution.py:336
  24.1 8.7 %collective-permute-start.7 = (bf16[64,2048]{1,0:T(8,128)(2,1)}, bf16[64,2048]{1,0:T(8,128)(2,1)S(1)}, u32[]{:S(2)}, u32[]{:S(2)}) collective-permute-start(bf16[64,2048]{1,0:T(8,128)(2,1)} %collective-permute-done.2.refs_2_), channel_id=1, source_target_pairs={{0,1},{2,0},{4,2},{6,4},{7,6},{5,7},{3,5},{1,3},{8,9},{10,8},{12,1... | collective-permute-start | bytes 786440 | tf_op jit(solution)/shard_map/ppermute | solution.py:339
  31.2 7.6 %collective-permute-start.6 = (bf16[64,2048]{1,0:T(8,128)(2,1)S(1)}, bf16[64,2048]{1,0:T(8,128)(2,1)S(1)}, u32[]{:S(2)}, u32[]{:S(2)}) collective-permute-start(bf16[64,2048]{1,0:T(8,128)(2,1)S(1)} %collective-permute-done.1.refs_0_), channel_id=1, source_target_pairs={{0,2},{2,4},{4,6},{6,7},{7,5},{5,3},{3,1},{1,0},{8,10},{10,12},{12... | collective-permute-start | bytes 786440 | tf_op jit(solution)/shard_map/ppermute | solution.py:336
  32.8 7.6 %collective-permute-start.9 = (bf16[64,2048]{1,0:T(8,128)(2,1)S(1)}, bf16[64,2048]{1,0:T(8,128)(2,1)S(1)}, u32[]{:S(2)}, u32[]{:S(2)}) collective-permute-start(bf16[64,2048]{1,0:T(8,128)(2,1)S(1)} %collective-permute-done.7.refs_1_), channel_id=1, source_target_pairs={{0,1},{2,0},{4,2},{6,4},{7,6},{5,7},{3,5},{1,3},{8,9},{10,8},{12,1... | collective-permute-start | bytes 786440 | tf_op jit(solution)/shard_map/ppermute | solution.py:339
  38.8 6.8 %collective-permute-start.8 = (bf16[64,2048]{1,0:T(8,128)(2,1)S(1)}, bf16[64,2048]{1,0:T(8,128)(2,1)S(1)}, u32[]{:S(2)}, u32[]{:S(2)}) collective-permute-start(bf16[64,2048]{1,0:T(8,128)(2,1)S(1)} %collective-permute-done.6.refs_0_), channel_id=1, source_target_pairs={{0,2},{2,4},{4,6},{6,7},{7,5},{5,3},{3,1},{1,0},{8,10},{10,12},{12... | collective-permute-start | bytes 786440 | tf_op jit(solution)/shard_map/ppermute | solution.py:336
  40.4 20.6 %collective-permute-start.13 = (bf16[1024,512]{1,0:T(8,128)(2,1)S(1)}, bf16[1024,512]{1,0:T(8,128)(2,1)S(1)}, u32[]{:S(2)}, u32[]{:S(2)}) collective-permute-start(bf16[1024,512]{1,0:T(8,128)(2,1)S(1)} %bitcast.20), channel_id=1, source_target_pairs={{0,8},{8,0},{16,24},{24,16},{1,9},{9,1},{17,25},{25,17},{2,10},{10... | collective-permute-start | bytes 3145736 | tf_op jit(solution)/shard_map/ppermute | solution.py:342
  50.2 10.7 %collective-permute-start.15 = (bf16[1024,512]{1,0:T(8,128)(2,1)S(1)}, bf16[1024,512]{1,0:T(8,128)(2,1)S(1)}, u32[]{:S(2)}, u32[]{:S(2)}) collective-permute-start(bf16[1024,512]{1,0:T(8,128)(2,1)S(1)} %collective-permute-done.14.refs_6_), channel_id=1, source_target_pairs={{0,8},{8,0},{16,24},{24,16},{1,9},{9,1},{17,25},{25,17},{2,10},{10... | collective-permute-start | bytes 3145736 | tf_op jit(solution)/shard_map/ppermute | solution.py:342
  50.7 4.4 %collective-permute-start.10 = (bf16[128,256]{1,0:T(8,128)(2,1)S(1)}, bf16[128,256]{1,0:T(8,128)(2,1)S(1)}, u32[]{:S(2)}, u32[]{:S(2)}) collective-permute-start(bf16[128,256]{1,0:T(8,128)(2,1)S(1)} %get-tuple-element.37), channel_id=1, source_target_pairs={{0,2},{1,3},{2,0},{3,1},{4,6},{5,7},{6,4},{7,5},{8,10},{9,11},{10,... | collective-permute-start | bytes 196616 | tf_op jit(solution)/shard_map/ppermute | solution.py:426
  52.3 7.5 %collective-permute-start.11 = (bf16[128,256]{1,0:T(8,128)(2,1)S(1)}, bf16[128,256]{1,0:T(8,128)(2,1)S(1)}, u32[]{:S(2)}, u32[]{:S(2)}) collective-permute-start(bf16[128,256]{1,0:T(8,128)(2,1)S(1)} %get-tuple-element.38), channel_id=1, source_target_pairs={{0,4},{1,5},{2,6},{3,7},{4,0},{5,1},{6,2},{7,3},{8,12},{9,13},{10,... | collective-permute-start | bytes 196616 | tf_op jit(solution)/shard_map/ppermute | solution.py:426
  54.8 6.2 %collective-permute-start.12 = (bf16[128,256]{1,0:T(8,128)(2,1)S(1)}, bf16[128,256]{1,0:T(8,128)(2,1)S(1)}, u32[]{:S(2)}, u32[]{:S(2)}) collective-permute-start(bf16[128,256]{1,0:T(8,128)(2,1)S(1)} %get-tuple-element.39), channel_id=1, source_target_pairs={{0,6},{1,7},{2,4},{3,5},{4,2},{5,3},{6,0},{7,1},{8,14},{9,15},{10,... | collective-permute-start | bytes 196616 | tf_op jit(solution)/shard_map/ppermute | solution.py:426
  61.7 6.7 %collective-permute-start.16 = (bf16[64,2048]{1,0:T(8,128)(2,1)S(1)}, bf16[64,2048]{1,0:T(8,128)(2,1)S(1)}, u32[]{:S(2)}, u32[]{:S(2)}) collective-permute-start(bf16[64,2048]{1,0:T(8,128)(2,1)S(1)} %get-tuple-element.44), channel_id=1, source_target_pairs={{0,1},{1,0},{2,3},{3,2},{4,5},{5,4},{6,7},{7,6},{8,9},{9,8},{10,11... | collective-permute-start | bytes 786440 | tf_op jit(solution)/shard_map/ppermute | solution.py:426

commit v3 on v2

--- a/solution.py
+++ b/solution.py
@@ -2,6 +2,7 @@
 
 import jax
 import jax.numpy as jnp
+import numpy as np
 from jax import lax
 from jax.experimental import pallas as pl
 from jax.experimental.pallas import tpu as pltpu
@@ -10,7 +11,9 @@
 epsilon = 1e-05
 theta_base = 1000000.0
 masked_score = -1e30
-vmem_bytes = 48 * 1024 * 1024
+column_chunks = 4
+vmem_bytes = 32 * 1024 * 1024
+most_vmem_bytes = 62 * 1024 * 1024
 
 
 def lanes_of(value):
@@ -34,7 +37,7 @@
     return found
 
 
-def stage_kernel(plan, final, length_ref, window_ref, sink_ref, *refs):
+def stage_kernel(plan, final, *refs):
     old, offsets, parts = plan["old"], plan["offsets"], plan["parts"]
     pieces, head_dim, ring = plan["pieces"], plan["head_dim"], plan["ring"]
     members = len(ring)
@@ -45,8 +48,9 @@
         del refs[:count]
         return taken
 
+    limits_ref = take(1)[0]
     tokens = take(sum(parts))
-    norm_gain, query_gain, key_gain, freq_ref, cache_ref, values_ref = take(6)
+    norm_gain, head_ref, cache_ref, values_ref = take(4)
     weights = take(pieces)
     if old:
         queries_in, keyval_in, stats_in = take(3)
@@ -68,14 +72,13 @@
     count = heads * rows
     rank = lax.axis_index("tensor")
     own = lax.axis_index("dp")
-    slot = rank // members if length_ref.shape[0] > 1 else 0
-    length = length_ref[slot]
-    window_len = window_ref[slot]
-    sink_total = sink_ref[slot]
+    length = limits_ref[0:1, 0:1]
+    window_len = limits_ref[1:2, 0:1]
+    sink_total = limits_ref[2:3, 0:1]
     place = table_entry([ring.index(one) for one in range(members)], rank % members)
     ids = [table_entry(ring, (place + offset + members) % members) for offset in offsets]
 
-    gain = norm_gain[...].astype(jnp.float32)
+    gain = norm_gain[...]
     start = 0
     for part in tokens:
         values = part[...].astype(jnp.float32)
@@ -101,16 +104,18 @@
         queries_out[:, pl.ds(0, old * count)] = queries_in[...]
         keyval_out[pl.ds(0, old * rows), :] = keyval_in[...]
     padding = jnp.zeros((head_dim, count), jnp.bfloat16)
+    query_gains = head_ref[:head_dim, :]
+    key_gains = head_ref[head_dim : 2 * head_dim, :]
     for block in range(fresh_blocks):
         position = length + ids[old + block] * rows + lax.broadcasted_iota(jnp.int32, (1, rows), 1)
-        angles = position.astype(jnp.float32) * freq_ref[...]
+        angles = position.astype(jnp.float32) * head_ref[2 * head_dim :, :]
         cosine, sine = jnp.cos(angles), jnp.sin(angles)
         here = pl.ds(block * rows, rows)
         turned = projected_ref[here, :].T
         roped = [
             norm_rope(
                 turned[head * head_dim : (head + 1) * head_dim],
-                query_gain[...] if head < heads else key_gain[...],
+                query_gains if head < heads else key_gains,
                 cosine,
                 sine,
             )
@@ -153,13 +158,12 @@
     cache_slots = cache_ref.shape[0]
     key_token = token_rows(0, blocks)
 
-    def attend_new(block, unused):
-        span = pl.ds(pl.multiple_of(block * count, count), count)
+    def attend_new():
+        span = pl.ds(old * count, fresh_blocks * count)
         queries = queries_out[:, span]
-        first = ids[old]
-        for other in range(old + 1, blocks):
-            first = jnp.where(block == other, ids[other], first)
-        at = first * rows + lane_token
+        at = jnp.concatenate(
+            [ids[block] * rows + lane_token for block in range(old, blocks)], axis=1
+        )
         scores = jnp.dot(cache_ref[...], queries, preferred_element_type=jnp.float32)
         cached = lax.broadcasted_iota(jnp.int32, (cache_slots, 1), 0)
         far_away = jnp.int32(1 << 29)
@@ -179,9 +183,8 @@
             values_ref[...], unnormed, preferred_element_type=jnp.float32
         ) + jnp.dot(new_values, near_unnormed, preferred_element_type=jnp.float32)
         stats_out[:, span] = pack(row_max, sums)
-        return unused
-
-    lax.fori_loop(old, blocks, attend_new, 0)
+
+    attend_new()
 
     if old:
         span = pl.ds(0, old * count)
@@ -208,7 +211,7 @@
             target = pl.ds(pl.multiple_of(ids[block] * rows, rows), rows)
             fresh_out[target, :] = keyval_out[pl.ds(block * rows, rows), :]
             sums = stats_out[:, pl.ds(block * count, count)]
-            result = sums[16:] / sums[8:9]
+            result = sums[16:] * (1.0 / sums[8:9])
             pair = (ids[block] // 2) ^ (rank % members // 2)
             to_row = pl.multiple_of((pair * 2 + ids[block] % 2) * rows, rows)
             joined_ref[pl.ds(to_row, rows), :] = jnp.concatenate(
@@ -218,37 +221,116 @@
             heads_out[pair][...] = joined_ref[pl.ds(pair * 2 * rows, 2 * rows), :]
 
 
-def output_kernel(members, pieces, *refs):
+def output_kernel(members, held, *refs):
     parts = refs[: members // 2]
-    weights = refs[members // 2 : members // 2 + pieces]
-    kept_ref, sent_ref, total_ref = refs[members // 2 + pieces :]
+    weights = refs[members // 2 : members // 2 + len(held)]
+    kept_ref, sent_ref, total_ref = refs[members // 2 + len(held) :]
     rows, depth = kept_ref.shape[0], parts[0].shape[1]
     width = weights[0].shape[1]
     member = lax.axis_index("tensor") % members
     own = lax.axis_index("dp")
-    for piece in range(pieces):
+    for place, piece in enumerate(held):
         total = None
         for pair in range(members // 2):
             from_row = pl.multiple_of(((member // 2) ^ pair) * depth, depth)
             term = jnp.dot(
                 parts[pair][...],
-                weights[piece][pl.ds(from_row, depth), :],
+                weights[place][pl.ds(from_row, depth), :],
                 preferred_element_type=jnp.float32,
             )
             total = term if total is None else total + term
         total_ref[...] = total
-        columns = pl.ds(pl.multiple_of((own ^ piece) * width, width), width)
+        columns = pl.ds(pl.multiple_of((own ^ piece) % len(held) * width, width), width)
         mine = pl.multiple_of(member % 2 * rows, rows)
         kept_ref[:, columns] = total_ref[pl.ds(mine, rows), :]
         sent_ref[:, columns] = total_ref[pl.ds(rows - mine, rows), :].astype(sent_ref.dtype)
 
 
+def columns_kernel(members, query_ref, keyval_ref, combined_ref, sides_ref, sems):
+    member = lax.axis_index("tensor") % members
+    query_cols = query_ref.shape[1] // members
+    lanes = combined_ref.shape[1] - query_cols
+    from_column = pl.multiple_of(member * query_cols, query_cols)
+    pair_column = pl.multiple_of(member // 2 * lanes, lanes)
+    depth = query_ref.shape[0]
+    chunk = depth // column_chunks
+    query_copies, side_copies = [], []
+    for part in range(column_chunks):
+        some = pl.ds(part * chunk, chunk)
+        for side in range(2):
+            side_copies.append(
+                pltpu.make_async_copy(
+                    keyval_ref.at[side, some, pl.ds(pair_column, lanes)],
+                    sides_ref.at[side, some],
+                    sems.at[side, part],
+                )
+            )
+        query_copies.append(
+            pltpu.make_async_copy(
+                query_ref.at[some, pl.ds(from_column, query_cols)],
+                combined_ref.at[some, pl.ds(0, query_cols)],
+                sems.at[2, part],
+            )
+        )
+    copies = side_copies + query_copies
+    for copy in copies:
+        copy.start()
+    for copy in side_copies:
+        copy.wait()
+    keys, values = sides_ref[0], sides_ref[1]
+    head_dim = lanes // 2
+    even = member % 2 == 0
+    low = lanes_of(keys) < head_dim
+
+    def turned(side):
+        return pltpu.roll(side.astype(jnp.float32), head_dim, 1).astype(jnp.bfloat16)
+
+    @pl.when(even)
+    def _():
+        combined_ref[:, query_cols:] = jnp.where(low, keys, turned(values))
+
+    @pl.when(jnp.logical_not(even))
+    def _():
+        combined_ref[:, query_cols:] = jnp.where(low, turned(keys), values)
+
+    for copy in query_copies:
+        copy.wait()
+
+
+def join_kernel(near_kept, near_came, far_kept, far_came, attended_ref):
+    width = near_kept.shape[1]
+    side = lax.axis_index("dp") // (lax.axis_size("dp") // 2)
+    for place, (kept, came) in enumerate(((near_kept, near_came), (far_kept, far_came))):
+        start = pl.multiple_of((side ^ place) * width, width)
+        attended_ref[:, pl.ds(start, width)] = (
+            kept[...] + came[...].astype(jnp.float32)
+        ).astype(attended_ref.dtype)
+
+
+def turn_kernel(members, length_ref, window_ref, sink_ref, *refs):
+    cache_ref, norm_gain, query_gain, key_gain, freq_ref = refs[:5]
+    values_ref, gain_ref, head_ref, limits_ref = refs[7:]
+    turned = cache_ref[0].astype(jnp.float32).T
+    row = lax.broadcasted_iota(jnp.int32, turned.shape, 0)
+    head_dim = turned.shape[0] // 2
+    values_ref[...] = jnp.where(row < head_dim, 1.0, turned).astype(jnp.bfloat16)
+    gain = norm_gain[...].astype(jnp.float32)
+    gain_ref[...] = jnp.concatenate([gain[one : one + 1] for one in range(gain.shape[0])], axis=1)
+    rows = head_ref.shape[1]
+    for place, one in enumerate((query_gain, key_gain)):
+        head_ref[pl.ds(place * head_dim, head_dim), :] = jnp.broadcast_to(
+            one[...], (rows, head_dim)
+        ).T
+    head_ref[pl.ds(2 * head_dim, head_dim // 2), :] = freq_ref[...]
+    slot = lax.axis_index("tensor") // members if length_ref.shape[0] > 1 else 0
+    line = lax.broadcasted_iota(jnp.int32, limits_ref.shape, 0)
+    limits_ref[...] = jnp.where(
+        line == 0, length_ref[slot], jnp.where(line == 1, window_ref[slot], sink_ref[slot])
+    )
+
+
 def whole_vmem():
     return pl.BlockSpec(memory_space=pltpu.VMEM)
-
-
-def in_smem():
-    return pl.BlockSpec(memory_space=pltpu.SMEM)
 
 
 def run_stage(plan, final, limits, tokens, shared, weights, state):
@@ -280,21 +362,16 @@
         scratch += [pltpu.VMEM((blocks * rows, query_cols), jnp.bfloat16)]
     else:
         out_shape = tuple(jax.ShapeDtypeStruct(*one) for one in state_shapes)
-    operands = [*tokens, *shared, *weights, *state]
+    operands = [limits, *tokens, *shared, *weights, *state]
     return pl.pallas_call(
         functools.partial(stage_kernel, plan, final),
         out_shape=out_shape,
-        in_specs=[in_smem()] * len(limits) + [whole_vmem()] * len(operands),
+        in_specs=[whole_vmem()] * len(operands),
         out_specs=(whole_vmem(),) * len(out_shape),
         scratch_shapes=scratch,
         compiler_params=pltpu.CompilerParams(vmem_limit_bytes=vmem_bytes),
-        cost_estimate=pl.CostEstimate(
-            flops=2 * fresh_blocks * rows * features * width
-            + 16 * fresh_blocks * count * slots * lanes,
-            bytes_accessed=4 * 1024 * 1024,
-            transcendentals=fresh_blocks * count * slots,
-        ),
-    )(*limits, *operands)
+        cost_estimate=pl.CostEstimate(flops=1024, bytes_accessed=1024, transcendentals=0),
+    )(*operands)
 
 
 def body(
@@ -341,86 +418,108 @@
     def from_dp(block, apart):
         return lax.ppermute(block, "dp", [(one, one ^ apart) for one in range(dp_size)])
 
-    query_local = lax.dynamic_slice_in_dim(query_weight, member * block_cols, block_cols, 1)
-    keyval_local = lax.dynamic_slice_in_dim(keyval_weight, member * head_dim, head_dim, 2)
-    combined = jnp.concatenate([query_local, keyval_local[0], keyval_local[1]], axis=1)
+    depth = query_weight.shape[0]
+    combined = pl.pallas_call(
+        functools.partial(columns_kernel, kv_heads),
+        out_shape=jax.ShapeDtypeStruct((depth, block_cols + 2 * head_dim), jnp.bfloat16),
+        in_specs=[pl.BlockSpec(memory_space=pltpu.HBM)] * 2,
+        out_specs=whole_vmem(),
+        scratch_shapes=[
+            pltpu.VMEM((2, depth, 2 * head_dim), jnp.bfloat16),
+            pltpu.SemaphoreType.DMA((3, column_chunks)),
+        ],
+        cost_estimate=pl.CostEstimate(flops=0, bytes_accessed=1 << 25, transcendentals=0),
+        compiler_params=pltpu.CompilerParams(vmem_limit_bytes=most_vmem_bytes),
+    )(query_weight, keyval_weight)
     far = dp_size // 2
-    pieces = {0: combined}
-    apart = far
+
+    def after(value, *others):
+        return lax.optimization_barrier((value, *others))[0]
+
+    pieces = {0: combined, far: from_dp(combined, far)}
+    steps = (kv_heads - 1) // 2
+    early = min(2, steps)
+    chain, chain_offsets = [tokens], [0]
+    ahead, behind = tokens, tokens
+    for step in range(1, early + 1):
+        ahead, behind = forward(ahead), backward(behind)
+        chain += [ahead, behind]
+        chain_offsets += [-step, step]
+    exponents = -2.0 * np.arange(head_dim // 2, dtype=np.float32) / np.float32(head_dim)
+    inverse_freq = np.power(np.float32(theta_base), exponents, dtype=np.float32)
+    inverse_freq = np.tile(inverse_freq[:, None], (1, rows))
+    cache_rows = keyval_cache[0]
+    features = norm_gain.shape[0]
+    values, gain_row, head_table, limits = pl.pallas_call(
+        functools.partial(turn_kernel, kv_heads),
+        out_shape=(
+            jax.ShapeDtypeStruct(cache_rows.shape[::-1], jnp.bfloat16),
+            jax.ShapeDtypeStruct((1, features), jnp.float32),
+            jax.ShapeDtypeStruct((2 * head_dim + head_dim // 2, rows), jnp.float32),
+            jax.ShapeDtypeStruct((8, 128), jnp.int32),
+        ),
+        in_specs=[pl.BlockSpec(memory_space=pltpu.SMEM)] * 3
+        + [whole_vmem()] * 5
+        + [pl.BlockSpec(memory_space=pl.ANY)] * 2,
+        out_specs=(whole_vmem(),) * 4,
+        compiler_params=pltpu.CompilerParams(vmem_limit_bytes=vmem_bytes),
+    )(
+        cached_lengths,
+        window,
+        sink_count,
+        keyval_cache,
+        norm_gain.reshape(-1, 128),
+        query_gain[None],
+        key_gain[None],
+        jnp.asarray(inverse_freq),
+        *chain[1:3],
+    )
+    out_local = after(output_weight, *chain[1:3]).reshape(kv_heads // 2, 2, block_cols, -1)
+    out_local = lax.dynamic_index_in_dim(out_local, member % 2, 1, keepdims=False)
+    out_local = out_local.reshape(kv_heads // 2 * block_cols, -1)
+    far_out = from_dp(after(out_local, pieces[far], values, *chain[1:]), far)
+    pieces[far], values, *unused = lax.optimization_barrier((pieces[far], values, *chain[1:]))
+    apart = far // 2
     while apart >= 1:
         for known in list(pieces):
             pieces[known ^ apart] = from_dp(pieces[known], apart)
         apart //= 2
     weights = [pieces[k] for k in range(dp_size)]
-
-    half_dim = head_dim // 2
-    inverse_freq = theta_base ** (-2.0 * jnp.arange(half_dim, dtype=jnp.float32) / head_dim)
-    cache_rows = keyval_cache[0]
-    turned = cache_rows.T
-    values = jnp.where(
-        lax.broadcasted_iota(jnp.int32, turned.shape, 0) < head_dim,
-        jnp.ones((), jnp.bfloat16),
-        turned,
-    )
     shared = (
-        norm_gain[None],
-        query_gain[:, None],
-        key_gain[:, None],
-        inverse_freq[:, None],
+        gain_row,
+        head_table,
         cache_rows,
         values,
     )
-    limits = (cached_lengths, window, sink_count)
-
-    def after(value, *others):
-        return lax.optimization_barrier((value, *others))[0]
-
-    out_local = output_weight.reshape(kv_heads // 2, 2, block_cols, -1)
-    out_local = lax.dynamic_index_in_dim(out_local, member % 2, 1, keepdims=False)
-    out_local = out_local.reshape(kv_heads // 2 * block_cols, -1)
-
-    ahead, behind = tokens, tokens
+
     offsets = []
-    state, before = (), ()
-    steps = (kv_heads - 1) // 2
-    for step in range(1, steps + 2):
-        final = step > steps
-        if before:
-            ahead, behind = after(ahead, *before), after(behind, *before)
-        before = state
-        ahead = forward(ahead)
-        if final:
-            arrived, arrived_offsets = [ahead], [-step]
-        else:
-            behind = backward(behind)
-            arrived, arrived_offsets = [ahead, behind], [-step, step]
-        if step == 1:
-            arrived, arrived_offsets = [tokens] + arrived, [0] + arrived_offsets
-            far_out = from_dp(after(out_local, pieces[far], ahead, behind), far)
+    state = ()
+    arrived, arrived_offsets = chain, chain_offsets
+    for step in range(early + 1, steps + 3):
+        final = step > steps + 1
         offsets += arrived_offsets
         plan = {
-            "old": len(offsets) - len(arrived),
+            "old": len(offsets) - len(arrived_offsets),
             "offsets": tuple(offsets),
-            "parts": (1,) * len(arrived),
+            "parts": (2,) if final else (1,) * len(arrived),
             "pieces": dp_size,
             "head_dim": head_dim,
             "ring": tuple(ring),
             "rows": rows,
         }
+        before = state
+        if not final:
+            if before:
+                ahead, behind = after(ahead, *before), after(behind, *before)
+            if step > steps:
+                ahead, behind = ahead[: rows // 2], behind[rows // 2 :]
+            ahead, behind = forward(ahead), backward(behind)
         state = run_stage(plan, final, limits, arrived, shared, weights, state)
-        if step == 1:
+        arrived = [ahead, behind]
+        arrived_offsets = [-step, step] if step <= steps else [step]
+        if not before:
             out_pieces = {0: after(out_local, *state)}
     *head_out, fresh = state
-    apart = far
-    while apart >= 1:
-        for known in list(out_pieces):
-            if known == 0 and apart == far:
-                out_pieces[far] = after(far_out, *head_out)
-            else:
-                out_pieces[known ^ apart] = from_dp(out_pieces[known], apart)
-        apart //= 2
-    out_weights = [out_pieces[k] for k in range(dp_size)]
-
     def from_member(block, apart):
         route = [(one, one ^ apart) for one in range(tensor_size)]
         return lax.ppermute(block, "tensor", route)
@@ -429,18 +528,41 @@
         from_member(head_out[pair], 2 * pair) for pair in range(1, kv_heads // 2)
     ]
     width = output_weight.shape[1]
-    kept, sent = pl.pallas_call(
-        functools.partial(output_kernel, kv_heads, dp_size),
-        out_shape=(
-            jax.ShapeDtypeStruct((rows, width * dp_size), jnp.float32),
-            jax.ShapeDtypeStruct((rows, width * dp_size), jnp.bfloat16),
-        ),
-        in_specs=[whole_vmem()] * (len(parts) + dp_size),
-        out_specs=(whole_vmem(),) * 2,
-        scratch_shapes=[pltpu.VMEM((2 * rows, width), jnp.float32)],
+
+    def project(held):
+        return pl.pallas_call(
+            functools.partial(output_kernel, kv_heads, held),
+            out_shape=(
+                jax.ShapeDtypeStruct((rows, width * len(held)), jnp.float32),
+                jax.ShapeDtypeStruct((rows, width * len(held)), jnp.bfloat16),
+            ),
+            in_specs=[whole_vmem()] * (len(parts) + len(held)),
+            out_specs=(whole_vmem(),) * 2,
+            scratch_shapes=[pltpu.VMEM((2 * rows, width), jnp.float32)],
+            compiler_params=pltpu.CompilerParams(vmem_limit_bytes=vmem_bytes),
+        )(*parts, *[out_pieces[piece] for piece in held])
+
+    def spread(known_pieces, apart):
+        while apart >= 1:
+            for known in known_pieces:
+                out_pieces[known ^ apart] = from_dp(out_pieces[known], apart)
+            known_pieces = known_pieces + [known ^ apart for known in known_pieces]
+            apart //= 2
+
+    spread([0], far // 2)
+    near_kept, near_sent = project(tuple(range(far)))
+    near_came = from_member(near_sent, 1)
+    out_pieces[far] = after(far_out, *parts[1:])
+    spread([far], far // 2)
+    far_kept, far_sent = project(tuple(range(far, dp_size)))
+    far_came = from_member(far_sent, 1)
+    attended = pl.pallas_call(
+        join_kernel,
+        out_shape=jax.ShapeDtypeStruct((rows, width * dp_size), jnp.bfloat16),
+        in_specs=[whole_vmem()] * 4,
+        out_specs=whole_vmem(),
         compiler_params=pltpu.CompilerParams(vmem_limit_bytes=vmem_bytes),
-    )(*parts, *out_weights)
-    attended = (kept + from_member(sent, 1).astype(jnp.float32)).astype(jnp.bfloat16)
+    )(near_kept, near_came, far_kept, far_came)
     return (attended, fresh[None])
 
 

time: 69.5 us -> 58.7 us (0.84)
  Pallas kernels: 21.7 us -> 16.6 us
  local copies, waits for them, and re-layouts: 5.44 us -> 1.36 us
  other arithmetic: 2.05 us -> 0 us
    pallas_call x4 -> x3, Pallas kernels: 21 us -> 12.7 us  [run_stage(): pl.pallas_call(functools.partial(stage_kernel, plan, final), out_shape=ou...]
    ppermute x6, waiting for transfers between devices: 6.17 us -> 2.58 us  [from_dp(): lax.ppermute(block, 'dp', [(one, one ^ apart) for one in range(dp_size)])]
    pallas_call x1 -> x5, Pallas kernels: 0.76 us -> 3.9 us  [the longest x1 1.94 us: body(): pl.pallas_call(functools.partial(columns_kernel, kv_heads), out_shape=jax...]
    ppermute x4, waiting for transfers between devices: 1.01 us -> 3.56 us  [forward(): return lax.ppermute(block, 'tensor', ring_route(1))]
    ppermute x3 -> x4, waiting for transfers between devices: 0.01 us -> 2.44 us  [backward(): return lax.ppermute(block, 'tensor', ring_route(-1))]
    broadcast_in_dim x3 -> x0, local copies, waits for them, and re-layouts: 2.07 us -> none  [the longest x1 1.36 us: body(): key_gain[:, None]]
    ppermute x4, starting transfers between devices: 6.36 us -> 8.1 us  [forward(): return lax.ppermute(block, 'tensor', ring_route(1))]
    ppermute x6, starting transfers between devices: 5.34 us -> 4.07 us  [from_dp(): lax.ppermute(block, 'dp', [(one, one ^ apart) for one in range(dp_size)])]
  transfers between devices with their start and end apart: 17 -> 19, of which waited for: 6 -> 11; matrix products, arithmetic and copies ran while one was open for 6% -> 2% of each run, Pallas kernels for 30% -> 27%
where the time goes in v3:
time: 58.7 us; the launch traced here: 58.5 us
  waiting for transfers between devices  19 us (32%)
  starting transfers between devices  18.7 us (32%)
  Pallas kernels  16.6 us (28%)
  between operations  2.76 us (5%)
  local copies, waits for them, and re-layouts  1.36 us (2%)
    pallas_call x3, Pallas kernels, run_stage(): pl.pallas_call(functools.partial(stage_kernel, plan, final), out_shape=ou...  12.7 us
    ppermute x5, waiting for transfers between devices, from_member(): return lax.ppermute(block, 'tensor', route)  10.5 us
    ppermute x4, starting transfers between devices, forward(): return lax.ppermute(block, 'tensor', ring_route(1))  8.1 us
    ppermute x5, starting transfers between devices, from_member(): return lax.ppermute(block, 'tensor', route)  5.21 us
    ppermute x6, starting transfers between devices, from_dp(): lax.ppermute(block, 'dp', [(one, one ^ apart) for one in range(dp_size)])  4.07 us
    ppermute x4, waiting for transfers between devices, forward(): return lax.ppermute(block, 'tensor', ring_route(1))  3.56 us
    ppermute x6, waiting for transfers between devices, from_dp(): lax.ppermute(block, 'dp', [(one, one ^ apart) for one in range(dp_size)])  2.58 us
    ppermute x4, waiting for transfers between devices, backward(): return lax.ppermute(block, 'tensor', ring_route(-1))  2.44 us
  transfers between devices with their start and end apart: 19, of which 11 were waited for; matrix products, arithmetic and copies ran while one was open for 2% of the time, Pallas kernels for 27%

profile of v3, /device:TPU:0, one launch (start us, length us, event | category | flops | bytes accessed | tf_op | source)
XLA Modules:
  0.0 58.5 jit_solution(16312729920664152809)
XLA Ops:
  0.7 3.1 %collective-permute-start = (bf16[64,2048]{1,0:T(8,128)(2,1)}, bf16[64,2048]{1,0:T(8,128)(2,1)S(1)}, u32[]{:S(2)}, u32[]{:S(2)}) collective-permute-start(bf16[64,2048]{1,0:T(8,128)(2,1)} %refs_1_.1), channel_id=1, source_target_pairs={{0,2},{2,4},{4,6},{6,7},{7,5},{5,3},{3,1},{1,0},{8,10},{10,12},{12... | collective-permute-start | bytes 786440 | tf_op jit(solution)/shard_map/ppermute | solution.py:413
  3.8 1.9 %shard_map.132.refs_10_.refs_7_ = bf16[512,384]{1,0:T(8,128)(2,1)} custom-call(bf16[512,2048]{1,0:T(8,128)(2,1)} %query_ref.1, bf16[2,512,512]{2,1,0:T(8,128)(2,1)} %keyval_ref.1), custom_call_target="tpu_custom_call" | custom-call | bytes 33554432 | tf_op jit(solution)/shard_map/pallas_call | solution.py:422
  5.7 2.0 %collective-permute-start.5 = (bf16[512,384]{1,0:T(8,128)(2,1)}, bf16[512,384]{1,0:T(8,128)(2,1)S(1)}, u32[]{:S(2)}, u32[]{:S(2)}) collective-permute-start(bf16[512,384]{1,0:T(8,128)(2,1)} %shard_map.132.refs_10_.refs_7_), channel_id=1, source_target_pairs={{0,16},{8,24},{16,0},{24,8},{1,17},{9,25},{17,1},{25,9},{2,18},{10... | collective-permute-start | bytes 1179656 | tf_op jit(solution)/shard_map/ppermute | solution.py:419
  7.8 2.4 %collective-permute-done.refs_5_.refs_2_ = bf16[64,2048]{1,0:T(8,128)(2,1)S(1)} collective-permute-done((bf16[64,2048]{1,0:T(8,128)(2,1)}, bf16[64,2048]{1,0:T(8,128)(2,1)S(1)}, u32[]{:S(2)}, u32[]{:S(2)}) %collective-permute-start) | collective-permute-done | bytes 262176 | tf_op jit(solution)/shard_map/ppermute | solution.py:413
  10.2 1.8 %collective-permute-start.2 = (bf16[64,2048]{1,0:T(8,128)(2,1)S(1)}, bf16[64,2048]{1,0:T(8,128)(2,1)S(1)}, u32[]{:S(2)}, u32[]{:S(2)}) collective-permute-start(bf16[64,2048]{1,0:T(8,128)(2,1)S(1)} %collective-permute-done.refs_5_.refs_2_), channel_id=1, source_target_pairs={{0,2},{2,4},{4,6},{6,7},{7,5},{5,3},{3,1},{1,0},{8,10},{10,12},{12... | collective-permute-start | bytes 786440 | tf_op jit(solution)/shard_map/ppermute | solution.py:413
  14.5 1.3 %constant_dynamic-slice_fusion = bf16[4,1,256,512]{3,2,1,0:T(8,128)(2,1)S(1)} fusion(bf16[4,2,256,512]{3,2,1,0:T(8,128)(2,1)} %bitcast.18, s32[]{:T(128)S(6)} %select_n.17), kind=kLoop, calls=%fused_computation | loop fusion | bytes 2097156 | tf_op jit(solution)/shard_map/jit(dynamic_index_in_dim)/dynamic_slice | solution.py:478
  15.8 0.8 %collective-permute-done.5.refs_12_.refs_9_ = bf16[512,384]{1,0:T(8,128)(2,1)S(1)} collective-permute-done((bf16[512,384]{1,0:T(8,128)(2,1)}, bf16[512,384]{1,0:T(8,128)(2,1)S(1)}, u32[]{:S(2)}, u32[]{:S(2)}) %collective-permute-start.5) | collective-permute-done | bytes 393248 | tf_op jit(solution)/shard_map/ppermute | solution.py:419
  16.6 1.1 %collective-permute-done.2.refs_4_ = bf16[64,2048]{1,0:T(8,128)(2,1)S(1)} collective-permute-done((bf16[64,2048]{1,0:T(8,128)(2,1)S(1)}, bf16[64,2048]{1,0:T(8,128)(2,1)S(1)}, u32[]{:S(2)}, u32[]{:S(2)}) %collective-permute-start.2) | collective-permute-done | bytes 262176 | tf_op jit(solution)/shard_map/ppermute | solution.py:413
  17.7 1.2 %collective-permute-done.4.refs_5_ = bf16[64,2048]{1,0:T(8,128)(2,1)S(1)} collective-permute-done((bf16[64,2048]{1,0:T(8,128)(2,1)S(1)}, bf16[64,2048]{1,0:T(8,128)(2,1)S(1)}, u32[]{:S(2)}, u32[]{:S(2)}) %collective-permute-start.4) | collective-permute-done | bytes 262176 | tf_op jit(solution)/shard_map/ppermute | solution.py:416
  18.9 1.5 %collective-permute-start.16 = (bf16[1024,512]{1,0:T(8,128)(2,1)S(1)}, bf16[1024,512]{1,0:T(8,128)(2,1)S(1)}, u32[]{:S(2)}, u32[]{:S(2)}) collective-permute-start(bf16[1024,512]{1,0:T(8,128)(2,1)S(1)} %bitcast.12), channel_id=1, source_target_pairs={{0,16},{8,24},{16,0},{24,8},{1,17},{9,25},{17,1},{25,9},{2,18},{10... | collective-permute-start | bytes 3145736 | tf_op jit(solution)/shard_map/ppermute | solution.py:419
  20.4 0.5 collective-permute-start.7
  20.9 1.6 %collective-permute-start.3 = (bf16[64,2048]{1,0:T(8,128)(2,1)S(1)}, bf16[64,2048]{1,0:T(8,128)(2,1)S(1)}, u32[]{:S(2)}, u32[]{:S(2)}) collective-permute-start(bf16[64,2048]{1,0:T(8,128)(2,1)S(1)} %collective-permute-done.2.refs_4_), channel_id=1, source_target_pairs={{0,2},{2,4},{4,6},{6,7},{7,5},{5,3},{3,1},{1,0},{8,10},{10,12},{12... | collective-permute-start | bytes 786440 | tf_op jit(solution)/shard_map/ppermute | solution.py:413
  22.5 0.4 collective-permute-start.9
  23.0 6.1 %shard_map.133 = (bf16[128,1280]{1,0:T(8,128)(2,1)S(1)}, bf16[320,128]{1,0:T(8,128)(2,1)S(1)}, f32[80,1280]{1,0:T(8,128)S(1)}) custom-call(s32[8,128]{1,0:T(8,128)S(1)} %get-tuple-element.29.refs_0_, bf16[64,2048]{1,0:T(8,128)(2,1)S(1)} %copy-done.2, bf16[64,2048]{1,0:T(8,128)(2,1)S(1)} %collective-permute-done.refs_5_.refs_2_, ...), custom_call_target="tpu_custom_call" | custom-call | flops 1024 | bytes 1024 | tf_op jit(solution)/shard_map/pallas_call | solution.py:366
  29.2 1.6 %collective-permute-start.8 = (bf16[32,2048]{1,0:T(8,128)(2,1)S(1)}, bf16[32,2048]{1,0:T(8,128)(2,1)S(1)}, u32[]{:S(2)}, u32[]{:S(2)}) collective-permute-start(bf16[32,2048]{1,0:T(8,128)(2,1)S(1)} %slice.6), channel_id=1, source_target_pairs={{0,2},{2,4},{4,6},{6,7},{7,5},{5,3},{3,1},{1,0},{8,10},{10,12},{12... | collective-permute-start | bytes 393224 | tf_op jit(solution)/shard_map/ppermute | solution.py:413
  30.8 0.7 %collective-permute-start.10 = (bf16[32,2048]{1,0:T(8,128)(2,1)S(1)}, bf16[32,2048]{1,0:T(8,128)(2,1)S(1)}, u32[]{:S(2)}, u32[]{:S(2)}) collective-permute-start(bf16[32,2048]{1,0:T(8,128)(2,1)S(1)} %slice.7), channel_id=1, source_target_pairs={{0,1},{2,0},{4,2},{6,4},{7,6},{5,7},{3,5},{1,3},{8,9},{10,8},{12,1... | collective-permute-start | bytes 393224 | tf_op jit(solution)/shard_map/ppermute | solution.py:416
  31.5 3.3 %shard_map.134 = (bf16[128,1792]{1,0:T(8,128)(2,1)S(1)}, bf16[448,128]{1,0:T(8,128)(2,1)S(1)}, f32[80,1792]{1,0:T(8,128)S(1)}) custom-call(s32[8,128]{1,0:T(8,128)S(1)} %get-tuple-element.29.refs_0_, bf16[64,2048]{1,0:T(8,128)(2,1)S(1)} %collective-permute-done.3.refs_1_, bf16[64,2048]{1,0:T(8,128)(2,1)S(1)} %collective-permute-done.9.refs_2_, ...), custom_call_target="tpu_custom_call" | custom-call | flops 1024 | bytes 1024 | tf_op jit(solution)/shard_map/pallas_call | solution.py:366
  34.8 1.2 %collective-permute-done.10.refs_2_ = bf16[32,2048]{1,0:T(8,128)(2,1)S(1)} collective-permute-done((bf16[32,2048]{1,0:T(8,128)(2,1)S(1)}, bf16[32,2048]{1,0:T(8,128)(2,1)S(1)}, u32[]{:S(2)}, u32[]{:S(2)}) %collective-permute-start.10) | collective-permute-done | bytes 131104 | tf_op jit(solution)/shard_map/ppermute | solution.py:416
  36.0 3.3 %shard_map.135 = (bf16[128,256]{1,0:T(8,128)(2,1)S(1)}, bf16[128,256]{1,0:T(8,128)(2,1)S(1)}, bf16[128,256]{1,0:T(8,128)(2,1)S(1)}, bf16[128,256]{1,0:T(8,128)(2,1)S(1)}, bf16[512,128]{1,0:T(8,128)(2,1)}) custom-call(s32[8,128]{1,0:T(8,128)S(1)} %get-tuple-element.29.refs_0_, bf16[32,2048]{1,0:T(8,128)(2,1)S(1)} %collective-permute-done.8.refs_1_, ...), custom_call_target="tpu_custom_call" | custom-call | flops 1024 | bytes 1024 | tf_op jit(solution)/shard_map/pallas_call | solution.py:366
  39.3 1.6 %collective-permute-start.11 = (bf16[128,256]{1,0:T(8,128)(2,1)S(1)}, bf16[128,256]{1,0:T(8,128)(2,1)S(1)}, u32[]{:S(2)}, u32[]{:S(2)}) collective-permute-start(bf16[128,256]{1,0:T(8,128)(2,1)S(1)} %get-tuple-element.44), channel_id=1, source_target_pairs={{0,2},{1,3},{2,0},{3,1},{4,6},{5,7},{6,4},{7,5},{8,10},{9,11},{10,... | collective-permute-start | bytes 196616 | tf_op jit(solution)/shard_map/ppermute | solution.py:525
  40.9 1.4 %collective-permute-start.12 = (bf16[128,256]{1,0:T(8,128)(2,1)S(1)}, bf16[128,256]{1,0:T(8,128)(2,1)S(1)}, u32[]{:S(2)}, u32[]{:S(2)}) collective-permute-start(bf16[128,256]{1,0:T(8,128)(2,1)S(1)} %get-tuple-element.45), channel_id=1, source_target_pairs={{0,4},{1,5},{2,6},{3,7},{4,0},{5,1},{6,2},{7,3},{8,12},{9,13},{10,... | collective-permute-start | bytes 196616 | tf_op jit(solution)/shard_map/ppermute | solution.py:525
  42.2 1.4 %collective-permute-start.13 = (bf16[128,256]{1,0:T(8,128)(2,1)S(1)}, bf16[128,256]{1,0:T(8,128)(2,1)S(1)}, u32[]{:S(2)}, u32[]{:S(2)}) collective-permute-start(bf16[128,256]{1,0:T(8,128)(2,1)S(1)} %get-tuple-element.46), channel_id=1, source_target_pairs={{0,6},{1,7},{2,4},{3,5},{4,2},{5,3},{6,0},{7,1},{8,14},{9,15},{10,... | collective-permute-start | bytes 196616 | tf_op jit(solution)/shard_map/ppermute | solution.py:525
  44.0 3.4 %collective-permute-done.12.refs_2_ = bf16[128,256]{1,0:T(8,128)(2,1)S(1)} collective-permute-done((bf16[128,256]{1,0:T(8,128)(2,1)S(1)}, bf16[128,256]{1,0:T(8,128)(2,1)S(1)}, u32[]{:S(2)}, u32[]{:S(2)}) %collective-permute-start.12) | collective-permute-done | bytes 65568 | tf_op jit(solution)/shard_map/ppermute | solution.py:525
  47.4 1.0 %collective-permute-done.13.refs_3_ = bf16[128,256]{1,0:T(8,128)(2,1)S(1)} collective-permute-done((bf16[128,256]{1,0:T(8,128)(2,1)S(1)}, bf16[128,256]{1,0:T(8,128)(2,1)S(1)}, u32[]{:S(2)}, u32[]{:S(2)}) %collective-permute-start.13) | collective-permute-done | bytes 65568 | tf_op jit(solution)/shard_map/ppermute | solution.py:525
  48.4 0.5 shard_map.136
  48.9 0.4 collective-permute-start.15
  49.3 1.7 %collective-permute-done.17.refs_5_ = bf16[1024,512]{1,0:T(8,128)(2,1)S(1)} collective-permute-done((bf16[1024,512]{1,0:T(8,128)(2,1)S(1)}, bf16[1024,512]{1,0:T(8,128)(2,1)S(1)}, u32[]{:S(2)}, u32[]{:S(2)}) %collective-permute-start.17) | collective-permute-done | bytes 1048608 | tf_op jit(solution)/shard_map/ppermute | solution.py:419
  51.1 0.5 shard_map.137
  51.6 0.4 collective-permute-start.18
  52.0 3.3 %collective-permute-done.15.near_came = bf16[64,1024]{1,0:T(8,128)(2,1)S(1)} collective-permute-done((bf16[64,1024]{1,0:T(8,128)(2,1)S(1)}, bf16[64,1024]{1,0:T(8,128)(2,1)S(1)}, u32[]{:S(2)}, u32[]{:S(2)}) %collective-permute-start.15) | collective-permute-done | bytes 131104 | tf_op jit(solution)/shard_map/ppermute | solution.py:525
  55.3 2.4 %collective-permute-done.18.far_came = bf16[64,1024]{1,0:T(8,128)(2,1)S(1)} collective-permute-done((bf16[64,1024]{1,0:T(8,128)(2,1)S(1)}, bf16[64,1024]{1,0:T(8,128)(2,1)S(1)}, u32[]{:S(2)}, u32[]{:S(2)}) %collective-permute-start.18) | collective-permute-done | bytes 131104 | tf_op jit(solution)/shard_map/ppermute | solution.py:525
  57.7 0.8 %shard_map.138 = bf16[64,2048]{1,0:T(8,128)(2,1)} custom-call(f32[64,1024]{1,0:T(8,128)S(1)} %get-tuple-element.49.near_kept, bf16[64,1024]{1,0:T(8,128)(2,1)S(1)} %collective-permute-done.15.near_came, f32[64,1024]{1,0:T(8,128)S(1)} %get-tuple-element.53.far_kept, bf16[64,1024]{1,0:T(8,128)(2,1)S(1)} %collective-permute-done.18.far_came), custom_call_target="tpu_custom_call" | custom-call | tf_op jit(solution)/shard_map/pallas_call | solution.py:559
  (31 shorter events, 0.9 us)
Async XLA Ops:
  0.6 13.5 %copy-start.3 = (f32[32,64]{1,0:T(8,128)S(1)}, f32[32,64]{1,0:T(8,128)}, u32[]{:S(2)}) copy-start(f32[32,64]{1,0:T(8,128)} %constant.33.clone.refs_4_) | copy-start | bytes 24580
  0.6 13.5 %copy-start = (bf16[1,2048,128]{2,1,0:T(8,128)(2,1)S(1)}, bf16[1,2048,128]{2,1,0:T(8,128)(2,1)}, u32[]{:S(2)}) copy-start(bf16[1,2048,128]{2,1,0:T(8,128)(2,1)} %refs_0_.1) | copy-start | bytes 1572868
  0.7 13.5 %copy-start.4 = (bf16[2048]{0:T(1024)(128)(2,1)S(1)}, bf16[2048]{0:T(1024)(128)(2,1)}, u32[]{:S(2)}) copy-start(bf16[2048]{0:T(1024)(128)(2,1)} %param.13) | copy-start | bytes 12292
  0.7 13.5 %copy-start.5 = (f32[64]{0:T(128)S(1)}, f32[64]{0:T(128)}, u32[]{:S(2)}) copy-start(f32[64]{0:T(128)} %param.16) | copy-start | bytes 772
  0.7 13.5 %copy-start.6 = (f32[64]{0:T(128)S(1)}, f32[64]{0:T(128)}, u32[]{:S(2)}) copy-start(f32[64]{0:T(128)} %param.17) | copy-start | bytes 772
  0.7 9.5 %collective-permute-start = (bf16[64,2048]{1,0:T(8,128)(2,1)}, bf16[64,2048]{1,0:T(8,128)(2,1)S(1)}, u32[]{:S(2)}, u32[]{:S(2)}) collective-permute-start(bf16[64,2048]{1,0:T(8,128)(2,1)} %refs_1_.1), channel_id=1, source_target_pairs={{0,2},{2,4},{4,6},{6,7},{7,5},{5,3},{3,1},{1,0},{8,10},{10,12},{12... | collective-permute-start | bytes 786440 | tf_op jit(solution)/shard_map/ppermute | solution.py:413
  3.8 8.3 %collective-permute-start.1 = (bf16[64,2048]{1,0:T(8,128)(2,1)}, bf16[64,2048]{1,0:T(8,128)(2,1)S(1)}, u32[]{:S(2)}, u32[]{:S(2)}) collective-permute-start(bf16[64,2048]{1,0:T(8,128)(2,1)} %refs_1_.1), channel_id=1, source_target_pairs={{0,1},{2,0},{4,2},{6,4},{7,6},{5,7},{3,5},{1,3},{8,9},{10,8},{12,1... | collective-permute-start | bytes 786440 | tf_op jit(solution)/shard_map/ppermute | solution.py:416
  5.7 14.7 %copy-start.1 = (bf16[512,384]{1,0:T(8,128)(2,1)S(1)}, bf16[512,384]{1,0:T(8,128)(2,1)}, u32[]{:S(2)}) copy-start(bf16[512,384]{1,0:T(8,128)(2,1)} %shard_map.132.refs_10_.refs_7_) | copy-start | bytes 1179652
  5.7 17.3 %copy-start.2 = (bf16[64,2048]{1,0:T(8,128)(2,1)S(1)}, bf16[64,2048]{1,0:T(8,128)(2,1)}, u32[]{:S(2)}) copy-start(bf16[64,2048]{1,0:T(8,128)(2,1)} %refs_1_.1) | copy-start | bytes 786436
  5.7 10.9 %collective-permute-start.5 = (bf16[512,384]{1,0:T(8,128)(2,1)}, bf16[512,384]{1,0:T(8,128)(2,1)S(1)}, u32[]{:S(2)}, u32[]{:S(2)}) collective-permute-start(bf16[512,384]{1,0:T(8,128)(2,1)} %shard_map.132.refs_10_.refs_7_), channel_id=1, source_target_pairs={{0,16},{8,24},{16,0},{24,8},{1,17},{9,25},{17,1},{25,9},{2,18},{10... | collective-permute-start | bytes 1179656 | tf_op jit(solution)/shard_map/ppermute | solution.py:419
  10.2 7.5 %collective-permute-start.2 = (bf16[64,2048]{1,0:T(8,128)(2,1)S(1)}, bf16[64,2048]{1,0:T(8,128)(2,1)S(1)}, u32[]{:S(2)}, u32[]{:S(2)}) collective-permute-start(bf16[64,2048]{1,0:T(8,128)(2,1)S(1)} %collective-permute-done.refs_5_.refs_2_), channel_id=1, source_target_pairs={{0,2},{2,4},{4,6},{6,7},{7,5},{5,3},{3,1},{1,0},{8,10},{10,12},{12... | collective-permute-start | bytes 786440 | tf_op jit(solution)/shard_map/ppermute | solution.py:413
  12.0 6.9 %collective-permute-start.4 = (bf16[64,2048]{1,0:T(8,128)(2,1)S(1)}, bf16[64,2048]{1,0:T(8,128)(2,1)S(1)}, u32[]{:S(2)}, u32[]{:S(2)}) collective-permute-start(bf16[64,2048]{1,0:T(8,128)(2,1)S(1)} %collective-permute-done.1.refs_6_.refs_3_), channel_id=1, source_target_pairs={{0,1},{2,0},{4,2},{6,4},{7,6},{5,7},{3,5},{1,3},{8,9},{10,8},{12,1... | collective-permute-start | bytes 786440 | tf_op jit(solution)/shard_map/ppermute | solution.py:416
  18.9 29.5 %collective-permute-start.16 = (bf16[1024,512]{1,0:T(8,128)(2,1)S(1)}, bf16[1024,512]{1,0:T(8,128)(2,1)S(1)}, u32[]{:S(2)}, u32[]{:S(2)}) collective-permute-start(bf16[1024,512]{1,0:T(8,128)(2,1)S(1)} %bitcast.12), channel_id=1, source_target_pairs={{0,16},{8,24},{16,0},{24,8},{1,17},{9,25},{17,1},{25,9},{2,18},{10... | collective-permute-start | bytes 3145736 | tf_op jit(solution)/shard_map/ppermute | solution.py:419
  20.4 2.5 %collective-permute-start.6 = (bf16[512,384]{1,0:T(8,128)(2,1)S(1)}, bf16[512,384]{1,0:T(8,128)(2,1)S(1)}, u32[]{:S(2)}, u32[]{:S(2)}) collective-permute-start(bf16[512,384]{1,0:T(8,128)(2,1)S(1)} %copy-done.1), channel_id=1, source_target_pairs={{0,8},{8,0},{16,24},{24,16},{1,9},{9,1},{17,25},{25,17},{2,10},{10... | collective-permute-start | bytes 1179656 | tf_op jit(solution)/shard_map/ppermute | solution.py:419
  20.4 2.5 %collective-permute-start.7 = (bf16[512,384]{1,0:T(8,128)(2,1)S(1)}, bf16[512,384]{1,0:T(8,128)(2,1)S(1)}, u32[]{:S(2)}, u32[]{:S(2)}) collective-permute-start(bf16[512,384]{1,0:T(8,128)(2,1)S(1)} %collective-permute-done.5.refs_12_.refs_9_), channel_id=1, source_target_pairs={{0,8},{8,0},{16,24},{24,16},{1,9},{9,1},{17,25},{25,17},{2,10},{10... | collective-permute-start | bytes 1179656 | tf_op jit(solution)/shard_map/ppermute | solution.py:419
  20.9 8.2 %collective-permute-start.3 = (bf16[64,2048]{1,0:T(8,128)(2,1)S(1)}, bf16[64,2048]{1,0:T(8,128)(2,1)S(1)}, u32[]{:S(2)}, u32[]{:S(2)}) collective-permute-start(bf16[64,2048]{1,0:T(8,128)(2,1)S(1)} %collective-permute-done.2.refs_4_), channel_id=1, source_target_pairs={{0,2},{2,4},{4,6},{6,7},{7,5},{5,3},{3,1},{1,0},{8,10},{10,12},{12... | collective-permute-start | bytes 786440 | tf_op jit(solution)/shard_map/ppermute | solution.py:413
  22.5 8.3 %collective-permute-start.9 = (bf16[64,2048]{1,0:T(8,128)(2,1)S(1)}, bf16[64,2048]{1,0:T(8,128)(2,1)S(1)}, u32[]{:S(2)}, u32[]{:S(2)}) collective-permute-start(bf16[64,2048]{1,0:T(8,128)(2,1)S(1)} %collective-permute-done.4.refs_5_), channel_id=1, source_target_pairs={{0,1},{2,0},{4,2},{6,4},{7,6},{5,7},{3,5},{1,3},{8,9},{10,8},{12,1... | collective-permute-start | bytes 786440 | tf_op jit(solution)/shard_map/ppermute | solution.py:416
  29.2 5.6 %collective-permute-start.8 = (bf16[32,2048]{1,0:T(8,128)(2,1)S(1)}, bf16[32,2048]{1,0:T(8,128)(2,1)S(1)}, u32[]{:S(2)}, u32[]{:S(2)}) collective-permute-start(bf16[32,2048]{1,0:T(8,128)(2,1)S(1)} %slice.6), channel_id=1, source_target_pairs={{0,2},{2,4},{4,6},{6,7},{7,5},{5,3},{3,1},{1,0},{8,10},{10,12},{12... | collective-permute-start | bytes 393224 | tf_op jit(solution)/shard_map/ppermute | solution.py:413
  30.8 5.2 %collective-permute-start.10 = (bf16[32,2048]{1,0:T(8,128)(2,1)S(1)}, bf16[32,2048]{1,0:T(8,128)(2,1)S(1)}, u32[]{:S(2)}, u32[]{:S(2)}) collective-permute-start(bf16[32,2048]{1,0:T(8,128)(2,1)S(1)} %slice.7), channel_id=1, source_target_pairs={{0,1},{2,0},{4,2},{6,4},{7,6},{5,7},{3,5},{1,3},{8,9},{10,8},{12,1... | collective-permute-start | bytes 393224 | tf_op jit(solution)/shard_map/ppermute | solution.py:416
  39.3 4.7 %collective-permute-start.11 = (bf16[128,256]{1,0:T(8,128)(2,1)S(1)}, bf16[128,256]{1,0:T(8,128)(2,1)S(1)}, u32[]{:S(2)}, u32[]{:S(2)}) collective-permute-start(bf16[128,256]{1,0:T(8,128)(2,1)S(1)} %get-tuple-element.44), channel_id=1, source_target_pairs={{0,2},{1,3},{2,0},{3,1},{4,6},{5,7},{6,4},{7,5},{8,10},{9,11},{10,... | collective-permute-start | bytes 196616 | tf_op jit(solution)/shard_map/ppermute | solution.py:525
  40.9 6.5 %collective-permute-start.12 = (bf16[128,256]{1,0:T(8,128)(2,1)S(1)}, bf16[128,256]{1,0:T(8,128)(2,1)S(1)}, u32[]{:S(2)}, u32[]{:S(2)}) collective-permute-start(bf16[128,256]{1,0:T(8,128)(2,1)S(1)} %get-tuple-element.45), channel_id=1, source_target_pairs={{0,4},{1,5},{2,6},{3,7},{4,0},{5,1},{6,2},{7,3},{8,12},{9,13},{10,... | collective-permute-start | bytes 196616 | tf_op jit(solution)/shard_map/ppermute | solution.py:525
  42.2 6.2 %collective-permute-start.13 = (bf16[128,256]{1,0:T(8,128)(2,1)S(1)}, bf16[128,256]{1,0:T(8,128)(2,1)S(1)}, u32[]{:S(2)}, u32[]{:S(2)}) collective-permute-start(bf16[128,256]{1,0:T(8,128)(2,1)S(1)} %get-tuple-element.46), channel_id=1, source_target_pairs={{0,6},{1,7},{2,4},{3,5},{4,2},{5,3},{6,0},{7,1},{8,14},{9,15},{10,... | collective-permute-start | bytes 196616 | tf_op jit(solution)/shard_map/ppermute | solution.py:525
  43.7 4.7 %collective-permute-start.14 = (bf16[1024,512]{1,0:T(8,128)(2,1)S(1)}, bf16[1024,512]{1,0:T(8,128)(2,1)S(1)}, u32[]{:S(2)}, u32[]{:S(2)}) collective-permute-start(bf16[1024,512]{1,0:T(8,128)(2,1)S(1)} %bitcast.13), channel_id=1, source_target_pairs={{0,8},{8,0},{16,24},{24,16},{1,9},{9,1},{17,25},{25,17},{2,10},{10... | collective-permute-start | bytes 3145736 | tf_op jit(solution)/shard_map/ppermute | solution.py:419
  48.4 2.7 %collective-permute-start.17 = (bf16[1024,512]{1,0:T(8,128)(2,1)S(1)}, bf16[1024,512]{1,0:T(8,128)(2,1)S(1)}, u32[]{:S(2)}, u32[]{:S(2)}) collective-permute-start(bf16[1024,512]{1,0:T(8,128)(2,1)S(1)} %collective-permute-done.16.refs_4_), channel_id=1, source_target_pairs={{0,8},{8,0},{16,24},{24,16},{1,9},{9,1},{17,25},{25,17},{2,10},{10... | collective-permute-start | bytes 3145736 | tf_op jit(solution)/shard_map/ppermute | solution.py:419
  48.9 6.4 %collective-permute-start.15 = (bf16[64,1024]{1,0:T(8,128)(2,1)S(1)}, bf16[64,1024]{1,0:T(8,128)(2,1)S(1)}, u32[]{:S(2)}, u32[]{:S(2)}) collective-permute-start(bf16[64,1024]{1,0:T(8,128)(2,1)S(1)} %get-tuple-element.50), channel_id=1, source_target_pairs={{0,1},{1,0},{2,3},{3,2},{4,5},{5,4},{6,7},{7,6},{8,9},{9,8},{10,11... | collective-permute-start | bytes 393224 | tf_op jit(solution)/shard_map/ppermute | solution.py:525
  51.6 6.1 %collective-permute-start.18 = (bf16[64,1024]{1,0:T(8,128)(2,1)S(1)}, bf16[64,1024]{1,0:T(8,128)(2,1)S(1)}, u32[]{:S(2)}, u32[]{:S(2)}) collective-permute-start(bf16[64,1024]{1,0:T(8,128)(2,1)S(1)} %get-tuple-element.54), channel_id=1, source_target_pairs={{0,1},{1,0},{2,3},{3,2},{4,5},{5,4},{6,7},{7,6},{8,9},{9,8},{10,11... | collective-permute-start | bytes 393224 | tf_op jit(solution)/shard_map/ppermute | solution.py:525

commit v4 on v3

--- a/solution.py
+++ b/solution.py
@@ -100,8 +100,9 @@
     projected_ref[...] = total
     scale = head_dim ** (-0.5)
 
+    if old and not final:
+        queries_out[:, pl.ds(0, old * count)] = queries_in[...]
     if old:
-        queries_out[:, pl.ds(0, old * count)] = queries_in[...]
         keyval_out[pl.ds(0, old * rows), :] = keyval_in[...]
     padding = jnp.zeros((head_dim, count), jnp.bfloat16)
     query_gains = head_ref[:head_dim, :]
@@ -184,8 +185,6 @@
         ) + jnp.dot(new_values, near_unnormed, preferred_element_type=jnp.float32)
         stats_out[:, span] = pack(row_max, sums)
 
-    attend_new()
-
     if old:
         span = pl.ds(0, old * count)
         at = jnp.concatenate([lane_token + ids[block] * rows for block in range(old)], axis=1)
@@ -205,6 +204,8 @@
         stats_out[:, span] = pack(row_max, sums) + jnp.where(
             lax.broadcasted_iota(jnp.int32, before.shape, 0) < 8, 0.0, before
         )
+
+    attend_new()
 
     if final:
         for block in range(blocks):

time: 58.7 us -> 58.4 us (level)
  no operation moved by 1% of the time
where the time goes in v4:
time: 58.4 us; the launch traced here: 58.1 us
  waiting for transfers between devices  19 us (33%)
  starting transfers between devices  18.7 us (32%)
  Pallas kernels  16.3 us (28%)
  between operations  2.76 us (5%)
  local copies, waits for them, and re-layouts  1.36 us (2%)
    pallas_call x3, Pallas kernels, run_stage(): pl.pallas_call(functools.partial(stage_kernel, plan, final), out_shape=ou...  12.4 us
    ppermute x5, waiting for transfers between devices, from_member(): return lax.ppermute(block, 'tensor', route)  10.5 us
    ppermute x4, starting transfers between devices, forward(): return lax.ppermute(block, 'tensor', ring_route(1))  8.1 us
    ppermute x5, starting transfers between devices, from_member(): return lax.ppermute(block, 'tensor', route)  5.19 us
    ppermute x6, starting transfers between devices, from_dp(): lax.ppermute(block, 'dp', [(one, one ^ apart) for one in range(dp_size)])  4.07 us
    ppermute x4, waiting for transfers between devices, forward(): return lax.ppermute(block, 'tensor', ring_route(1))  3.56 us
    ppermute x6, waiting for transfers between devices, from_dp(): lax.ppermute(block, 'dp', [(one, one ^ apart) for one in range(dp_size)])  2.59 us
    ppermute x4, waiting for transfers between devices, backward(): return lax.ppermute(block, 'tensor', ring_route(-1))  2.37 us
  transfers between devices with their start and end apart: 19, of which 11 were waited for; matrix products, arithmetic and copies ran while one was open for 2% of the time, Pallas kernels for 27%

profile of v4, /device:TPU:0, one launch (start us, length us, event | category | flops | bytes accessed | tf_op | source)
XLA Modules:
  0.0 58.1 jit_solution(2206093747951611556)
XLA Ops:
  0.7 3.1 %collective-permute-start = (bf16[64,2048]{1,0:T(8,128)(2,1)}, bf16[64,2048]{1,0:T(8,128)(2,1)S(1)}, u32[]{:S(2)}, u32[]{:S(2)}) collective-permute-start(bf16[64,2048]{1,0:T(8,128)(2,1)} %refs_1_.1), channel_id=1, source_target_pairs={{0,2},{2,4},{4,6},{6,7},{7,5},{5,3},{3,1},{1,0},{8,10},{10,12},{12... | collective-permute-start | bytes 786440 | tf_op jit(solution)/shard_map/ppermute | solution.py:414
  3.8 1.9 %shard_map.132.refs_10_.refs_7_ = bf16[512,384]{1,0:T(8,128)(2,1)} custom-call(bf16[512,2048]{1,0:T(8,128)(2,1)} %query_ref.1, bf16[2,512,512]{2,1,0:T(8,128)(2,1)} %keyval_ref.1), custom_call_target="tpu_custom_call" | custom-call | bytes 33554432 | tf_op jit(solution)/shard_map/pallas_call | solution.py:423
  5.7 2.0 %collective-permute-start.5 = (bf16[512,384]{1,0:T(8,128)(2,1)}, bf16[512,384]{1,0:T(8,128)(2,1)S(1)}, u32[]{:S(2)}, u32[]{:S(2)}) collective-permute-start(bf16[512,384]{1,0:T(8,128)(2,1)} %shard_map.132.refs_10_.refs_7_), channel_id=1, source_target_pairs={{0,16},{8,24},{16,0},{24,8},{1,17},{9,25},{17,1},{25,9},{2,18},{10... | collective-permute-start | bytes 1179656 | tf_op jit(solution)/shard_map/ppermute | solution.py:420
  7.8 2.4 %collective-permute-done.refs_5_.refs_2_ = bf16[64,2048]{1,0:T(8,128)(2,1)S(1)} collective-permute-done((bf16[64,2048]{1,0:T(8,128)(2,1)}, bf16[64,2048]{1,0:T(8,128)(2,1)S(1)}, u32[]{:S(2)}, u32[]{:S(2)}) %collective-permute-start) | collective-permute-done | bytes 262176 | tf_op jit(solution)/shard_map/ppermute | solution.py:414
  10.2 1.8 %collective-permute-start.2 = (bf16[64,2048]{1,0:T(8,128)(2,1)S(1)}, bf16[64,2048]{1,0:T(8,128)(2,1)S(1)}, u32[]{:S(2)}, u32[]{:S(2)}) collective-permute-start(bf16[64,2048]{1,0:T(8,128)(2,1)S(1)} %collective-permute-done.refs_5_.refs_2_), channel_id=1, source_target_pairs={{0,2},{2,4},{4,6},{6,7},{7,5},{5,3},{3,1},{1,0},{8,10},{10,12},{12... | collective-permute-start | bytes 786440 | tf_op jit(solution)/shard_map/ppermute | solution.py:414
  14.5 1.3 %constant_dynamic-slice_fusion = bf16[4,1,256,512]{3,2,1,0:T(8,128)(2,1)S(1)} fusion(bf16[4,2,256,512]{3,2,1,0:T(8,128)(2,1)} %bitcast.18, s32[]{:T(128)S(6)} %select_n.17), kind=kLoop, calls=%fused_computation | loop fusion | bytes 2097156 | tf_op jit(solution)/shard_map/jit(dynamic_index_in_dim)/dynamic_slice | solution.py:479
  15.8 0.8 %collective-permute-done.5.refs_12_.refs_9_ = bf16[512,384]{1,0:T(8,128)(2,1)S(1)} collective-permute-done((bf16[512,384]{1,0:T(8,128)(2,1)}, bf16[512,384]{1,0:T(8,128)(2,1)S(1)}, u32[]{:S(2)}, u32[]{:S(2)}) %collective-permute-start.5) | collective-permute-done | bytes 393248 | tf_op jit(solution)/shard_map/ppermute | solution.py:420
  16.6 1.1 %collective-permute-done.2.refs_4_ = bf16[64,2048]{1,0:T(8,128)(2,1)S(1)} collective-permute-done((bf16[64,2048]{1,0:T(8,128)(2,1)S(1)}, bf16[64,2048]{1,0:T(8,128)(2,1)S(1)}, u32[]{:S(2)}, u32[]{:S(2)}) %collective-permute-start.2) | collective-permute-done | bytes 262176 | tf_op jit(solution)/shard_map/ppermute | solution.py:414
  17.7 1.2 %collective-permute-done.4.refs_5_ = bf16[64,2048]{1,0:T(8,128)(2,1)S(1)} collective-permute-done((bf16[64,2048]{1,0:T(8,128)(2,1)S(1)}, bf16[64,2048]{1,0:T(8,128)(2,1)S(1)}, u32[]{:S(2)}, u32[]{:S(2)}) %collective-permute-start.4) | collective-permute-done | bytes 262176 | tf_op jit(solution)/shard_map/ppermute | solution.py:417
  18.9 1.5 %collective-permute-start.16 = (bf16[1024,512]{1,0:T(8,128)(2,1)S(1)}, bf16[1024,512]{1,0:T(8,128)(2,1)S(1)}, u32[]{:S(2)}, u32[]{:S(2)}) collective-permute-start(bf16[1024,512]{1,0:T(8,128)(2,1)S(1)} %bitcast.12), channel_id=1, source_target_pairs={{0,16},{8,24},{16,0},{24,8},{1,17},{9,25},{17,1},{25,9},{2,18},{10... | collective-permute-start | bytes 3145736 | tf_op jit(solution)/shard_map/ppermute | solution.py:420
  20.4 0.5 collective-permute-start.7
  20.9 1.6 %collective-permute-start.3 = (bf16[64,2048]{1,0:T(8,128)(2,1)S(1)}, bf16[64,2048]{1,0:T(8,128)(2,1)S(1)}, u32[]{:S(2)}, u32[]{:S(2)}) collective-permute-start(bf16[64,2048]{1,0:T(8,128)(2,1)S(1)} %collective-permute-done.2.refs_4_), channel_id=1, source_target_pairs={{0,2},{2,4},{4,6},{6,7},{7,5},{5,3},{3,1},{1,0},{8,10},{10,12},{12... | collective-permute-start | bytes 786440 | tf_op jit(solution)/shard_map/ppermute | solution.py:414
  22.5 0.4 collective-permute-start.9
  23.0 6.1 %shard_map.133 = (bf16[128,1280]{1,0:T(8,128)(2,1)S(1)}, bf16[320,128]{1,0:T(8,128)(2,1)S(1)}, f32[80,1280]{1,0:T(8,128)S(1)}) custom-call(s32[8,128]{1,0:T(8,128)S(1)} %get-tuple-element.29.refs_0_, bf16[64,2048]{1,0:T(8,128)(2,1)S(1)} %copy-done.2, bf16[64,2048]{1,0:T(8,128)(2,1)S(1)} %collective-permute-done.refs_5_.refs_2_, ...), custom_call_target="tpu_custom_call" | custom-call | flops 1024 | bytes 1024 | tf_op jit(solution)/shard_map/pallas_call | solution.py:367
  29.2 1.6 %collective-permute-start.8 = (bf16[32,2048]{1,0:T(8,128)(2,1)S(1)}, bf16[32,2048]{1,0:T(8,128)(2,1)S(1)}, u32[]{:S(2)}, u32[]{:S(2)}) collective-permute-start(bf16[32,2048]{1,0:T(8,128)(2,1)S(1)} %slice.6), channel_id=1, source_target_pairs={{0,2},{2,4},{4,6},{6,7},{7,5},{5,3},{3,1},{1,0},{8,10},{10,12},{12... | collective-permute-start | bytes 393224 | tf_op jit(solution)/shard_map/ppermute | solution.py:414
  30.8 0.7 %collective-permute-start.10 = (bf16[32,2048]{1,0:T(8,128)(2,1)S(1)}, bf16[32,2048]{1,0:T(8,128)(2,1)S(1)}, u32[]{:S(2)}, u32[]{:S(2)}) collective-permute-start(bf16[32,2048]{1,0:T(8,128)(2,1)S(1)} %slice.7), channel_id=1, source_target_pairs={{0,1},{2,0},{4,2},{6,4},{7,6},{5,7},{3,5},{1,3},{8,9},{10,8},{12,1... | collective-permute-start | bytes 393224 | tf_op jit(solution)/shard_map/ppermute | solution.py:417
  31.5 3.4 %shard_map.134 = (bf16[128,1792]{1,0:T(8,128)(2,1)S(1)}, bf16[448,128]{1,0:T(8,128)(2,1)S(1)}, f32[80,1792]{1,0:T(8,128)S(1)}) custom-call(s32[8,128]{1,0:T(8,128)S(1)} %get-tuple-element.29.refs_0_, bf16[64,2048]{1,0:T(8,128)(2,1)S(1)} %collective-permute-done.3.refs_1_, bf16[64,2048]{1,0:T(8,128)(2,1)S(1)} %collective-permute-done.9.refs_2_, ...), custom_call_target="tpu_custom_call" | custom-call | flops 1024 | bytes 1024 | tf_op jit(solution)/shard_map/pallas_call | solution.py:367
  34.9 1.1 %collective-permute-done.10.refs_2_ = bf16[32,2048]{1,0:T(8,128)(2,1)S(1)} collective-permute-done((bf16[32,2048]{1,0:T(8,128)(2,1)S(1)}, bf16[32,2048]{1,0:T(8,128)(2,1)S(1)}, u32[]{:S(2)}, u32[]{:S(2)}) %collective-permute-start.10) | collective-permute-done | bytes 131104 | tf_op jit(solution)/shard_map/ppermute | solution.py:417
  36.0 2.9 %shard_map.135 = (bf16[128,256]{1,0:T(8,128)(2,1)S(1)}, bf16[128,256]{1,0:T(8,128)(2,1)S(1)}, bf16[128,256]{1,0:T(8,128)(2,1)S(1)}, bf16[128,256]{1,0:T(8,128)(2,1)S(1)}, bf16[512,128]{1,0:T(8,128)(2,1)}) custom-call(s32[8,128]{1,0:T(8,128)S(1)} %get-tuple-element.29.refs_0_, bf16[32,2048]{1,0:T(8,128)(2,1)S(1)} %collective-permute-done.8.refs_1_, ...), custom_call_target="tpu_custom_call" | custom-call | flops 1024 | bytes 1024 | tf_op jit(solution)/shard_map/pallas_call | solution.py:367
  39.0 1.6 %collective-permute-start.11 = (bf16[128,256]{1,0:T(8,128)(2,1)S(1)}, bf16[128,256]{1,0:T(8,128)(2,1)S(1)}, u32[]{:S(2)}, u32[]{:S(2)}) collective-permute-start(bf16[128,256]{1,0:T(8,128)(2,1)S(1)} %get-tuple-element.44), channel_id=1, source_target_pairs={{0,2},{1,3},{2,0},{3,1},{4,6},{5,7},{6,4},{7,5},{8,10},{9,11},{10,... | collective-permute-start | bytes 196616 | tf_op jit(solution)/shard_map/ppermute | solution.py:526
  40.5 1.4 %collective-permute-start.12 = (bf16[128,256]{1,0:T(8,128)(2,1)S(1)}, bf16[128,256]{1,0:T(8,128)(2,1)S(1)}, u32[]{:S(2)}, u32[]{:S(2)}) collective-permute-start(bf16[128,256]{1,0:T(8,128)(2,1)S(1)} %get-tuple-element.45), channel_id=1, source_target_pairs={{0,4},{1,5},{2,6},{3,7},{4,0},{5,1},{6,2},{7,3},{8,12},{9,13},{10,... | collective-permute-start | bytes 196616 | tf_op jit(solution)/shard_map/ppermute | solution.py:526
  41.9 1.4 %collective-permute-start.13 = (bf16[128,256]{1,0:T(8,128)(2,1)S(1)}, bf16[128,256]{1,0:T(8,128)(2,1)S(1)}, u32[]{:S(2)}, u32[]{:S(2)}) collective-permute-start(bf16[128,256]{1,0:T(8,128)(2,1)S(1)} %get-tuple-element.46), channel_id=1, source_target_pairs={{0,6},{1,7},{2,4},{3,5},{4,2},{5,3},{6,0},{7,1},{8,14},{9,15},{10,... | collective-permute-start | bytes 196616 | tf_op jit(solution)/shard_map/ppermute | solution.py:526
  43.7 3.4 %collective-permute-done.12.refs_2_ = bf16[128,256]{1,0:T(8,128)(2,1)S(1)} collective-permute-done((bf16[128,256]{1,0:T(8,128)(2,1)S(1)}, bf16[128,256]{1,0:T(8,128)(2,1)S(1)}, u32[]{:S(2)}, u32[]{:S(2)}) %collective-permute-start.12) | collective-permute-done | bytes 65568 | tf_op jit(solution)/shard_map/ppermute | solution.py:526
  47.1 1.0 %collective-permute-done.13.refs_3_ = bf16[128,256]{1,0:T(8,128)(2,1)S(1)} collective-permute-done((bf16[128,256]{1,0:T(8,128)(2,1)S(1)}, bf16[128,256]{1,0:T(8,128)(2,1)S(1)}, u32[]{:S(2)}, u32[]{:S(2)}) %collective-permute-start.13) | collective-permute-done | bytes 65568 | tf_op jit(solution)/shard_map/ppermute | solution.py:526
  48.1 0.5 shard_map.136
  48.6 0.4 collective-permute-start.15
  49.0 1.7 %collective-permute-done.17.refs_5_ = bf16[1024,512]{1,0:T(8,128)(2,1)S(1)} collective-permute-done((bf16[1024,512]{1,0:T(8,128)(2,1)S(1)}, bf16[1024,512]{1,0:T(8,128)(2,1)S(1)}, u32[]{:S(2)}, u32[]{:S(2)}) %collective-permute-start.17) | collective-permute-done | bytes 1048608 | tf_op jit(solution)/shard_map/ppermute | solution.py:420
  50.8 0.5 shard_map.137
  51.3 0.4 collective-permute-start.18
  51.7 3.3 %collective-permute-done.15.near_came = bf16[64,1024]{1,0:T(8,128)(2,1)S(1)} collective-permute-done((bf16[64,1024]{1,0:T(8,128)(2,1)S(1)}, bf16[64,1024]{1,0:T(8,128)(2,1)S(1)}, u32[]{:S(2)}, u32[]{:S(2)}) %collective-permute-start.15) | collective-permute-done | bytes 131104 | tf_op jit(solution)/shard_map/ppermute | solution.py:526
  55.0 2.4 %collective-permute-done.18.far_came = bf16[64,1024]{1,0:T(8,128)(2,1)S(1)} collective-permute-done((bf16[64,1024]{1,0:T(8,128)(2,1)S(1)}, bf16[64,1024]{1,0:T(8,128)(2,1)S(1)}, u32[]{:S(2)}, u32[]{:S(2)}) %collective-permute-start.18) | collective-permute-done | bytes 131104 | tf_op jit(solution)/shard_map/ppermute | solution.py:526
  57.4 0.8 %shard_map.138 = bf16[64,2048]{1,0:T(8,128)(2,1)} custom-call(f32[64,1024]{1,0:T(8,128)S(1)} %get-tuple-element.49.near_kept, bf16[64,1024]{1,0:T(8,128)(2,1)S(1)} %collective-permute-done.15.near_came, f32[64,1024]{1,0:T(8,128)S(1)} %get-tuple-element.53.far_kept, bf16[64,1024]{1,0:T(8,128)(2,1)S(1)} %collective-permute-done.18.far_came), custom_call_target="tpu_custom_call" | custom-call | tf_op jit(solution)/shard_map/pallas_call | solution.py:560
  (31 shorter events, 0.9 us)
Async XLA Ops:
  0.6 13.5 %copy-start.3 = (f32[32,64]{1,0:T(8,128)S(1)}, f32[32,64]{1,0:T(8,128)}, u32[]{:S(2)}) copy-start(f32[32,64]{1,0:T(8,128)} %constant.33.clone.refs_4_) | copy-start | bytes 24580
  0.6 13.5 %copy-start = (bf16[1,2048,128]{2,1,0:T(8,128)(2,1)S(1)}, bf16[1,2048,128]{2,1,0:T(8,128)(2,1)}, u32[]{:S(2)}) copy-start(bf16[1,2048,128]{2,1,0:T(8,128)(2,1)} %refs_0_.1) | copy-start | bytes 1572868
  0.7 13.5 %copy-start.4 = (bf16[2048]{0:T(1024)(128)(2,1)S(1)}, bf16[2048]{0:T(1024)(128)(2,1)}, u32[]{:S(2)}) copy-start(bf16[2048]{0:T(1024)(128)(2,1)} %param.13) | copy-start | bytes 12292
  0.7 13.5 %copy-start.5 = (f32[64]{0:T(128)S(1)}, f32[64]{0:T(128)}, u32[]{:S(2)}) copy-start(f32[64]{0:T(128)} %param.16) | copy-start | bytes 772
  0.7 13.5 %copy-start.6 = (f32[64]{0:T(128)S(1)}, f32[64]{0:T(128)}, u32[]{:S(2)}) copy-start(f32[64]{0:T(128)} %param.17) | copy-start | bytes 772
  0.7 9.5 %collective-permute-start = (bf16[64,2048]{1,0:T(8,128)(2,1)}, bf16[64,2048]{1,0:T(8,128)(2,1)S(1)}, u32[]{:S(2)}, u32[]{:S(2)}) collective-permute-start(bf16[64,2048]{1,0:T(8,128)(2,1)} %refs_1_.1), channel_id=1, source_target_pairs={{0,2},{2,4},{4,6},{6,7},{7,5},{5,3},{3,1},{1,0},{8,10},{10,12},{12... | collective-permute-start | bytes 786440 | tf_op jit(solution)/shard_map/ppermute | solution.py:414
  3.8 8.3 %collective-permute-start.1 = (bf16[64,2048]{1,0:T(8,128)(2,1)}, bf16[64,2048]{1,0:T(8,128)(2,1)S(1)}, u32[]{:S(2)}, u32[]{:S(2)}) collective-permute-start(bf16[64,2048]{1,0:T(8,128)(2,1)} %refs_1_.1), channel_id=1, source_target_pairs={{0,1},{2,0},{4,2},{6,4},{7,6},{5,7},{3,5},{1,3},{8,9},{10,8},{12,1... | collective-permute-start | bytes 786440 | tf_op jit(solution)/shard_map/ppermute | solution.py:417
  5.7 14.7 %copy-start.1 = (bf16[512,384]{1,0:T(8,128)(2,1)S(1)}, bf16[512,384]{1,0:T(8,128)(2,1)}, u32[]{:S(2)}) copy-start(bf16[512,384]{1,0:T(8,128)(2,1)} %shard_map.132.refs_10_.refs_7_) | copy-start | bytes 1179652
  5.7 17.3 %copy-start.2 = (bf16[64,2048]{1,0:T(8,128)(2,1)S(1)}, bf16[64,2048]{1,0:T(8,128)(2,1)}, u32[]{:S(2)}) copy-start(bf16[64,2048]{1,0:T(8,128)(2,1)} %refs_1_.1) | copy-start | bytes 786436
  5.7 10.9 %collective-permute-start.5 = (bf16[512,384]{1,0:T(8,128)(2,1)}, bf16[512,384]{1,0:T(8,128)(2,1)S(1)}, u32[]{:S(2)}, u32[]{:S(2)}) collective-permute-start(bf16[512,384]{1,0:T(8,128)(2,1)} %shard_map.132.refs_10_.refs_7_), channel_id=1, source_target_pairs={{0,16},{8,24},{16,0},{24,8},{1,17},{9,25},{17,1},{25,9},{2,18},{10... | collective-permute-start | bytes 1179656 | tf_op jit(solution)/shard_map/ppermute | solution.py:420
  10.2 7.5 %collective-permute-start.2 = (bf16[64,2048]{1,0:T(8,128)(2,1)S(1)}, bf16[64,2048]{1,0:T(8,128)(2,1)S(1)}, u32[]{:S(2)}, u32[]{:S(2)}) collective-permute-start(bf16[64,2048]{1,0:T(8,128)(2,1)S(1)} %collective-permute-done.refs_5_.refs_2_), channel_id=1, source_target_pairs={{0,2},{2,4},{4,6},{6,7},{7,5},{5,3},{3,1},{1,0},{8,10},{10,12},{12... | collective-permute-start | bytes 786440 | tf_op jit(solution)/shard_map/ppermute | solution.py:414
  12.0 6.9 %collective-permute-start.4 = (bf16[64,2048]{1,0:T(8,128)(2,1)S(1)}, bf16[64,2048]{1,0:T(8,128)(2,1)S(1)}, u32[]{:S(2)}, u32[]{:S(2)}) collective-permute-start(bf16[64,2048]{1,0:T(8,128)(2,1)S(1)} %collective-permute-done.1.refs_6_.refs_3_), channel_id=1, source_target_pairs={{0,1},{2,0},{4,2},{6,4},{7,6},{5,7},{3,5},{1,3},{8,9},{10,8},{12,1... | collective-permute-start | bytes 786440 | tf_op jit(solution)/shard_map/ppermute | solution.py:417
  18.9 29.2 %collective-permute-start.16 = (bf16[1024,512]{1,0:T(8,128)(2,1)S(1)}, bf16[1024,512]{1,0:T(8,128)(2,1)S(1)}, u32[]{:S(2)}, u32[]{:S(2)}) collective-permute-start(bf16[1024,512]{1,0:T(8,128)(2,1)S(1)} %bitcast.12), channel_id=1, source_target_pairs={{0,16},{8,24},{16,0},{24,8},{1,17},{9,25},{17,1},{25,9},{2,18},{10... | collective-permute-start | bytes 3145736 | tf_op jit(solution)/shard_map/ppermute | solution.py:420
  20.4 2.5 %collective-permute-start.6 = (bf16[512,384]{1,0:T(8,128)(2,1)S(1)}, bf16[512,384]{1,0:T(8,128)(2,1)S(1)}, u32[]{:S(2)}, u32[]{:S(2)}) collective-permute-start(bf16[512,384]{1,0:T(8,128)(2,1)S(1)} %copy-done.1), channel_id=1, source_target_pairs={{0,8},{8,0},{16,24},{24,16},{1,9},{9,1},{17,25},{25,17},{2,10},{10... | collective-permute-start | bytes 1179656 | tf_op jit(solution)/shard_map/ppermute | solution.py:420
  20.4 2.5 %collective-permute-start.7 = (bf16[512,384]{1,0:T(8,128)(2,1)S(1)}, bf16[512,384]{1,0:T(8,128)(2,1)S(1)}, u32[]{:S(2)}, u32[]{:S(2)}) collective-permute-start(bf16[512,384]{1,0:T(8,128)(2,1)S(1)} %collective-permute-done.5.refs_12_.refs_9_), channel_id=1, source_target_pairs={{0,8},{8,0},{16,24},{24,16},{1,9},{9,1},{17,25},{25,17},{2,10},{10... | collective-permute-start | bytes 1179656 | tf_op jit(solution)/shard_map/ppermute | solution.py:420
  20.9 8.2 %collective-permute-start.3 = (bf16[64,2048]{1,0:T(8,128)(2,1)S(1)}, bf16[64,2048]{1,0:T(8,128)(2,1)S(1)}, u32[]{:S(2)}, u32[]{:S(2)}) collective-permute-start(bf16[64,2048]{1,0:T(8,128)(2,1)S(1)} %collective-permute-done.2.refs_4_), channel_id=1, source_target_pairs={{0,2},{2,4},{4,6},{6,7},{7,5},{5,3},{3,1},{1,0},{8,10},{10,12},{12... | collective-permute-start | bytes 786440 | tf_op jit(solution)/shard_map/ppermute | solution.py:414
  22.5 8.3 %collective-permute-start.9 = (bf16[64,2048]{1,0:T(8,128)(2,1)S(1)}, bf16[64,2048]{1,0:T(8,128)(2,1)S(1)}, u32[]{:S(2)}, u32[]{:S(2)}) collective-permute-start(bf16[64,2048]{1,0:T(8,128)(2,1)S(1)} %collective-permute-done.4.refs_5_), channel_id=1, source_target_pairs={{0,1},{2,0},{4,2},{6,4},{7,6},{5,7},{3,5},{1,3},{8,9},{10,8},{12,1... | collective-permute-start | bytes 786440 | tf_op jit(solution)/shard_map/ppermute | solution.py:417
  29.2 5.7 %collective-permute-start.8 = (bf16[32,2048]{1,0:T(8,128)(2,1)S(1)}, bf16[32,2048]{1,0:T(8,128)(2,1)S(1)}, u32[]{:S(2)}, u32[]{:S(2)}) collective-permute-start(bf16[32,2048]{1,0:T(8,128)(2,1)S(1)} %slice.6), channel_id=1, source_target_pairs={{0,2},{2,4},{4,6},{6,7},{7,5},{5,3},{3,1},{1,0},{8,10},{10,12},{12... | collective-permute-start | bytes 393224 | tf_op jit(solution)/shard_map/ppermute | solution.py:414
  30.8 5.2 %collective-permute-start.10 = (bf16[32,2048]{1,0:T(8,128)(2,1)S(1)}, bf16[32,2048]{1,0:T(8,128)(2,1)S(1)}, u32[]{:S(2)}, u32[]{:S(2)}) collective-permute-start(bf16[32,2048]{1,0:T(8,128)(2,1)S(1)} %slice.7), channel_id=1, source_target_pairs={{0,1},{2,0},{4,2},{6,4},{7,6},{5,7},{3,5},{1,3},{8,9},{10,8},{12,1... | collective-permute-start | bytes 393224 | tf_op jit(solution)/shard_map/ppermute | solution.py:417
  39.0 4.7 %collective-permute-start.11 = (bf16[128,256]{1,0:T(8,128)(2,1)S(1)}, bf16[128,256]{1,0:T(8,128)(2,1)S(1)}, u32[]{:S(2)}, u32[]{:S(2)}) collective-permute-start(bf16[128,256]{1,0:T(8,128)(2,1)S(1)} %get-tuple-element.44), channel_id=1, source_target_pairs={{0,2},{1,3},{2,0},{3,1},{4,6},{5,7},{6,4},{7,5},{8,10},{9,11},{10,... | collective-permute-start | bytes 196616 | tf_op jit(solution)/shard_map/ppermute | solution.py:526
  40.5 6.6 %collective-permute-start.12 = (bf16[128,256]{1,0:T(8,128)(2,1)S(1)}, bf16[128,256]{1,0:T(8,128)(2,1)S(1)}, u32[]{:S(2)}, u32[]{:S(2)}) collective-permute-start(bf16[128,256]{1,0:T(8,128)(2,1)S(1)} %get-tuple-element.45), channel_id=1, source_target_pairs={{0,4},{1,5},{2,6},{3,7},{4,0},{5,1},{6,2},{7,3},{8,12},{9,13},{10,... | collective-permute-start | bytes 196616 | tf_op jit(solution)/shard_map/ppermute | solution.py:526
  41.9 6.2 %collective-permute-start.13 = (bf16[128,256]{1,0:T(8,128)(2,1)S(1)}, bf16[128,256]{1,0:T(8,128)(2,1)S(1)}, u32[]{:S(2)}, u32[]{:S(2)}) collective-permute-start(bf16[128,256]{1,0:T(8,128)(2,1)S(1)} %get-tuple-element.46), channel_id=1, source_target_pairs={{0,6},{1,7},{2,4},{3,5},{4,2},{5,3},{6,0},{7,1},{8,14},{9,15},{10,... | collective-permute-start | bytes 196616 | tf_op jit(solution)/shard_map/ppermute | solution.py:526
  43.3 4.8 %collective-permute-start.14 = (bf16[1024,512]{1,0:T(8,128)(2,1)S(1)}, bf16[1024,512]{1,0:T(8,128)(2,1)S(1)}, u32[]{:S(2)}, u32[]{:S(2)}) collective-permute-start(bf16[1024,512]{1,0:T(8,128)(2,1)S(1)} %bitcast.13), channel_id=1, source_target_pairs={{0,8},{8,0},{16,24},{24,16},{1,9},{9,1},{17,25},{25,17},{2,10},{10... | collective-permute-start | bytes 3145736 | tf_op jit(solution)/shard_map/ppermute | solution.py:420
  48.1 2.7 %collective-permute-start.17 = (bf16[1024,512]{1,0:T(8,128)(2,1)S(1)}, bf16[1024,512]{1,0:T(8,128)(2,1)S(1)}, u32[]{:S(2)}, u32[]{:S(2)}) collective-permute-start(bf16[1024,512]{1,0:T(8,128)(2,1)S(1)} %collective-permute-done.16.refs_4_), channel_id=1, source_target_pairs={{0,8},{8,0},{16,24},{24,16},{1,9},{9,1},{17,25},{25,17},{2,10},{10... | collective-permute-start | bytes 3145736 | tf_op jit(solution)/shard_map/ppermute | solution.py:420
  48.6 6.4 %collective-permute-start.15 = (bf16[64,1024]{1,0:T(8,128)(2,1)S(1)}, bf16[64,1024]{1,0:T(8,128)(2,1)S(1)}, u32[]{:S(2)}, u32[]{:S(2)}) collective-permute-start(bf16[64,1024]{1,0:T(8,128)(2,1)S(1)} %get-tuple-element.50), channel_id=1, source_target_pairs={{0,1},{1,0},{2,3},{3,2},{4,5},{5,4},{6,7},{7,6},{8,9},{9,8},{10,11... | collective-permute-start | bytes 393224 | tf_op jit(solution)/shard_map/ppermute | solution.py:526
  51.3 6.1 %collective-permute-start.18 = (bf16[64,1024]{1,0:T(8,128)(2,1)S(1)}, bf16[64,1024]{1,0:T(8,128)(2,1)S(1)}, u32[]{:S(2)}, u32[]{:S(2)}) collective-permute-start(bf16[64,1024]{1,0:T(8,128)(2,1)S(1)} %get-tuple-element.54), channel_id=1, source_target_pairs={{0,1},{1,0},{2,3},{3,2},{4,5},{5,4},{6,7},{7,6},{8,9},{9,8},{10,11... | collective-permute-start | bytes 393224 | tf_op jit(solution)/shard_map/ppermute | solution.py:526

commit v5 on v4

--- a/solution.py
+++ b/solution.py
@@ -298,14 +298,15 @@
         copy.wait()
 
 
-def join_kernel(near_kept, near_came, far_kept, far_came, attended_ref):
-    width = near_kept.shape[1]
+def join_kernel(place, kept, came, *refs):
+    attended_ref, total_ref, sem = refs[-3:]
+    width = kept.shape[1]
     side = lax.axis_index("dp") // (lax.axis_size("dp") // 2)
-    for place, (kept, came) in enumerate(((near_kept, near_came), (far_kept, far_came))):
-        start = pl.multiple_of((side ^ place) * width, width)
-        attended_ref[:, pl.ds(start, width)] = (
-            kept[...] + came[...].astype(jnp.float32)
-        ).astype(attended_ref.dtype)
+    start = pl.multiple_of((side ^ place) * width, width)
+    total_ref[...] = (kept[...] + came[...].astype(jnp.float32)).astype(total_ref.dtype)
+    copy = pltpu.make_async_copy(total_ref, attended_ref.at[:, pl.ds(start, width)], sem)
+    copy.start()
+    copy.wait()
 
 
 def turn_kernel(members, length_ref, window_ref, sink_ref, *refs):
@@ -557,13 +558,22 @@
     spread([far], far // 2)
     far_kept, far_sent = project(tuple(range(far, dp_size)))
     far_came = from_member(far_sent, 1)
-    attended = pl.pallas_call(
-        join_kernel,
-        out_shape=jax.ShapeDtypeStruct((rows, width * dp_size), jnp.bfloat16),
-        in_specs=[whole_vmem()] * 4,
-        out_specs=whole_vmem(),
-        compiler_params=pltpu.CompilerParams(vmem_limit_bytes=vmem_bytes),
-    )(near_kept, near_came, far_kept, far_came)
+
+    def join(place, kept, came, *held):
+        return pl.pallas_call(
+            functools.partial(join_kernel, place),
+            out_shape=jax.ShapeDtypeStruct((rows, width * dp_size), jnp.bfloat16),
+            in_specs=[whole_vmem()] * 2 + [pl.BlockSpec(memory_space=pl.ANY)] * len(held),
+            out_specs=pl.BlockSpec(memory_space=pl.ANY),
+            input_output_aliases={2: 0} if held else {},
+            scratch_shapes=[
+                pltpu.VMEM(kept.shape, jnp.bfloat16),
+                pltpu.SemaphoreType.DMA,
+            ],
+            compiler_params=pltpu.CompilerParams(vmem_limit_bytes=vmem_bytes),
+        )(kept, came, *held)
+
+    attended = join(1, far_kept, far_came, join(0, near_kept, near_came))
     return (attended, fresh[None])
 
 

time: 58.4 us -> 58.5 us (level)
  waiting for transfers between devices: 19 us -> 18.3 us
  Pallas kernels: 16.3 us -> 16.9 us
    ppermute x5, waiting for transfers between devices: 10.5 us -> 9.79 us  [from_member(): return lax.ppermute(block, 'tensor', route)]
    pallas_call x1 -> x2, Pallas kernels: 0.76 us -> 1.37 us  [join(): pl.pallas_call(functools.partial(join_kernel, place), out_shape=jax.Shape...]
  transfers between devices with their start and end apart: 19 -> 19, of which waited for: 11 -> 11; matrix products, arithmetic and copies ran while one was open for 2% -> 2% of each run, Pallas kernels for 27% -> 28%
where the time goes in v5:
time: 58.5 us; the launch traced here: 58.2 us
  starting transfers between devices  18.7 us (32%)
  waiting for transfers between devices  18.3 us (31%)
  Pallas kernels  16.9 us (29%)
  between operations  2.93 us (5%)
  local copies, waits for them, and re-layouts  1.36 us (2%)
    pallas_call x3, Pallas kernels, run_stage(): pl.pallas_call(functools.partial(stage_kernel, plan, final), out_shape=ou...  12.4 us
    ppermute x5, waiting for transfers between devices, from_member(): return lax.ppermute(block, 'tensor', route)  9.79 us
    ppermute x4, starting transfers between devices, forward(): return lax.ppermute(block, 'tensor', ring_route(1))  8.1 us
    ppermute x5, starting transfers between devices, from_member(): return lax.ppermute(block, 'tensor', route)  5.19 us
    ppermute x6, starting transfers between devices, from_dp(): lax.ppermute(block, 'dp', [(one, one ^ apart) for one in range(dp_size)])  4.07 us
    ppermute x4, waiting for transfers between devices, forward(): return lax.ppermute(block, 'tensor', ring_route(1))  3.56 us
    ppermute x6, waiting for transfers between devices, from_dp(): lax.ppermute(block, 'dp', [(one, one ^ apart) for one in range(dp_size)])  2.59 us
    ppermute x4, waiting for transfers between devices, backward(): return lax.ppermute(block, 'tensor', ring_route(-1))  2.37 us
  transfers between devices with their start and end apart: 19, of which 11 were waited for; matrix products, arithmetic and copies ran while one was open for 2% of the time, Pallas kernels for 28%

profile of v5, /device:TPU:0, one launch (start us, length us, event | category | flops | bytes accessed | tf_op | source)
XLA Modules:
  0.0 58.2 jit_solution(15253129625828860672)
XLA Ops:
  0.7 3.1 %collective-permute-start = (bf16[64,2048]{1,0:T(8,128)(2,1)}, bf16[64,2048]{1,0:T(8,128)(2,1)S(1)}, u32[]{:S(2)}, u32[]{:S(2)}) collective-permute-start(bf16[64,2048]{1,0:T(8,128)(2,1)} %refs_1_.1), channel_id=1, source_target_pairs={{0,2},{2,4},{4,6},{6,7},{7,5},{5,3},{3,1},{1,0},{8,10},{10,12},{12... | collective-permute-start | bytes 786440 | tf_op jit(solution)/shard_map/ppermute | solution.py:415
  3.8 1.9 %shard_map.132.refs_10_.refs_7_ = bf16[512,384]{1,0:T(8,128)(2,1)} custom-call(bf16[512,2048]{1,0:T(8,128)(2,1)} %query_ref.1, bf16[2,512,512]{2,1,0:T(8,128)(2,1)} %keyval_ref.1), custom_call_target="tpu_custom_call" | custom-call | bytes 33554432 | tf_op jit(solution)/shard_map/pallas_call | solution.py:424
  5.7 2.0 %collective-permute-start.5 = (bf16[512,384]{1,0:T(8,128)(2,1)}, bf16[512,384]{1,0:T(8,128)(2,1)S(1)}, u32[]{:S(2)}, u32[]{:S(2)}) collective-permute-start(bf16[512,384]{1,0:T(8,128)(2,1)} %shard_map.132.refs_10_.refs_7_), channel_id=1, source_target_pairs={{0,16},{8,24},{16,0},{24,8},{1,17},{9,25},{17,1},{25,9},{2,18},{10... | collective-permute-start | bytes 1179656 | tf_op jit(solution)/shard_map/ppermute | solution.py:421
  7.8 2.4 %collective-permute-done.refs_5_.refs_2_ = bf16[64,2048]{1,0:T(8,128)(2,1)S(1)} collective-permute-done((bf16[64,2048]{1,0:T(8,128)(2,1)}, bf16[64,2048]{1,0:T(8,128)(2,1)S(1)}, u32[]{:S(2)}, u32[]{:S(2)}) %collective-permute-start) | collective-permute-done | bytes 262176 | tf_op jit(solution)/shard_map/ppermute | solution.py:415
  10.2 1.8 %collective-permute-start.2 = (bf16[64,2048]{1,0:T(8,128)(2,1)S(1)}, bf16[64,2048]{1,0:T(8,128)(2,1)S(1)}, u32[]{:S(2)}, u32[]{:S(2)}) collective-permute-start(bf16[64,2048]{1,0:T(8,128)(2,1)S(1)} %collective-permute-done.refs_5_.refs_2_), channel_id=1, source_target_pairs={{0,2},{2,4},{4,6},{6,7},{7,5},{5,3},{3,1},{1,0},{8,10},{10,12},{12... | collective-permute-start | bytes 786440 | tf_op jit(solution)/shard_map/ppermute | solution.py:415
  14.5 1.3 %constant_dynamic-slice_fusion = bf16[4,1,256,512]{3,2,1,0:T(8,128)(2,1)S(1)} fusion(bf16[4,2,256,512]{3,2,1,0:T(8,128)(2,1)} %bitcast.18, s32[]{:T(128)S(6)} %select_n.17), kind=kLoop, calls=%fused_computation | loop fusion | bytes 2097156 | tf_op jit(solution)/shard_map/jit(dynamic_index_in_dim)/dynamic_slice | solution.py:480
  15.8 0.8 %collective-permute-done.5.refs_12_.refs_9_ = bf16[512,384]{1,0:T(8,128)(2,1)S(1)} collective-permute-done((bf16[512,384]{1,0:T(8,128)(2,1)}, bf16[512,384]{1,0:T(8,128)(2,1)S(1)}, u32[]{:S(2)}, u32[]{:S(2)}) %collective-permute-start.5) | collective-permute-done | bytes 393248 | tf_op jit(solution)/shard_map/ppermute | solution.py:421
  16.6 1.1 %collective-permute-done.2.refs_4_ = bf16[64,2048]{1,0:T(8,128)(2,1)S(1)} collective-permute-done((bf16[64,2048]{1,0:T(8,128)(2,1)S(1)}, bf16[64,2048]{1,0:T(8,128)(2,1)S(1)}, u32[]{:S(2)}, u32[]{:S(2)}) %collective-permute-start.2) | collective-permute-done | bytes 262176 | tf_op jit(solution)/shard_map/ppermute | solution.py:415
  17.7 1.2 %collective-permute-done.4.refs_5_ = bf16[64,2048]{1,0:T(8,128)(2,1)S(1)} collective-permute-done((bf16[64,2048]{1,0:T(8,128)(2,1)S(1)}, bf16[64,2048]{1,0:T(8,128)(2,1)S(1)}, u32[]{:S(2)}, u32[]{:S(2)}) %collective-permute-start.4) | collective-permute-done | bytes 262176 | tf_op jit(solution)/shard_map/ppermute | solution.py:418
  18.9 1.5 %collective-permute-start.14 = (bf16[1024,512]{1,0:T(8,128)(2,1)S(1)}, bf16[1024,512]{1,0:T(8,128)(2,1)S(1)}, u32[]{:S(2)}, u32[]{:S(2)}) collective-permute-start(bf16[1024,512]{1,0:T(8,128)(2,1)S(1)} %bitcast.12), channel_id=1, source_target_pairs={{0,16},{8,24},{16,0},{24,8},{1,17},{9,25},{17,1},{25,9},{2,18},{10... | collective-permute-start | bytes 3145736 | tf_op jit(solution)/shard_map/ppermute | solution.py:421
  20.4 0.5 collective-permute-start.7
  20.9 1.6 %collective-permute-start.3 = (bf16[64,2048]{1,0:T(8,128)(2,1)S(1)}, bf16[64,2048]{1,0:T(8,128)(2,1)S(1)}, u32[]{:S(2)}, u32[]{:S(2)}) collective-permute-start(bf16[64,2048]{1,0:T(8,128)(2,1)S(1)} %collective-permute-done.2.refs_4_), channel_id=1, source_target_pairs={{0,2},{2,4},{4,6},{6,7},{7,5},{5,3},{3,1},{1,0},{8,10},{10,12},{12... | collective-permute-start | bytes 786440 | tf_op jit(solution)/shard_map/ppermute | solution.py:415
  22.5 0.4 collective-permute-start.9
  23.0 6.1 %shard_map.133 = (bf16[128,1280]{1,0:T(8,128)(2,1)S(1)}, bf16[320,128]{1,0:T(8,128)(2,1)S(1)}, f32[80,1280]{1,0:T(8,128)S(1)}) custom-call(s32[8,128]{1,0:T(8,128)S(1)} %get-tuple-element.29.refs_0_, bf16[64,2048]{1,0:T(8,128)(2,1)S(1)} %copy-done.2, bf16[64,2048]{1,0:T(8,128)(2,1)S(1)} %collective-permute-done.refs_5_.refs_2_, ...), custom_call_target="tpu_custom_call" | custom-call | flops 1024 | bytes 1024 | tf_op jit(solution)/shard_map/pallas_call | solution.py:368
  29.2 1.6 %collective-permute-start.8 = (bf16[32,2048]{1,0:T(8,128)(2,1)S(1)}, bf16[32,2048]{1,0:T(8,128)(2,1)S(1)}, u32[]{:S(2)}, u32[]{:S(2)}) collective-permute-start(bf16[32,2048]{1,0:T(8,128)(2,1)S(1)} %slice.6), channel_id=1, source_target_pairs={{0,2},{2,4},{4,6},{6,7},{7,5},{5,3},{3,1},{1,0},{8,10},{10,12},{12... | collective-permute-start | bytes 393224 | tf_op jit(solution)/shard_map/ppermute | solution.py:415
  30.8 0.7 %collective-permute-start.10 = (bf16[32,2048]{1,0:T(8,128)(2,1)S(1)}, bf16[32,2048]{1,0:T(8,128)(2,1)S(1)}, u32[]{:S(2)}, u32[]{:S(2)}) collective-permute-start(bf16[32,2048]{1,0:T(8,128)(2,1)S(1)} %slice.7), channel_id=1, source_target_pairs={{0,1},{2,0},{4,2},{6,4},{7,6},{5,7},{3,5},{1,3},{8,9},{10,8},{12,1... | collective-permute-start | bytes 393224 | tf_op jit(solution)/shard_map/ppermute | solution.py:418
  31.5 3.4 %shard_map.134 = (bf16[128,1792]{1,0:T(8,128)(2,1)S(1)}, bf16[448,128]{1,0:T(8,128)(2,1)S(1)}, f32[80,1792]{1,0:T(8,128)S(1)}) custom-call(s32[8,128]{1,0:T(8,128)S(1)} %get-tuple-element.29.refs_0_, bf16[64,2048]{1,0:T(8,128)(2,1)S(1)} %collective-permute-done.3.refs_1_, bf16[64,2048]{1,0:T(8,128)(2,1)S(1)} %collective-permute-done.9.refs_2_, ...), custom_call_target="tpu_custom_call" | custom-call | flops 1024 | bytes 1024 | tf_op jit(solution)/shard_map/pallas_call | solution.py:368
  34.9 1.1 %collective-permute-done.10.refs_2_ = bf16[32,2048]{1,0:T(8,128)(2,1)S(1)} collective-permute-done((bf16[32,2048]{1,0:T(8,128)(2,1)S(1)}, bf16[32,2048]{1,0:T(8,128)(2,1)S(1)}, u32[]{:S(2)}, u32[]{:S(2)}) %collective-permute-start.10) | collective-permute-done | bytes 131104 | tf_op jit(solution)/shard_map/ppermute | solution.py:418
  36.0 2.9 %shard_map.135 = (bf16[128,256]{1,0:T(8,128)(2,1)S(1)}, bf16[128,256]{1,0:T(8,128)(2,1)S(1)}, bf16[128,256]{1,0:T(8,128)(2,1)S(1)}, bf16[128,256]{1,0:T(8,128)(2,1)S(1)}, bf16[512,128]{1,0:T(8,128)(2,1)}) custom-call(s32[8,128]{1,0:T(8,128)S(1)} %get-tuple-element.29.refs_0_, bf16[32,2048]{1,0:T(8,128)(2,1)S(1)} %collective-permute-done.8.refs_1_, ...), custom_call_target="tpu_custom_call" | custom-call | flops 1024 | bytes 1024 | tf_op jit(solution)/shard_map/pallas_call | solution.py:368
  39.0 1.6 %collective-permute-start.11 = (bf16[128,256]{1,0:T(8,128)(2,1)S(1)}, bf16[128,256]{1,0:T(8,128)(2,1)S(1)}, u32[]{:S(2)}, u32[]{:S(2)}) collective-permute-start(bf16[128,256]{1,0:T(8,128)(2,1)S(1)} %get-tuple-element.44), channel_id=1, source_target_pairs={{0,2},{1,3},{2,0},{3,1},{4,6},{5,7},{6,4},{7,5},{8,10},{9,11},{10,... | collective-permute-start | bytes 196616 | tf_op jit(solution)/shard_map/ppermute | solution.py:527
  40.5 1.4 %collective-permute-start.12 = (bf16[128,256]{1,0:T(8,128)(2,1)S(1)}, bf16[128,256]{1,0:T(8,128)(2,1)S(1)}, u32[]{:S(2)}, u32[]{:S(2)}) collective-permute-start(bf16[128,256]{1,0:T(8,128)(2,1)S(1)} %get-tuple-element.45), channel_id=1, source_target_pairs={{0,4},{1,5},{2,6},{3,7},{4,0},{5,1},{6,2},{7,3},{8,12},{9,13},{10,... | collective-permute-start | bytes 196616 | tf_op jit(solution)/shard_map/ppermute | solution.py:527
  41.9 1.4 %collective-permute-start.13 = (bf16[128,256]{1,0:T(8,128)(2,1)S(1)}, bf16[128,256]{1,0:T(8,128)(2,1)S(1)}, u32[]{:S(2)}, u32[]{:S(2)}) collective-permute-start(bf16[128,256]{1,0:T(8,128)(2,1)S(1)} %get-tuple-element.46), channel_id=1, source_target_pairs={{0,6},{1,7},{2,4},{3,5},{4,2},{5,3},{6,0},{7,1},{8,14},{9,15},{10,... | collective-permute-start | bytes 196616 | tf_op jit(solution)/shard_map/ppermute | solution.py:527
  43.7 3.4 %collective-permute-done.12.refs_2_ = bf16[128,256]{1,0:T(8,128)(2,1)S(1)} collective-permute-done((bf16[128,256]{1,0:T(8,128)(2,1)S(1)}, bf16[128,256]{1,0:T(8,128)(2,1)S(1)}, u32[]{:S(2)}, u32[]{:S(2)}) %collective-permute-start.12) | collective-permute-done | bytes 65568 | tf_op jit(solution)/shard_map/ppermute | solution.py:527
  47.1 1.0 %collective-permute-done.13.refs_3_ = bf16[128,256]{1,0:T(8,128)(2,1)S(1)} collective-permute-done((bf16[128,256]{1,0:T(8,128)(2,1)S(1)}, bf16[128,256]{1,0:T(8,128)(2,1)S(1)}, u32[]{:S(2)}, u32[]{:S(2)}) %collective-permute-start.13) | collective-permute-done | bytes 65568 | tf_op jit(solution)/shard_map/ppermute | solution.py:527
  48.1 0.5 shard_map.137
  48.6 0.4 collective-permute-start.18
  49.0 1.7 %collective-permute-done.15.refs_5_ = bf16[1024,512]{1,0:T(8,128)(2,1)S(1)} collective-permute-done((bf16[1024,512]{1,0:T(8,128)(2,1)S(1)}, bf16[1024,512]{1,0:T(8,128)(2,1)S(1)}, u32[]{:S(2)}, u32[]{:S(2)}) %collective-permute-start.15) | collective-permute-done | bytes 1048608 | tf_op jit(solution)/shard_map/ppermute | solution.py:421
  50.8 0.5 shard_map.136
  51.7 3.3 %collective-permute-done.18.came = bf16[64,1024]{1,0:T(8,128)(2,1)S(1)} collective-permute-done((bf16[64,1024]{1,0:T(8,128)(2,1)S(1)}, bf16[64,1024]{1,0:T(8,128)(2,1)S(1)}, u32[]{:S(2)}, u32[]{:S(2)}) %collective-permute-start.18) | collective-permute-done | bytes 131104 | tf_op jit(solution)/shard_map/ppermute | solution.py:527
  55.0 0.7 %shard_map.138.refs_0_ = bf16[64,2048]{1,0:T(8,128)(2,1)} custom-call(f32[64,1024]{1,0:T(8,128)S(1)} %get-tuple-element.53.kept, bf16[64,1024]{1,0:T(8,128)(2,1)S(1)} %collective-permute-done.18.came), custom_call_target="tpu_custom_call" | custom-call | tf_op jit(solution)/shard_map/pallas_call | solution.py:563
  55.7 1.7 %collective-permute-done.16.came = bf16[64,1024]{1,0:T(8,128)(2,1)S(1)} collective-permute-done((bf16[64,1024]{1,0:T(8,128)(2,1)S(1)}, bf16[64,1024]{1,0:T(8,128)(2,1)S(1)}, u32[]{:S(2)}, u32[]{:S(2)}) %collective-permute-start.16) | collective-permute-done | bytes 131104 | tf_op jit(solution)/shard_map/ppermute | solution.py:527
  57.4 0.7 %shard_map.139 = bf16[64,2048]{1,0:T(8,128)(2,1)} custom-call(f32[64,1024]{1,0:T(8,128)S(1)} %get-tuple-element.50.kept, bf16[64,1024]{1,0:T(8,128)(2,1)S(1)} %collective-permute-done.16.came, bf16[64,2048]{1,0:T(8,128)(2,1)} %shard_map.138.refs_0_), custom_call_target="tpu_custom_call", output_to_operand_aliasing={{}: (2, {})} | custom-call | tf_op jit(solution)/shard_map/pallas_call | solution.py:563
  (32 shorter events, 1.3 us)
Async XLA Ops:
  0.6 13.5 %copy-start.3 = (f32[32,64]{1,0:T(8,128)S(1)}, f32[32,64]{1,0:T(8,128)}, u32[]{:S(2)}) copy-start(f32[32,64]{1,0:T(8,128)} %constant.33.clone.refs_4_) | copy-start | bytes 24580
  0.6 13.5 %copy-start = (bf16[1,2048,128]{2,1,0:T(8,128)(2,1)S(1)}, bf16[1,2048,128]{2,1,0:T(8,128)(2,1)}, u32[]{:S(2)}) copy-start(bf16[1,2048,128]{2,1,0:T(8,128)(2,1)} %refs_0_.1) | copy-start | bytes 1572868
  0.7 13.5 %copy-start.4 = (bf16[2048]{0:T(1024)(128)(2,1)S(1)}, bf16[2048]{0:T(1024)(128)(2,1)}, u32[]{:S(2)}) copy-start(bf16[2048]{0:T(1024)(128)(2,1)} %param.13) | copy-start | bytes 12292
  0.7 13.5 %copy-start.5 = (f32[64]{0:T(128)S(1)}, f32[64]{0:T(128)}, u32[]{:S(2)}) copy-start(f32[64]{0:T(128)} %param.16) | copy-start | bytes 772
  0.7 13.5 %copy-start.6 = (f32[64]{0:T(128)S(1)}, f32[64]{0:T(128)}, u32[]{:S(2)}) copy-start(f32[64]{0:T(128)} %param.17) | copy-start | bytes 772
  0.7 9.5 %collective-permute-start = (bf16[64,2048]{1,0:T(8,128)(2,1)}, bf16[64,2048]{1,0:T(8,128)(2,1)S(1)}, u32[]{:S(2)}, u32[]{:S(2)}) collective-permute-start(bf16[64,2048]{1,0:T(8,128)(2,1)} %refs_1_.1), channel_id=1, source_target_pairs={{0,2},{2,4},{4,6},{6,7},{7,5},{5,3},{3,1},{1,0},{8,10},{10,12},{12... | collective-permute-start | bytes 786440 | tf_op jit(solution)/shard_map/ppermute | solution.py:415
  3.8 8.3 %collective-permute-start.1 = (bf16[64,2048]{1,0:T(8,128)(2,1)}, bf16[64,2048]{1,0:T(8,128)(2,1)S(1)}, u32[]{:S(2)}, u32[]{:S(2)}) collective-permute-start(bf16[64,2048]{1,0:T(8,128)(2,1)} %refs_1_.1), channel_id=1, source_target_pairs={{0,1},{2,0},{4,2},{6,4},{7,6},{5,7},{3,5},{1,3},{8,9},{10,8},{12,1... | collective-permute-start | bytes 786440 | tf_op jit(solution)/shard_map/ppermute | solution.py:418
  5.7 14.7 %copy-start.1 = (bf16[512,384]{1,0:T(8,128)(2,1)S(1)}, bf16[512,384]{1,0:T(8,128)(2,1)}, u32[]{:S(2)}) copy-start(bf16[512,384]{1,0:T(8,128)(2,1)} %shard_map.132.refs_10_.refs_7_) | copy-start | bytes 1179652
  5.7 17.3 %copy-start.2 = (bf16[64,2048]{1,0:T(8,128)(2,1)S(1)}, bf16[64,2048]{1,0:T(8,128)(2,1)}, u32[]{:S(2)}) copy-start(bf16[64,2048]{1,0:T(8,128)(2,1)} %refs_1_.1) | copy-start | bytes 786436
  5.7 10.9 %collective-permute-start.5 = (bf16[512,384]{1,0:T(8,128)(2,1)}, bf16[512,384]{1,0:T(8,128)(2,1)S(1)}, u32[]{:S(2)}, u32[]{:S(2)}) collective-permute-start(bf16[512,384]{1,0:T(8,128)(2,1)} %shard_map.132.refs_10_.refs_7_), channel_id=1, source_target_pairs={{0,16},{8,24},{16,0},{24,8},{1,17},{9,25},{17,1},{25,9},{2,18},{10... | collective-permute-start | bytes 1179656 | tf_op jit(solution)/shard_map/ppermute | solution.py:421
  10.2 7.5 %collective-permute-start.2 = (bf16[64,2048]{1,0:T(8,128)(2,1)S(1)}, bf16[64,2048]{1,0:T(8,128)(2,1)S(1)}, u32[]{:S(2)}, u32[]{:S(2)}) collective-permute-start(bf16[64,2048]{1,0:T(8,128)(2,1)S(1)} %collective-permute-done.refs_5_.refs_2_), channel_id=1, source_target_pairs={{0,2},{2,4},{4,6},{6,7},{7,5},{5,3},{3,1},{1,0},{8,10},{10,12},{12... | collective-permute-start | bytes 786440 | tf_op jit(solution)/shard_map/ppermute | solution.py:415
  12.0 6.9 %collective-permute-start.4 = (bf16[64,2048]{1,0:T(8,128)(2,1)S(1)}, bf16[64,2048]{1,0:T(8,128)(2,1)S(1)}, u32[]{:S(2)}, u32[]{:S(2)}) collective-permute-start(bf16[64,2048]{1,0:T(8,128)(2,1)S(1)} %collective-permute-done.1.refs_6_.refs_3_), channel_id=1, source_target_pairs={{0,1},{2,0},{4,2},{6,4},{7,6},{5,7},{3,5},{1,3},{8,9},{10,8},{12,1... | collective-permute-start | bytes 786440 | tf_op jit(solution)/shard_map/ppermute | solution.py:418
  18.9 29.2 %collective-permute-start.14 = (bf16[1024,512]{1,0:T(8,128)(2,1)S(1)}, bf16[1024,512]{1,0:T(8,128)(2,1)S(1)}, u32[]{:S(2)}, u32[]{:S(2)}) collective-permute-start(bf16[1024,512]{1,0:T(8,128)(2,1)S(1)} %bitcast.12), channel_id=1, source_target_pairs={{0,16},{8,24},{16,0},{24,8},{1,17},{9,25},{17,1},{25,9},{2,18},{10... | collective-permute-start | bytes 3145736 | tf_op jit(solution)/shard_map/ppermute | solution.py:421
  20.4 2.5 %collective-permute-start.6 = (bf16[512,384]{1,0:T(8,128)(2,1)S(1)}, bf16[512,384]{1,0:T(8,128)(2,1)S(1)}, u32[]{:S(2)}, u32[]{:S(2)}) collective-permute-start(bf16[512,384]{1,0:T(8,128)(2,1)S(1)} %copy-done.1), channel_id=1, source_target_pairs={{0,8},{8,0},{16,24},{24,16},{1,9},{9,1},{17,25},{25,17},{2,10},{10... | collective-permute-start | bytes 1179656 | tf_op jit(solution)/shard_map/ppermute | solution.py:421
  20.4 2.5 %collective-permute-start.7 = (bf16[512,384]{1,0:T(8,128)(2,1)S(1)}, bf16[512,384]{1,0:T(8,128)(2,1)S(1)}, u32[]{:S(2)}, u32[]{:S(2)}) collective-permute-start(bf16[512,384]{1,0:T(8,128)(2,1)S(1)} %collective-permute-done.5.refs_12_.refs_9_), channel_id=1, source_target_pairs={{0,8},{8,0},{16,24},{24,16},{1,9},{9,1},{17,25},{25,17},{2,10},{10... | collective-permute-start | bytes 1179656 | tf_op jit(solution)/shard_map/ppermute | solution.py:421
  20.9 8.2 %collective-permute-start.3 = (bf16[64,2048]{1,0:T(8,128)(2,1)S(1)}, bf16[64,2048]{1,0:T(8,128)(2,1)S(1)}, u32[]{:S(2)}, u32[]{:S(2)}) collective-permute-start(bf16[64,2048]{1,0:T(8,128)(2,1)S(1)} %collective-permute-done.2.refs_4_), channel_id=1, source_target_pairs={{0,2},{2,4},{4,6},{6,7},{7,5},{5,3},{3,1},{1,0},{8,10},{10,12},{12... | collective-permute-start | bytes 786440 | tf_op jit(solution)/shard_map/ppermute | solution.py:415
  22.5 8.3 %collective-permute-start.9 = (bf16[64,2048]{1,0:T(8,128)(2,1)S(1)}, bf16[64,2048]{1,0:T(8,128)(2,1)S(1)}, u32[]{:S(2)}, u32[]{:S(2)}) collective-permute-start(bf16[64,2048]{1,0:T(8,128)(2,1)S(1)} %collective-permute-done.4.refs_5_), channel_id=1, source_target_pairs={{0,1},{2,0},{4,2},{6,4},{7,6},{5,7},{3,5},{1,3},{8,9},{10,8},{12,1... | collective-permute-start | bytes 786440 | tf_op jit(solution)/shard_map/ppermute | solution.py:418
  29.2 5.7 %collective-permute-start.8 = (bf16[32,2048]{1,0:T(8,128)(2,1)S(1)}, bf16[32,2048]{1,0:T(8,128)(2,1)S(1)}, u32[]{:S(2)}, u32[]{:S(2)}) collective-permute-start(bf16[32,2048]{1,0:T(8,128)(2,1)S(1)} %slice.6), channel_id=1, source_target_pairs={{0,2},{2,4},{4,6},{6,7},{7,5},{5,3},{3,1},{1,0},{8,10},{10,12},{12... | collective-permute-start | bytes 393224 | tf_op jit(solution)/shard_map/ppermute | solution.py:415
  30.8 5.2 %collective-permute-start.10 = (bf16[32,2048]{1,0:T(8,128)(2,1)S(1)}, bf16[32,2048]{1,0:T(8,128)(2,1)S(1)}, u32[]{:S(2)}, u32[]{:S(2)}) collective-permute-start(bf16[32,2048]{1,0:T(8,128)(2,1)S(1)} %slice.7), channel_id=1, source_target_pairs={{0,1},{2,0},{4,2},{6,4},{7,6},{5,7},{3,5},{1,3},{8,9},{10,8},{12,1... | collective-permute-start | bytes 393224 | tf_op jit(solution)/shard_map/ppermute | solution.py:418
  39.0 4.7 %collective-permute-start.11 = (bf16[128,256]{1,0:T(8,128)(2,1)S(1)}, bf16[128,256]{1,0:T(8,128)(2,1)S(1)}, u32[]{:S(2)}, u32[]{:S(2)}) collective-permute-start(bf16[128,256]{1,0:T(8,128)(2,1)S(1)} %get-tuple-element.44), channel_id=1, source_target_pairs={{0,2},{1,3},{2,0},{3,1},{4,6},{5,7},{6,4},{7,5},{8,10},{9,11},{10,... | collective-permute-start | bytes 196616 | tf_op jit(solution)/shard_map/ppermute | solution.py:527
  40.5 6.6 %collective-permute-start.12 = (bf16[128,256]{1,0:T(8,128)(2,1)S(1)}, bf16[128,256]{1,0:T(8,128)(2,1)S(1)}, u32[]{:S(2)}, u32[]{:S(2)}) collective-permute-start(bf16[128,256]{1,0:T(8,128)(2,1)S(1)} %get-tuple-element.45), channel_id=1, source_target_pairs={{0,4},{1,5},{2,6},{3,7},{4,0},{5,1},{6,2},{7,3},{8,12},{9,13},{10,... | collective-permute-start | bytes 196616 | tf_op jit(solution)/shard_map/ppermute | solution.py:527
  41.9 6.2 %collective-permute-start.13 = (bf16[128,256]{1,0:T(8,128)(2,1)S(1)}, bf16[128,256]{1,0:T(8,128)(2,1)S(1)}, u32[]{:S(2)}, u32[]{:S(2)}) collective-permute-start(bf16[128,256]{1,0:T(8,128)(2,1)S(1)} %get-tuple-element.46), channel_id=1, source_target_pairs={{0,6},{1,7},{2,4},{3,5},{4,2},{5,3},{6,0},{7,1},{8,14},{9,15},{10,... | collective-permute-start | bytes 196616 | tf_op jit(solution)/shard_map/ppermute | solution.py:527
  43.3 4.8 %collective-permute-start.17 = (bf16[1024,512]{1,0:T(8,128)(2,1)S(1)}, bf16[1024,512]{1,0:T(8,128)(2,1)S(1)}, u32[]{:S(2)}, u32[]{:S(2)}) collective-permute-start(bf16[1024,512]{1,0:T(8,128)(2,1)S(1)} %bitcast.13), channel_id=1, source_target_pairs={{0,8},{8,0},{16,24},{24,16},{1,9},{9,1},{17,25},{25,17},{2,10},{10... | collective-permute-start | bytes 3145736 | tf_op jit(solution)/shard_map/ppermute | solution.py:421
  48.1 2.7 %collective-permute-start.15 = (bf16[1024,512]{1,0:T(8,128)(2,1)S(1)}, bf16[1024,512]{1,0:T(8,128)(2,1)S(1)}, u32[]{:S(2)}, u32[]{:S(2)}) collective-permute-start(bf16[1024,512]{1,0:T(8,128)(2,1)S(1)} %collective-permute-done.14.refs_4_), channel_id=1, source_target_pairs={{0,8},{8,0},{16,24},{24,16},{1,9},{9,1},{17,25},{25,17},{2,10},{10... | collective-permute-start | bytes 3145736 | tf_op jit(solution)/shard_map/ppermute | solution.py:421
  48.6 6.4 %collective-permute-start.18 = (bf16[64,1024]{1,0:T(8,128)(2,1)S(1)}, bf16[64,1024]{1,0:T(8,128)(2,1)S(1)}, u32[]{:S(2)}, u32[]{:S(2)}) collective-permute-start(bf16[64,1024]{1,0:T(8,128)(2,1)S(1)} %get-tuple-element.54), channel_id=1, source_target_pairs={{0,1},{1,0},{2,3},{3,2},{4,5},{5,4},{6,7},{7,6},{8,9},{9,8},{10,11... | collective-permute-start | bytes 393224 | tf_op jit(solution)/shard_map/ppermute | solution.py:527
  51.3 6.1 %collective-permute-start.16 = (bf16[64,1024]{1,0:T(8,128)(2,1)S(1)}, bf16[64,1024]{1,0:T(8,128)(2,1)S(1)}, u32[]{:S(2)}, u32[]{:S(2)}) collective-permute-start(bf16[64,1024]{1,0:T(8,128)(2,1)S(1)} %get-tuple-element.51), channel_id=1, source_target_pairs={{0,1},{1,0},{2,3},{3,2},{4,5},{5,4},{6,7},{7,6},{8,9},{9,8},{10,11... | collective-permute-start | bytes 393224 | tf_op jit(solution)/shard_map/ppermute | solution.py:527

commit v6 on v4

--- a/solution.py
+++ b/solution.py
@@ -298,14 +298,21 @@
         copy.wait()
 
 
-def join_kernel(near_kept, near_came, far_kept, far_came, attended_ref):
+def join_kernel(near_kept, near_came, far_kept, far_came, attended_ref, total_ref, sems):
     width = near_kept.shape[1]
     side = lax.axis_index("dp") // (lax.axis_size("dp") // 2)
+    copies = []
     for place, (kept, came) in enumerate(((near_kept, near_came), (far_kept, far_came))):
         start = pl.multiple_of((side ^ place) * width, width)
-        attended_ref[:, pl.ds(start, width)] = (
-            kept[...] + came[...].astype(jnp.float32)
-        ).astype(attended_ref.dtype)
+        total_ref[place] = (kept[...] + came[...].astype(jnp.float32)).astype(total_ref.dtype)
+        copies.append(
+            pltpu.make_async_copy(
+                total_ref.at[place], attended_ref.at[:, pl.ds(start, width)], sems.at[place]
+            )
+        )
+        copies[place].start()
+    for copy in copies:
+        copy.wait()
 
 
 def turn_kernel(members, length_ref, window_ref, sink_ref, *refs):
@@ -561,7 +568,11 @@
         join_kernel,
         out_shape=jax.ShapeDtypeStruct((rows, width * dp_size), jnp.bfloat16),
         in_specs=[whole_vmem()] * 4,
-        out_specs=whole_vmem(),
+        out_specs=pl.BlockSpec(memory_space=pl.ANY),
+        scratch_shapes=[
+            pltpu.VMEM((2, *near_kept.shape), jnp.bfloat16),
+            pltpu.SemaphoreType.DMA((2,)),
+        ],
         compiler_params=pltpu.CompilerParams(vmem_limit_bytes=vmem_bytes),
     )(near_kept, near_came, far_kept, far_came)
     return (attended, fresh[None])

time: 58.4 us -> 58.5 us (level)
  no operation moved by 1% of the time
where the time goes in v6:
time: 58.5 us; the launch traced here: 58.3 us
  waiting for transfers between devices  19 us (32%)
  starting transfers between devices  18.7 us (32%)
  Pallas kernels  16.3 us (28%)
  between operations  2.92 us (5%)
  local copies, waits for them, and re-layouts  1.36 us (2%)
    pallas_call x3, Pallas kernels, run_stage(): pl.pallas_call(functools.partial(stage_kernel, plan, final), out_shape=ou...  12.4 us
    ppermute x5, waiting for transfers between devices, from_member(): return lax.ppermute(block, 'tensor', route)  10.5 us
    ppermute x4, starting transfers between devices, forward(): return lax.ppermute(block, 'tensor', ring_route(1))  8.1 us
    ppermute x5, starting transfers between devices, from_member(): return lax.ppermute(block, 'tensor', route)  5.19 us
    ppermute x6, starting transfers between devices, from_dp(): lax.ppermute(block, 'dp', [(one, one ^ apart) for one in range(dp_size)])  4.07 us
    ppermute x4, waiting for transfers between devices, forward(): return lax.ppermute(block, 'tensor', ring_route(1))  3.56 us
    ppermute x6, waiting for transfers between devices, from_dp(): lax.ppermute(block, 'dp', [(one, one ^ apart) for one in range(dp_size)])  2.59 us
    ppermute x4, waiting for transfers between devices, backward(): return lax.ppermute(block, 'tensor', ring_route(-1))  2.37 us
  transfers between devices with their start and end apart: 19, of which 11 were waited for; matrix products, arithmetic and copies ran while one was open for 2% of the time, Pallas kernels for 27%

profile of v6, /device:TPU:0, one launch (start us, length us, event | category | flops | bytes accessed | tf_op | source)
XLA Modules:
  0.0 58.3 jit_solution(9521556252707566591)
XLA Ops:
  0.7 3.1 %collective-permute-start = (bf16[64,2048]{1,0:T(8,128)(2,1)}, bf16[64,2048]{1,0:T(8,128)(2,1)S(1)}, u32[]{:S(2)}, u32[]{:S(2)}) collective-permute-start(bf16[64,2048]{1,0:T(8,128)(2,1)} %refs_1_.1), channel_id=1, source_target_pairs={{0,2},{2,4},{4,6},{6,7},{7,5},{5,3},{3,1},{1,0},{8,10},{10,12},{12... | collective-permute-start | bytes 786440 | tf_op jit(solution)/shard_map/ppermute | solution.py:421
  3.8 1.9 %shard_map.132.refs_10_.refs_7_ = bf16[512,384]{1,0:T(8,128)(2,1)} custom-call(bf16[512,2048]{1,0:T(8,128)(2,1)} %query_ref.1, bf16[2,512,512]{2,1,0:T(8,128)(2,1)} %keyval_ref.1), custom_call_target="tpu_custom_call" | custom-call | bytes 33554432 | tf_op jit(solution)/shard_map/pallas_call | solution.py:430
  5.7 2.0 %collective-permute-start.5 = (bf16[512,384]{1,0:T(8,128)(2,1)}, bf16[512,384]{1,0:T(8,128)(2,1)S(1)}, u32[]{:S(2)}, u32[]{:S(2)}) collective-permute-start(bf16[512,384]{1,0:T(8,128)(2,1)} %shard_map.132.refs_10_.refs_7_), channel_id=1, source_target_pairs={{0,16},{8,24},{16,0},{24,8},{1,17},{9,25},{17,1},{25,9},{2,18},{10... | collective-permute-start | bytes 1179656 | tf_op jit(solution)/shard_map/ppermute | solution.py:427
  7.8 2.4 %collective-permute-done.refs_5_.refs_2_ = bf16[64,2048]{1,0:T(8,128)(2,1)S(1)} collective-permute-done((bf16[64,2048]{1,0:T(8,128)(2,1)}, bf16[64,2048]{1,0:T(8,128)(2,1)S(1)}, u32[]{:S(2)}, u32[]{:S(2)}) %collective-permute-start) | collective-permute-done | bytes 262176 | tf_op jit(solution)/shard_map/ppermute | solution.py:421
  10.2 1.8 %collective-permute-start.2 = (bf16[64,2048]{1,0:T(8,128)(2,1)S(1)}, bf16[64,2048]{1,0:T(8,128)(2,1)S(1)}, u32[]{:S(2)}, u32[]{:S(2)}) collective-permute-start(bf16[64,2048]{1,0:T(8,128)(2,1)S(1)} %collective-permute-done.refs_5_.refs_2_), channel_id=1, source_target_pairs={{0,2},{2,4},{4,6},{6,7},{7,5},{5,3},{3,1},{1,0},{8,10},{10,12},{12... | collective-permute-start | bytes 786440 | tf_op jit(solution)/shard_map/ppermute | solution.py:421
  14.5 1.3 %constant_dynamic-slice_fusion = bf16[4,1,256,512]{3,2,1,0:T(8,128)(2,1)S(1)} fusion(bf16[4,2,256,512]{3,2,1,0:T(8,128)(2,1)} %bitcast.18, s32[]{:T(128)S(6)} %select_n.17), kind=kLoop, calls=%fused_computation | loop fusion | bytes 2097156 | tf_op jit(solution)/shard_map/jit(dynamic_index_in_dim)/dynamic_slice | solution.py:486
  15.8 0.8 %collective-permute-done.5.refs_12_.refs_9_ = bf16[512,384]{1,0:T(8,128)(2,1)S(1)} collective-permute-done((bf16[512,384]{1,0:T(8,128)(2,1)}, bf16[512,384]{1,0:T(8,128)(2,1)S(1)}, u32[]{:S(2)}, u32[]{:S(2)}) %collective-permute-start.5) | collective-permute-done | bytes 393248 | tf_op jit(solution)/shard_map/ppermute | solution.py:427
  16.6 1.1 %collective-permute-done.2.refs_4_ = bf16[64,2048]{1,0:T(8,128)(2,1)S(1)} collective-permute-done((bf16[64,2048]{1,0:T(8,128)(2,1)S(1)}, bf16[64,2048]{1,0:T(8,128)(2,1)S(1)}, u32[]{:S(2)}, u32[]{:S(2)}) %collective-permute-start.2) | collective-permute-done | bytes 262176 | tf_op jit(solution)/shard_map/ppermute | solution.py:421
  17.7 1.2 %collective-permute-done.4.refs_5_ = bf16[64,2048]{1,0:T(8,128)(2,1)S(1)} collective-permute-done((bf16[64,2048]{1,0:T(8,128)(2,1)S(1)}, bf16[64,2048]{1,0:T(8,128)(2,1)S(1)}, u32[]{:S(2)}, u32[]{:S(2)}) %collective-permute-start.4) | collective-permute-done | bytes 262176 | tf_op jit(solution)/shard_map/ppermute | solution.py:424
  18.9 1.5 %collective-permute-start.16 = (bf16[1024,512]{1,0:T(8,128)(2,1)S(1)}, bf16[1024,512]{1,0:T(8,128)(2,1)S(1)}, u32[]{:S(2)}, u32[]{:S(2)}) collective-permute-start(bf16[1024,512]{1,0:T(8,128)(2,1)S(1)} %bitcast.12), channel_id=1, source_target_pairs={{0,16},{8,24},{16,0},{24,8},{1,17},{9,25},{17,1},{25,9},{2,18},{10... | collective-permute-start | bytes 3145736 | tf_op jit(solution)/shard_map/ppermute | solution.py:427
  20.4 0.5 collective-permute-start.7
  20.9 1.6 %collective-permute-start.3 = (bf16[64,2048]{1,0:T(8,128)(2,1)S(1)}, bf16[64,2048]{1,0:T(8,128)(2,1)S(1)}, u32[]{:S(2)}, u32[]{:S(2)}) collective-permute-start(bf16[64,2048]{1,0:T(8,128)(2,1)S(1)} %collective-permute-done.2.refs_4_), channel_id=1, source_target_pairs={{0,2},{2,4},{4,6},{6,7},{7,5},{5,3},{3,1},{1,0},{8,10},{10,12},{12... | collective-permute-start | bytes 786440 | tf_op jit(solution)/shard_map/ppermute | solution.py:421
  22.5 0.4 collective-permute-start.9
  23.0 6.1 %shard_map.133 = (bf16[128,1280]{1,0:T(8,128)(2,1)S(1)}, bf16[320,128]{1,0:T(8,128)(2,1)S(1)}, f32[80,1280]{1,0:T(8,128)S(1)}) custom-call(s32[8,128]{1,0:T(8,128)S(1)} %get-tuple-element.29.refs_0_, bf16[64,2048]{1,0:T(8,128)(2,1)S(1)} %copy-done.2, bf16[64,2048]{1,0:T(8,128)(2,1)S(1)} %collective-permute-done.refs_5_.refs_2_, ...), custom_call_target="tpu_custom_call" | custom-call | flops 1024 | bytes 1024 | tf_op jit(solution)/shard_map/pallas_call | solution.py:374
  29.2 1.6 %collective-permute-start.8 = (bf16[32,2048]{1,0:T(8,128)(2,1)S(1)}, bf16[32,2048]{1,0:T(8,128)(2,1)S(1)}, u32[]{:S(2)}, u32[]{:S(2)}) collective-permute-start(bf16[32,2048]{1,0:T(8,128)(2,1)S(1)} %slice.6), channel_id=1, source_target_pairs={{0,2},{2,4},{4,6},{6,7},{7,5},{5,3},{3,1},{1,0},{8,10},{10,12},{12... | collective-permute-start | bytes 393224 | tf_op jit(solution)/shard_map/ppermute | solution.py:421
  30.8 0.7 %collective-permute-start.10 = (bf16[32,2048]{1,0:T(8,128)(2,1)S(1)}, bf16[32,2048]{1,0:T(8,128)(2,1)S(1)}, u32[]{:S(2)}, u32[]{:S(2)}) collective-permute-start(bf16[32,2048]{1,0:T(8,128)(2,1)S(1)} %slice.7), channel_id=1, source_target_pairs={{0,1},{2,0},{4,2},{6,4},{7,6},{5,7},{3,5},{1,3},{8,9},{10,8},{12,1... | collective-permute-start | bytes 393224 | tf_op jit(solution)/shard_map/ppermute | solution.py:424
  31.5 3.4 %shard_map.134 = (bf16[128,1792]{1,0:T(8,128)(2,1)S(1)}, bf16[448,128]{1,0:T(8,128)(2,1)S(1)}, f32[80,1792]{1,0:T(8,128)S(1)}) custom-call(s32[8,128]{1,0:T(8,128)S(1)} %get-tuple-element.29.refs_0_, bf16[64,2048]{1,0:T(8,128)(2,1)S(1)} %collective-permute-done.3.refs_1_, bf16[64,2048]{1,0:T(8,128)(2,1)S(1)} %collective-permute-done.9.refs_2_, ...), custom_call_target="tpu_custom_call" | custom-call | flops 1024 | bytes 1024 | tf_op jit(solution)/shard_map/pallas_call | solution.py:374
  34.9 1.1 %collective-permute-done.10.refs_2_ = bf16[32,2048]{1,0:T(8,128)(2,1)S(1)} collective-permute-done((bf16[32,2048]{1,0:T(8,128)(2,1)S(1)}, bf16[32,2048]{1,0:T(8,128)(2,1)S(1)}, u32[]{:S(2)}, u32[]{:S(2)}) %collective-permute-start.10) | collective-permute-done | bytes 131104 | tf_op jit(solution)/shard_map/ppermute | solution.py:424
  36.0 2.9 %shard_map.135 = (bf16[128,256]{1,0:T(8,128)(2,1)S(1)}, bf16[128,256]{1,0:T(8,128)(2,1)S(1)}, bf16[128,256]{1,0:T(8,128)(2,1)S(1)}, bf16[128,256]{1,0:T(8,128)(2,1)S(1)}, bf16[512,128]{1,0:T(8,128)(2,1)}) custom-call(s32[8,128]{1,0:T(8,128)S(1)} %get-tuple-element.29.refs_0_, bf16[32,2048]{1,0:T(8,128)(2,1)S(1)} %collective-permute-done.8.refs_1_, ...), custom_call_target="tpu_custom_call" | custom-call | flops 1024 | bytes 1024 | tf_op jit(solution)/shard_map/pallas_call | solution.py:374
  39.0 1.6 %collective-permute-start.11 = (bf16[128,256]{1,0:T(8,128)(2,1)S(1)}, bf16[128,256]{1,0:T(8,128)(2,1)S(1)}, u32[]{:S(2)}, u32[]{:S(2)}) collective-permute-start(bf16[128,256]{1,0:T(8,128)(2,1)S(1)} %get-tuple-element.44), channel_id=1, source_target_pairs={{0,2},{1,3},{2,0},{3,1},{4,6},{5,7},{6,4},{7,5},{8,10},{9,11},{10,... | collective-permute-start | bytes 196616 | tf_op jit(solution)/shard_map/ppermute | solution.py:533
  40.5 1.4 %collective-permute-start.12 = (bf16[128,256]{1,0:T(8,128)(2,1)S(1)}, bf16[128,256]{1,0:T(8,128)(2,1)S(1)}, u32[]{:S(2)}, u32[]{:S(2)}) collective-permute-start(bf16[128,256]{1,0:T(8,128)(2,1)S(1)} %get-tuple-element.45), channel_id=1, source_target_pairs={{0,4},{1,5},{2,6},{3,7},{4,0},{5,1},{6,2},{7,3},{8,12},{9,13},{10,... | collective-permute-start | bytes 196616 | tf_op jit(solution)/shard_map/ppermute | solution.py:533
  41.9 1.4 %collective-permute-start.13 = (bf16[128,256]{1,0:T(8,128)(2,1)S(1)}, bf16[128,256]{1,0:T(8,128)(2,1)S(1)}, u32[]{:S(2)}, u32[]{:S(2)}) collective-permute-start(bf16[128,256]{1,0:T(8,128)(2,1)S(1)} %get-tuple-element.46), channel_id=1, source_target_pairs={{0,6},{1,7},{2,4},{3,5},{4,2},{5,3},{6,0},{7,1},{8,14},{9,15},{10,... | collective-permute-start | bytes 196616 | tf_op jit(solution)/shard_map/ppermute | solution.py:533
  43.7 3.4 %collective-permute-done.12.refs_2_ = bf16[128,256]{1,0:T(8,128)(2,1)S(1)} collective-permute-done((bf16[128,256]{1,0:T(8,128)(2,1)S(1)}, bf16[128,256]{1,0:T(8,128)(2,1)S(1)}, u32[]{:S(2)}, u32[]{:S(2)}) %collective-permute-start.12) | collective-permute-done | bytes 65568 | tf_op jit(solution)/shard_map/ppermute | solution.py:533
  47.1 1.0 %collective-permute-done.13.refs_3_ = bf16[128,256]{1,0:T(8,128)(2,1)S(1)} collective-permute-done((bf16[128,256]{1,0:T(8,128)(2,1)S(1)}, bf16[128,256]{1,0:T(8,128)(2,1)S(1)}, u32[]{:S(2)}, u32[]{:S(2)}) %collective-permute-start.13) | collective-permute-done | bytes 65568 | tf_op jit(solution)/shard_map/ppermute | solution.py:533
  48.1 0.5 shard_map.136
  48.6 0.4 collective-permute-start.15
  49.0 1.7 %collective-permute-done.17.refs_5_ = bf16[1024,512]{1,0:T(8,128)(2,1)S(1)} collective-permute-done((bf16[1024,512]{1,0:T(8,128)(2,1)S(1)}, bf16[1024,512]{1,0:T(8,128)(2,1)S(1)}, u32[]{:S(2)}, u32[]{:S(2)}) %collective-permute-start.17) | collective-permute-done | bytes 1048608 | tf_op jit(solution)/shard_map/ppermute | solution.py:427
  50.8 0.5 shard_map.137
  51.3 0.4 collective-permute-start.18
  51.7 3.3 %collective-permute-done.15.near_came = bf16[64,1024]{1,0:T(8,128)(2,1)S(1)} collective-permute-done((bf16[64,1024]{1,0:T(8,128)(2,1)S(1)}, bf16[64,1024]{1,0:T(8,128)(2,1)S(1)}, u32[]{:S(2)}, u32[]{:S(2)}) %collective-permute-start.15) | collective-permute-done | bytes 131104 | tf_op jit(solution)/shard_map/ppermute | solution.py:533
  55.0 2.4 %collective-permute-done.18.far_came = bf16[64,1024]{1,0:T(8,128)(2,1)S(1)} collective-permute-done((bf16[64,1024]{1,0:T(8,128)(2,1)S(1)}, bf16[64,1024]{1,0:T(8,128)(2,1)S(1)}, u32[]{:S(2)}, u32[]{:S(2)}) %collective-permute-start.18) | collective-permute-done | bytes 131104 | tf_op jit(solution)/shard_map/ppermute | solution.py:533
  57.4 0.7 %shard_map.138 = bf16[64,2048]{1,0:T(8,128)(2,1)} custom-call(f32[64,1024]{1,0:T(8,128)S(1)} %get-tuple-element.49.near_kept, bf16[64,1024]{1,0:T(8,128)(2,1)S(1)} %collective-permute-done.15.near_came, f32[64,1024]{1,0:T(8,128)S(1)} %get-tuple-element.53.far_kept, bf16[64,1024]{1,0:T(8,128)(2,1)S(1)} %collective-permute-done.18.far_came), custom_call_target="tpu_custom_call" | custom-call | tf_op jit(solution)/shard_map/pallas_call | solution.py:567
  (31 shorter events, 0.9 us)
Async XLA Ops:
  0.6 13.5 %copy-start.3 = (f32[32,64]{1,0:T(8,128)S(1)}, f32[32,64]{1,0:T(8,128)}, u32[]{:S(2)}) copy-start(f32[32,64]{1,0:T(8,128)} %constant.33.clone.refs_4_) | copy-start | bytes 24580
  0.6 13.5 %copy-start = (bf16[1,2048,128]{2,1,0:T(8,128)(2,1)S(1)}, bf16[1,2048,128]{2,1,0:T(8,128)(2,1)}, u32[]{:S(2)}) copy-start(bf16[1,2048,128]{2,1,0:T(8,128)(2,1)} %refs_0_.1) | copy-start | bytes 1572868
  0.7 13.5 %copy-start.4 = (bf16[2048]{0:T(1024)(128)(2,1)S(1)}, bf16[2048]{0:T(1024)(128)(2,1)}, u32[]{:S(2)}) copy-start(bf16[2048]{0:T(1024)(128)(2,1)} %param.13) | copy-start | bytes 12292
  0.7 13.5 %copy-start.5 = (f32[64]{0:T(128)S(1)}, f32[64]{0:T(128)}, u32[]{:S(2)}) copy-start(f32[64]{0:T(128)} %param.16) | copy-start | bytes 772
  0.7 13.5 %copy-start.6 = (f32[64]{0:T(128)S(1)}, f32[64]{0:T(128)}, u32[]{:S(2)}) copy-start(f32[64]{0:T(128)} %param.17) | copy-start | bytes 772
  0.7 9.5 %collective-permute-start = (bf16[64,2048]{1,0:T(8,128)(2,1)}, bf16[64,2048]{1,0:T(8,128)(2,1)S(1)}, u32[]{:S(2)}, u32[]{:S(2)}) collective-permute-start(bf16[64,2048]{1,0:T(8,128)(2,1)} %refs_1_.1), channel_id=1, source_target_pairs={{0,2},{2,4},{4,6},{6,7},{7,5},{5,3},{3,1},{1,0},{8,10},{10,12},{12... | collective-permute-start | bytes 786440 | tf_op jit(solution)/shard_map/ppermute | solution.py:421
  3.8 8.3 %collective-permute-start.1 = (bf16[64,2048]{1,0:T(8,128)(2,1)}, bf16[64,2048]{1,0:T(8,128)(2,1)S(1)}, u32[]{:S(2)}, u32[]{:S(2)}) collective-permute-start(bf16[64,2048]{1,0:T(8,128)(2,1)} %refs_1_.1), channel_id=1, source_target_pairs={{0,1},{2,0},{4,2},{6,4},{7,6},{5,7},{3,5},{1,3},{8,9},{10,8},{12,1... | collective-permute-start | bytes 786440 | tf_op jit(solution)/shard_map/ppermute | solution.py:424
  5.7 14.7 %copy-start.1 = (bf16[512,384]{1,0:T(8,128)(2,1)S(1)}, bf16[512,384]{1,0:T(8,128)(2,1)}, u32[]{:S(2)}) copy-start(bf16[512,384]{1,0:T(8,128)(2,1)} %shard_map.132.refs_10_.refs_7_) | copy-start | bytes 1179652
  5.7 17.3 %copy-start.2 = (bf16[64,2048]{1,0:T(8,128)(2,1)S(1)}, bf16[64,2048]{1,0:T(8,128)(2,1)}, u32[]{:S(2)}) copy-start(bf16[64,2048]{1,0:T(8,128)(2,1)} %refs_1_.1) | copy-start | bytes 786436
  5.7 10.9 %collective-permute-start.5 = (bf16[512,384]{1,0:T(8,128)(2,1)}, bf16[512,384]{1,0:T(8,128)(2,1)S(1)}, u32[]{:S(2)}, u32[]{:S(2)}) collective-permute-start(bf16[512,384]{1,0:T(8,128)(2,1)} %shard_map.132.refs_10_.refs_7_), channel_id=1, source_target_pairs={{0,16},{8,24},{16,0},{24,8},{1,17},{9,25},{17,1},{25,9},{2,18},{10... | collective-permute-start | bytes 1179656 | tf_op jit(solution)/shard_map/ppermute | solution.py:427
  10.2 7.5 %collective-permute-start.2 = (bf16[64,2048]{1,0:T(8,128)(2,1)S(1)}, bf16[64,2048]{1,0:T(8,128)(2,1)S(1)}, u32[]{:S(2)}, u32[]{:S(2)}) collective-permute-start(bf16[64,2048]{1,0:T(8,128)(2,1)S(1)} %collective-permute-done.refs_5_.refs_2_), channel_id=1, source_target_pairs={{0,2},{2,4},{4,6},{6,7},{7,5},{5,3},{3,1},{1,0},{8,10},{10,12},{12... | collective-permute-start | bytes 786440 | tf_op jit(solution)/shard_map/ppermute | solution.py:421
  12.0 6.9 %collective-permute-start.4 = (bf16[64,2048]{1,0:T(8,128)(2,1)S(1)}, bf16[64,2048]{1,0:T(8,128)(2,1)S(1)}, u32[]{:S(2)}, u32[]{:S(2)}) collective-permute-start(bf16[64,2048]{1,0:T(8,128)(2,1)S(1)} %collective-permute-done.1.refs_6_.refs_3_), channel_id=1, source_target_pairs={{0,1},{2,0},{4,2},{6,4},{7,6},{5,7},{3,5},{1,3},{8,9},{10,8},{12,1... | collective-permute-start | bytes 786440 | tf_op jit(solution)/shard_map/ppermute | solution.py:424
  18.9 29.2 %collective-permute-start.16 = (bf16[1024,512]{1,0:T(8,128)(2,1)S(1)}, bf16[1024,512]{1,0:T(8,128)(2,1)S(1)}, u32[]{:S(2)}, u32[]{:S(2)}) collective-permute-start(bf16[1024,512]{1,0:T(8,128)(2,1)S(1)} %bitcast.12), channel_id=1, source_target_pairs={{0,16},{8,24},{16,0},{24,8},{1,17},{9,25},{17,1},{25,9},{2,18},{10... | collective-permute-start | bytes 3145736 | tf_op jit(solution)/shard_map/ppermute | solution.py:427
  20.4 2.5 %collective-permute-start.6 = (bf16[512,384]{1,0:T(8,128)(2,1)S(1)}, bf16[512,384]{1,0:T(8,128)(2,1)S(1)}, u32[]{:S(2)}, u32[]{:S(2)}) collective-permute-start(bf16[512,384]{1,0:T(8,128)(2,1)S(1)} %copy-done.1), channel_id=1, source_target_pairs={{0,8},{8,0},{16,24},{24,16},{1,9},{9,1},{17,25},{25,17},{2,10},{10... | collective-permute-start | bytes 1179656 | tf_op jit(solution)/shard_map/ppermute | solution.py:427
  20.4 2.5 %collective-permute-start.7 = (bf16[512,384]{1,0:T(8,128)(2,1)S(1)}, bf16[512,384]{1,0:T(8,128)(2,1)S(1)}, u32[]{:S(2)}, u32[]{:S(2)}) collective-permute-start(bf16[512,384]{1,0:T(8,128)(2,1)S(1)} %collective-permute-done.5.refs_12_.refs_9_), channel_id=1, source_target_pairs={{0,8},{8,0},{16,24},{24,16},{1,9},{9,1},{17,25},{25,17},{2,10},{10... | collective-permute-start | bytes 1179656 | tf_op jit(solution)/shard_map/ppermute | solution.py:427
  20.9 8.2 %collective-permute-start.3 = (bf16[64,2048]{1,0:T(8,128)(2,1)S(1)}, bf16[64,2048]{1,0:T(8,128)(2,1)S(1)}, u32[]{:S(2)}, u32[]{:S(2)}) collective-permute-start(bf16[64,2048]{1,0:T(8,128)(2,1)S(1)} %collective-permute-done.2.refs_4_), channel_id=1, source_target_pairs={{0,2},{2,4},{4,6},{6,7},{7,5},{5,3},{3,1},{1,0},{8,10},{10,12},{12... | collective-permute-start | bytes 786440 | tf_op jit(solution)/shard_map/ppermute | solution.py:421
  22.5 8.3 %collective-permute-start.9 = (bf16[64,2048]{1,0:T(8,128)(2,1)S(1)}, bf16[64,2048]{1,0:T(8,128)(2,1)S(1)}, u32[]{:S(2)}, u32[]{:S(2)}) collective-permute-start(bf16[64,2048]{1,0:T(8,128)(2,1)S(1)} %collective-permute-done.4.refs_5_), channel_id=1, source_target_pairs={{0,1},{2,0},{4,2},{6,4},{7,6},{5,7},{3,5},{1,3},{8,9},{10,8},{12,1... | collective-permute-start | bytes 786440 | tf_op jit(solution)/shard_map/ppermute | solution.py:424
  29.2 5.7 %collective-permute-start.8 = (bf16[32,2048]{1,0:T(8,128)(2,1)S(1)}, bf16[32,2048]{1,0:T(8,128)(2,1)S(1)}, u32[]{:S(2)}, u32[]{:S(2)}) collective-permute-start(bf16[32,2048]{1,0:T(8,128)(2,1)S(1)} %slice.6), channel_id=1, source_target_pairs={{0,2},{2,4},{4,6},{6,7},{7,5},{5,3},{3,1},{1,0},{8,10},{10,12},{12... | collective-permute-start | bytes 393224 | tf_op jit(solution)/shard_map/ppermute | solution.py:421
  30.8 5.2 %collective-permute-start.10 = (bf16[32,2048]{1,0:T(8,128)(2,1)S(1)}, bf16[32,2048]{1,0:T(8,128)(2,1)S(1)}, u32[]{:S(2)}, u32[]{:S(2)}) collective-permute-start(bf16[32,2048]{1,0:T(8,128)(2,1)S(1)} %slice.7), channel_id=1, source_target_pairs={{0,1},{2,0},{4,2},{6,4},{7,6},{5,7},{3,5},{1,3},{8,9},{10,8},{12,1... | collective-permute-start | bytes 393224 | tf_op jit(solution)/shard_map/ppermute | solution.py:424
  39.0 4.7 %collective-permute-start.11 = (bf16[128,256]{1,0:T(8,128)(2,1)S(1)}, bf16[128,256]{1,0:T(8,128)(2,1)S(1)}, u32[]{:S(2)}, u32[]{:S(2)}) collective-permute-start(bf16[128,256]{1,0:T(8,128)(2,1)S(1)} %get-tuple-element.44), channel_id=1, source_target_pairs={{0,2},{1,3},{2,0},{3,1},{4,6},{5,7},{6,4},{7,5},{8,10},{9,11},{10,... | collective-permute-start | bytes 196616 | tf_op jit(solution)/shard_map/ppermute | solution.py:533
  40.5 6.6 %collective-permute-start.12 = (bf16[128,256]{1,0:T(8,128)(2,1)S(1)}, bf16[128,256]{1,0:T(8,128)(2,1)S(1)}, u32[]{:S(2)}, u32[]{:S(2)}) collective-permute-start(bf16[128,256]{1,0:T(8,128)(2,1)S(1)} %get-tuple-element.45), channel_id=1, source_target_pairs={{0,4},{1,5},{2,6},{3,7},{4,0},{5,1},{6,2},{7,3},{8,12},{9,13},{10,... | collective-permute-start | bytes 196616 | tf_op jit(solution)/shard_map/ppermute | solution.py:533
  41.9 6.2 %collective-permute-start.13 = (bf16[128,256]{1,0:T(8,128)(2,1)S(1)}, bf16[128,256]{1,0:T(8,128)(2,1)S(1)}, u32[]{:S(2)}, u32[]{:S(2)}) collective-permute-start(bf16[128,256]{1,0:T(8,128)(2,1)S(1)} %get-tuple-element.46), channel_id=1, source_target_pairs={{0,6},{1,7},{2,4},{3,5},{4,2},{5,3},{6,0},{7,1},{8,14},{9,15},{10,... | collective-permute-start | bytes 196616 | tf_op jit(solution)/shard_map/ppermute | solution.py:533
  43.3 4.8 %collective-permute-start.14 = (bf16[1024,512]{1,0:T(8,128)(2,1)S(1)}, bf16[1024,512]{1,0:T(8,128)(2,1)S(1)}, u32[]{:S(2)}, u32[]{:S(2)}) collective-permute-start(bf16[1024,512]{1,0:T(8,128)(2,1)S(1)} %bitcast.13), channel_id=1, source_target_pairs={{0,8},{8,0},{16,24},{24,16},{1,9},{9,1},{17,25},{25,17},{2,10},{10... | collective-permute-start | bytes 3145736 | tf_op jit(solution)/shard_map/ppermute | solution.py:427
  48.1 2.7 %collective-permute-start.17 = (bf16[1024,512]{1,0:T(8,128)(2,1)S(1)}, bf16[1024,512]{1,0:T(8,128)(2,1)S(1)}, u32[]{:S(2)}, u32[]{:S(2)}) collective-permute-start(bf16[1024,512]{1,0:T(8,128)(2,1)S(1)} %collective-permute-done.16.refs_4_), channel_id=1, source_target_pairs={{0,8},{8,0},{16,24},{24,16},{1,9},{9,1},{17,25},{25,17},{2,10},{10... | collective-permute-start | bytes 3145736 | tf_op jit(solution)/shard_map/ppermute | solution.py:427
  48.6 6.4 %collective-permute-start.15 = (bf16[64,1024]{1,0:T(8,128)(2,1)S(1)}, bf16[64,1024]{1,0:T(8,128)(2,1)S(1)}, u32[]{:S(2)}, u32[]{:S(2)}) collective-permute-start(bf16[64,1024]{1,0:T(8,128)(2,1)S(1)} %get-tuple-element.50), channel_id=1, source_target_pairs={{0,1},{1,0},{2,3},{3,2},{4,5},{5,4},{6,7},{7,6},{8,9},{9,8},{10,11... | collective-permute-start | bytes 393224 | tf_op jit(solution)/shard_map/ppermute | solution.py:533
  51.3 6.1 %collective-permute-start.18 = (bf16[64,1024]{1,0:T(8,128)(2,1)S(1)}, bf16[64,1024]{1,0:T(8,128)(2,1)S(1)}, u32[]{:S(2)}, u32[]{:S(2)}) collective-permute-start(bf16[64,1024]{1,0:T(8,128)(2,1)S(1)} %get-tuple-element.54), channel_id=1, source_target_pairs={{0,1},{1,0},{2,3},{3,2},{4,5},{5,4},{6,7},{7,6},{8,9},{9,8},{10,11... | collective-permute-start | bytes 393224 | tf_op jit(solution)/shard_map/ppermute | solution.py:533
